TPU v7x, 32 devices: a whole 2x2x4 slice. The times are simulated.
32 devices in a mesh: dp: 8 (over z, y), tensor: 4 (over x, core).
Axes of the slice: x: 2, y: 2, z: 4, core: 2. Of those that a mesh axis runs over, the one named last changes fastest.
Arguments:
- tokens: bfloat16 [16384, 1280], P(('dp', 'tensor')), may hold values from -6 to 6
- cotangent: bfloat16 [16384, 1280], P(('dp', 'tensor')), may hold values from -6 to 6
- lengths: int32 [16], P('dp'), may hold values from 256 to 1024, as said below
- key_mask: int32 [16, 1024], P('dp'), may hold values 0 or 1
- qkv_weight: float32 [1280, 3, 1280], P('dp', None, 'tensor'), may hold values from -0.15625 to 0.15625
- out_weight: float32 [1280, 1280], P(('tensor', 'dp')), may hold values from -4 to 4
- up_weight: float32 [1280, 5120], P('dp', 'tensor'), may hold values from -0.15625 to 0.15625
- down_weight: float32 [5120, 1280], P(('tensor', 'dp')), may hold values from -0.078125 to 0.078125
- norm_params: float32 [4, 1280], P(None, 'dp')
- qkv_first: float32 [1280, 3, 1280], P('dp', None, 'tensor'), may hold values from -0.001953125 to 0.001953125
- qkv_second: float32 [1280, 3, 1280], P('dp', None, 'tensor'), may hold values from 5.493164e-08 to 9.155273e-07
- out_first: float32 [1280, 1280], P(('tensor', 'dp')), may hold values from -0.00010681152 to 0.00010681152
- out_second: float32 [1280, 1280], P(('tensor', 'dp')), may hold values from 1.4038086e-10 to 2.2583009e-09
- up_first: float32 [1280, 5120], P('dp', 'tensor'), may hold values from -0.00024414062 to 0.00024414062
- up_second: float32 [1280, 5120], P('dp', 'tensor'), may hold values from 1.1596679e-09 to 4.577637e-09
- down_first: float32 [5120, 1280], P(('tensor', 'dp')), may hold values from -0.0004272461 to 0.0004272461
- down_second: float32 [5120, 1280], P(('tensor', 'dp')), may hold values from 3.2958984e-09 to 1.3183594e-08
- norm_first: float32 [4, 1280], P(None, 'dp'), may hold values from -0.0029296875 to 0.0029296875
- norm_second: float32 [4, 1280], P(None, 'dp'), may hold values from 1.2207032e-07 to 2.0141601e-06
Outputs:
- layer_out: bfloat16 [16384, 1280], P(('dp', 'tensor'))
- input_grad: bfloat16 [16384, 1280], P(('dp', 'tensor'))
- grad_norm: float32 [], replicated
- qkv_new: float32 [1280, 3, 1280], P('dp', None, 'tensor')
- qkv_first_new: float32 [1280, 3, 1280], P('dp', None, 'tensor')
- qkv_second_new: float32 [1280, 3, 1280], P('dp', None, 'tensor')
- out_new: float32 [1280, 1280], P(('tensor', 'dp'))
- out_first_new: float32 [1280, 1280], P(('tensor', 'dp'))
- out_second_new: float32 [1280, 1280], P(('tensor', 'dp'))
- up_new: float32 [1280, 5120], P('dp', 'tensor')
- up_first_new: float32 [1280, 5120], P('dp', 'tensor')
- up_second_new: float32 [1280, 5120], P('dp', 'tensor')
- down_new: float32 [5120, 1280], P(('tensor', 'dp'))
- down_first_new: float32 [5120, 1280], P(('tensor', 'dp'))
- down_second_new: float32 [5120, 1280], P(('tensor', 'dp'))
- norm_new: float32 [4, 1280], P(None, 'dp')
- norm_first_new: float32 [4, 1280], P(None, 'dp')
- norm_second_new: float32 [4, 1280], P(None, 'dp')
- shift_grad: float32 [1280], P('dp')
Inputs may be any that keep to these rules, and one draw needn't show every extreme that they name: `lengths`: tokens that count in each cell, from its first position; some cell has all 1024 in every draw.
All inputs are finite; a program needn't handle non-finite values. No bound on the sum of `key_mask` on one device may be relied on, other than what follows from the above.
Results may differ from a plain program's by a relative error of at most 0.02.
Values may be sent and summed in bfloat16 or wider, within the bound.
No kernel may reach another device: no remote copies, remote signals or barrier semaphores. Data moves between devices by JAX's collectives and lax.ppermute only.
A program may use at most 192 MiB of HBM per device.

v0:
```python
from functools import partial

import jax
import jax.numpy as jnp
from jax import lax
from jax.sharding import PartitionSpec as P

HD = 64
L = 1024
STEP = 5


NORM_EPS = 1e-05
CLIP_LIMIT = 1.0
BETA_FIRST = 0.5
BETA_SECOND = 0.5
ADAM_EPS = 1e-08
DECAY_RATE = 0.01
RATE_QKV = 0.03
RATE_OUT = 0.5
RATE_UP = 0.03
RATE_DOWN = 0.015
RATE_NORM = 0.2


def layer_norm_parts(values, gain_row, shift_row):
    centered = values - jnp.mean(values, axis=-1, keepdims=True)
    inverse = lax.rsqrt(jnp.mean(centered * centered, axis=-1, keepdims=True) + NORM_EPS)
    normed = centered * inverse
    return (normed * gain_row + shift_row, normed, inverse)


def layer_norm_back(grad_normed, normed, inverse, gain_row):
    scaled = grad_normed * gain_row
    return inverse * (
        scaled
        - jnp.mean(scaled, axis=-1, keepdims=True)
        - normed * jnp.mean(scaled * normed, axis=-1, keepdims=True)
    )


def cell_forward(packed):
    qkv_cell, valid_cell = packed
    scores = jnp.einsum(
        "qhe,khe->hqk", qkv_cell[:, 0], qkv_cell[:, 1], preferred_element_type=jnp.float32
    ) * HD ** (-0.5)
    masked = jnp.where(valid_cell[None, None, :], scores, -1e30)
    row_max = jnp.max(masked, axis=-1, keepdims=True)
    log_total = row_max + jnp.log(jnp.sum(jnp.exp(masked - row_max), axis=-1, keepdims=True))
    weights = jnp.exp(masked - log_total).astype(jnp.bfloat16)
    context = jnp.einsum(
        "hqk,khe->qhe", weights, qkv_cell[:, 2], preferred_element_type=jnp.float32
    )
    return (context.astype(jnp.bfloat16), log_total)


def cell_backward(packed):
    qkv_cell, valid_cell, log_total, grad_context = packed
    score_scale = HD ** (-0.5)
    queries = qkv_cell[:, 0]
    key_rows = qkv_cell[:, 1]
    values = qkv_cell[:, 2]
    scores = (
        jnp.einsum("qhe,khe->hqk", queries, key_rows, preferred_element_type=jnp.float32)
        * score_scale
    )
    masked = jnp.where(valid_cell[None, None, :], scores, -1e30)
    weights = jnp.exp(masked - log_total)
    weights_low = weights.astype(jnp.bfloat16)
    grad_weights = jnp.einsum(
        "qhe,khe->hqk", grad_context, values, preferred_element_type=jnp.float32
    )
    row_terms = jnp.sum(weights * grad_weights, axis=-1, keepdims=True)
    grad_scores = (weights * (grad_weights - row_terms)).astype(jnp.bfloat16)
    grad_queries = (
        jnp.einsum("hqk,khe->qhe", grad_scores, key_rows, preferred_element_type=jnp.float32)
        * score_scale
    )
    grad_keys = (
        jnp.einsum("hqk,qhe->khe", grad_scores, queries, preferred_element_type=jnp.float32)
        * score_scale
    )
    grad_values = jnp.einsum(
        "hqk,qhe->khe", weights_low, grad_context, preferred_element_type=jnp.float32
    )
    return jnp.stack([grad_queries, grad_keys, grad_values], axis=1).astype(jnp.bfloat16)


def adam_update(master, grad_sum, moment_one, moment_two, step_rate, clip_factor):
    clipped = grad_sum * clip_factor
    one_new = BETA_FIRST * moment_one + (1.0 - BETA_FIRST) * clipped
    two_new = BETA_SECOND * moment_two + (1.0 - BETA_SECOND) * clipped * clipped
    one_hat = one_new / (1.0 - BETA_FIRST**STEP)
    two_hat = two_new / (1.0 - BETA_SECOND**STEP)
    master_new = master - step_rate * (
        one_hat / (jnp.sqrt(two_hat) + ADAM_EPS) + DECAY_RATE * master
    )
    return (master_new, one_new, two_new)


def on_device(
    tokens,
    cotangent,
    lengths,
    key_mask,
    qkv_weight,
    out_weight,
    up_weight,
    down_weight,
    norm_params,
    qkv_first,
    qkv_second,
    out_first,
    out_second,
    up_first,
    up_second,
    down_first,
    down_second,
    norm_first,
    norm_second,
):
    qkv_full, out_full, up_full, down_full, norm_full = (
        lax.all_gather(qkv_weight.astype(jnp.bfloat16), "dp", axis=0, tiled=True),
        lax.all_gather(out_weight.astype(jnp.bfloat16), "dp", axis=0, tiled=True),
        lax.all_gather(up_weight.astype(jnp.bfloat16), "dp", axis=0, tiled=True),
        lax.all_gather(down_weight.astype(jnp.bfloat16), "dp", axis=0, tiled=True),
        lax.all_gather(norm_params.astype(jnp.bfloat16), "dp", axis=1, tiled=True),
    )
    norm_values = norm_full.astype(jnp.float32)
    cell_count = lengths.shape[0]
    head_count = qkv_full.shape[2] // HD
    positions = jnp.arange(L, dtype=jnp.int32)
    key_valid = (positions[None, :] < lengths[:, None]) & (
        (key_mask == 1) | (positions[None, :] == 0)
    )
    stream_in = tokens.astype(jnp.float32)
    ln_one, normed_one, inverse_one = layer_norm_parts(stream_in, norm_values[0], norm_values[1])
    group_one = lax.all_gather(ln_one.astype(jnp.bfloat16), "tensor", axis=0, tiled=True)
    projected = jnp.einsum(
        "td,dcf->tcf", group_one, qkv_full, preferred_element_type=jnp.float32
    ).astype(jnp.bfloat16)
    qkv_cells = projected.reshape(cell_count, L, 3, head_count, HD)
    context, log_total = lax.map(cell_forward, (qkv_cells, key_valid))
    context = context.reshape(cell_count * L, head_count * HD)
    row_block = context
    residual = stream_in + lax.psum_scatter(
        jnp.dot(row_block, out_full, preferred_element_type=jnp.float32).astype(jnp.bfloat16),
        "tensor",
        scatter_dimension=0,
        tiled=True,
    ).astype(jnp.float32)
    ln_two, normed_two, inverse_two = layer_norm_parts(residual, norm_values[2], norm_values[3])
    group_two = lax.all_gather(ln_two.astype(jnp.bfloat16), "tensor", axis=0, tiled=True)
    hidden_pre = jnp.dot(group_two, up_full, preferred_element_type=jnp.float32)
    hidden = jax.nn.gelu(hidden_pre, approximate=False).astype(jnp.bfloat16)
    row_block = hidden
    layer_out = (
        residual
        + lax.psum_scatter(
            jnp.dot(row_block, down_full, preferred_element_type=jnp.float32).astype(jnp.bfloat16),
            "tensor",
            scatter_dimension=0,
            tiled=True,
        ).astype(jnp.float32)
    ).astype(jnp.bfloat16)
    grad_group = lax.all_gather(cotangent, "tensor", axis=0, tiled=True)
    grad_hidden = jnp.einsum("td,fd->tf", grad_group, down_full, preferred_element_type=jnp.float32)
    grad_down = jnp.einsum("tf,td->fd", hidden, grad_group, preferred_element_type=jnp.float32)
    gelu_value, gelu_pull = jax.vjp(partial(jax.nn.gelu, approximate=False), hidden_pre)
    grad_pre = gelu_pull(grad_hidden)[0].astype(jnp.bfloat16)
    grad_up = jnp.einsum("td,tf->df", group_two, grad_pre, preferred_element_type=jnp.float32)
    row_block = grad_pre
    grad_ln_two = lax.psum_scatter(
        jnp.einsum("tf,df->td", row_block, up_full, preferred_element_type=jnp.float32).astype(
            jnp.bfloat16
        ),
        "tensor",
        scatter_dimension=0,
        tiled=True,
    ).astype(jnp.float32)
    grad_residual = cotangent.astype(jnp.float32) + layer_norm_back(
        grad_ln_two, normed_two, inverse_two, norm_values[2]
    )
    gain_two = jnp.sum(grad_ln_two * normed_two, axis=0)
    shift_two = jnp.sum(grad_ln_two, axis=0)
    residual_group = lax.all_gather(
        grad_residual.astype(jnp.bfloat16), "tensor", axis=0, tiled=True
    )
    grad_out = jnp.einsum("tf,td->fd", context, residual_group, preferred_element_type=jnp.float32)
    grad_context = jnp.einsum(
        "td,fd->tf", residual_group, out_full, preferred_element_type=jnp.float32
    ).astype(jnp.bfloat16)
    grad_cells = lax.map(
        cell_backward,
        (qkv_cells, key_valid, log_total, grad_context.reshape(cell_count, L, head_count, HD)),
    )
    grad_projected = grad_cells.reshape(cell_count * L, 3, head_count * HD)
    grad_qkv = jnp.einsum(
        "td,tcf->dcf", group_one, grad_projected, preferred_element_type=jnp.float32
    )
    row_block = grad_projected
    grad_ln_one = lax.psum_scatter(
        jnp.einsum("tcf,dcf->td", row_block, qkv_full, preferred_element_type=jnp.float32).astype(
            jnp.bfloat16
        ),
        "tensor",
        scatter_dimension=0,
        tiled=True,
    ).astype(jnp.float32)
    input_grad = (
        grad_residual + layer_norm_back(grad_ln_one, normed_one, inverse_one, norm_values[0])
    ).astype(jnp.bfloat16)
    gain_one = jnp.sum(grad_ln_one * normed_one, axis=0)
    shift_one = jnp.sum(grad_ln_one, axis=0)
    norm_local = jnp.stack([gain_one, shift_one, gain_two, shift_two])
    norm_group = lax.psum(norm_local, "tensor")
    summed_qkv, summed_out, summed_up, summed_down, summed_norm = (
        lax.psum_scatter(
            grad_qkv.astype(jnp.bfloat16), "dp", scatter_dimension=0, tiled=True
        ).astype(jnp.float32),
        lax.psum_scatter(
            grad_out.astype(jnp.bfloat16), "dp", scatter_dimension=0, tiled=True
        ).astype(jnp.float32),
        lax.psum_scatter(
            grad_up.astype(jnp.bfloat16), "dp", scatter_dimension=0, tiled=True
        ).astype(jnp.float32),
        lax.psum_scatter(
            grad_down.astype(jnp.bfloat16), "dp", scatter_dimension=0, tiled=True
        ).astype(jnp.float32),
        lax.psum_scatter(
            norm_group.astype(jnp.bfloat16), "dp", scatter_dimension=1, tiled=True
        ).astype(jnp.float32),
    )
    local_squares = (
        jnp.sum(summed_qkv * summed_qkv)
        + jnp.sum(summed_out * summed_out)
        + jnp.sum(summed_up * summed_up)
        + jnp.sum(summed_down * summed_down)
        + jnp.sum(summed_norm * summed_norm) / lax.axis_size("tensor")
    )
    squares_total = lax.psum(local_squares, ("dp", "tensor"))
    grad_norm = jnp.sqrt(squares_total)
    clip_factor = jnp.minimum(1.0, CLIP_LIMIT / grad_norm)
    qkv_new, qkv_one, qkv_two = adam_update(
        qkv_weight, summed_qkv, qkv_first, qkv_second, RATE_QKV, clip_factor
    )
    out_new, out_one, out_two = adam_update(
        out_weight, summed_out, out_first, out_second, RATE_OUT, clip_factor
    )
    up_new, up_one, up_two = adam_update(
        up_weight, summed_up, up_first, up_second, RATE_UP, clip_factor
    )
    down_new, down_one, down_two = adam_update(
        down_weight, summed_down, down_first, down_second, RATE_DOWN, clip_factor
    )
    norm_new, norm_one, norm_two = adam_update(
        norm_params, summed_norm, norm_first, norm_second, RATE_NORM, clip_factor
    )
    shift_grad = clip_factor * summed_norm[3]
    return (
        layer_out,
        input_grad,
        grad_norm,
        qkv_new,
        qkv_one,
        qkv_two,
        out_new,
        out_one,
        out_two,
        up_new,
        up_one,
        up_two,
        down_new,
        down_one,
        down_two,
        norm_new,
        norm_one,
        norm_two,
        shift_grad,
    )


def solution(mesh):
    return jax.shard_map(
        on_device,
        mesh=mesh,
        in_specs=(
            P(("dp", "tensor"), None),
            P(("dp", "tensor"), None),
            P("dp"),
            P("dp", None),
            P("dp", None, "tensor"),
            P(("tensor", "dp"), None),
            P("dp", "tensor"),
            P(("tensor", "dp"), None),
            P(None, "dp"),
            P("dp", None, "tensor"),
            P("dp", None, "tensor"),
            P(("tensor", "dp"), None),
            P(("tensor", "dp"), None),
            P("dp", "tensor"),
            P("dp", "tensor"),
            P(("tensor", "dp"), None),
            P(("tensor", "dp"), None),
            P(None, "dp"),
            P(None, "dp"),
        ),
        out_specs=(
            P(("dp", "tensor"), None),
            P(("dp", "tensor"), None),
            P(),
            P("dp", None, "tensor"),
            P("dp", None, "tensor"),
            P("dp", None, "tensor"),
            P(("tensor", "dp"), None),
            P(("tensor", "dp"), None),
            P(("tensor", "dp"), None),
            P("dp", "tensor"),
            P("dp", "tensor"),
            P("dp", "tensor"),
            P(("tensor", "dp"), None),
            P(("tensor", "dp"), None),
            P(("tensor", "dp"), None),
            P(None, "dp"),
            P(None, "dp"),
            P(None, "dp"),
            P("dp"),
        ),
        check_vma=False,
    )
```

profile of v0, /device:TPU:0, one launch (start us, length us, event | category | flops | bytes accessed | tf_op | source)
XLA Modules:
  0.0 1131.7 jit_solution(14597372235053009157)
XLA Ops:
  7.3 2.0 convert_element_type.132
  10.0 27.9 %all-gather = bf16[8,160,4]{1,2,0:T(4,128)(2,1)S(1)} all-gather(bf16[1,160,4]{1,2,0:T(4,128)(2,1)S(1)} %convert_bitcast_fusion), channel_id=1, replica_groups=mesh['dp'=8,'tensor'=4] {'dp'}, dimensions={0}, use_global_device_ids=true | all-gather | bytes 11520 | tf_op jit(solution)/shard_map/all_gather | solution.py:127
  44.5 36.4 %all_gather.30 = bf16[320,1280]{1,0:T(8,128)(2,1)} all-gather(bf16[40,1280]{1,0:T(8,128)(2,1)S(1)} %convert_element_type.134), channel_id=1, replica_groups=mesh['dp'=8,'tensor'=4] {'dp'}, dimensions={0}, use_global_device_ids=true | all-gather | bytes 921600 | tf_op jit(solution)/shard_map/all_gather | solution.py:124
  80.9 4.0 all-gather.11.cloned.1.call-done
  85.0 42.0 %all-gather.9.cloned.1.call-done = bf16[2048,1280]{1,0:T(8,128)(2,1)} async-done(((bf16[512,1280]{1,0:T(8,128)(2,1)}), bf16[2048,1280]{1,0:T(8,128)(2,1)}) %all-gather.9.cloned.1.call-update) | async-done | bytes 5242896 | tf_op jit(solution)/shard_map/all_gather | solution.py:138
  127.0 9.4 fusion.46
  136.4 10.0 reshape.177
  146.4 5.3 copy.73
  151.6 35.9 %while.22 = (s32[]{:T(128)}, bf16[2,1024,5,64]{1,3,2,0:T(8,128)(2,1)}, f32[2,5,1024,1]{2,1,3,0:T(8,128)}, bf16[2,1024,3,5,64]{1,4,3,2,0:T(8,128)(2,1)}, pred[2,1024]{1,0:T(4,128)(4,1)S(1)}, /*index=5*/s32[]{:T(128)}) while((s32[]{:T(128)}, bf16[2,1024,5,64]{1,3,2,0:T(8,128)(2,1)}, f32[2,5,1024,1]{2,1,3,0:T(8,128)}, ...), condition=%wide.region_5.6_spmd, body=%wide.region_2.5_spmd.sunk | while | flops 1400171520 | bytes 77878448 | solution.py:143
  153.6 4.0 fusion.125
  157.6 5.0 exponential_reduce_fusion.2
  163.2 6.5 fusion.126
  171.4 4.0 fusion.125
  175.4 5.0 exponential_reduce_fusion.2
  181.1 6.5 fusion.126
  187.5 2.7 copy.74
  191.7 5.1 convolution_convert_fusion.2
  198.8 49.6 %reduce-scatter.12.cloned.1.call-done = bf16[512,1280]{1,0:T(8,128)(2,1)} async-done(((bf16[2048,1280]{1,0:T(8,128)(2,1)}), bf16[512,1280]{1,0:T(8,128)(2,1)}) %reduce-scatter.12.cloned.1.call-update) | async-done | bytes 1310736 | tf_op jit(solution)/shard_map/reduce_scatter | solution.py:146
  255.7 57.5 %all-gather.15.cloned.1.call-done = bf16[1280,1280]{1,0:T(8,128)(2,1)} async-done(((bf16[160,1280]{1,0:T(8,128)(2,1)}), bf16[1280,1280]{1,0:T(8,128)(2,1)}) %all-gather.15.cloned.1.call-update) | async-done | bytes 3276816 | tf_op jit(solution)/shard_map/all_gather | solution.py:125
  313.2 41.1 %all-gather.13.cloned.1.call-done = bf16[2048,1280]{1,0:T(8,128)(2,1)} async-done(((bf16[512,1280]{1,0:T(8,128)(2,1)}), bf16[2048,1280]{1,0:T(8,128)(2,1)}) %all-gather.13.cloned.1.call-update) | async-done | bytes 5242896 | tf_op jit(solution)/shard_map/all_gather | solution.py:153
  354.3 12.2 %fusion.90 = f32[2048,1280]{1,0:T(8,128)} fusion(bf16[2048,1280]{1,0:T(8,128)(2,1)} %all-gather.13.cloned.1.call-done, bf16[1280,1280]{1,0:T(8,128)(2,1)} %all-gather.15.cloned.1.call-done), kind=kOutput, calls=%fused_computation.171 | convolution fusion | flops 6710886400 | bytes 19005440 | tf_op jit(solution)/shard_map/dot_general | solution.py:154
  366.5 52.7 %all-gather.17.cloned.1.call-done = bf16[1280,1280]{1,0:T(8,128)(2,1)} async-done(((bf16[160,1280]{1,0:T(8,128)(2,1)}), bf16[1280,1280]{1,0:T(8,128)(2,1)}) %all-gather.17.cloned.1.call-update) | async-done | bytes 3276816 | tf_op jit(solution)/shard_map/all_gather | solution.py:126
  419.2 40.7 %all-gather.19.cloned.1.call-done = bf16[2048,1280]{1,0:T(8,128)(2,1)} async-done(((bf16[512,1280]{1,0:T(8,128)(2,1)}), bf16[2048,1280]{1,0:T(8,128)(2,1)}) %all-gather.19.cloned.1.call-update) | async-done | bytes 5242896 | tf_op jit(solution)/shard_map/all_gather | solution.py:166
  459.9 34.8 %add_convert_fusion = (bf16[2048,1280]{1,0:T(8,128)(2,1)S(1)}, f32[2048,1280]{1,0:T(8,128)}) fusion(f32[2048,1280]{1,0:T(8,128)} %fusion.90, bf16[2048,1280]{1,0:T(8,128)(2,1)} %all-gather.19.cloned.1.call-done, bf16[1280,1280]{1,0:T(8,128)(2,1)} %all-gather.17.cloned.1.call-done), kind=kOutput, calls=%fused_computation.53 | convolution fusion | flops 6899630080 | bytes 34734080 | tf_op jit(solution)/shard_map/td,fd->tf/dot_general | solution.py:167
  494.7 2.4 copy-done.62
  497.1 8.7 convolution_convert_fusion
  506.0 51.3 %reduce-scatter.16.cloned.1.call-done = bf16[512,1280]{1,0:T(8,128)(2,1)} async-done(((bf16[2048,1280]{1,0:T(8,128)(2,1)}), bf16[512,1280]{1,0:T(8,128)(2,1)}) %reduce-scatter.16.cloned.1.call-update) | async-done | bytes 1310736 | tf_op jit(solution)/shard_map/reduce_scatter | solution.py:173
  557.3 3.4 fusion.71
  560.8 2.3 fusion.83
  563.2 11.2 multiply_convert_fusion.1
  574.4 11.8 %convolution_convert_fusion.3 = bf16[1280,1280]{1,0:T(8,128)(2,1)} fusion(bf16[2048,1280]{1,0:T(8,128)(2,1)} %multiply_convert_fusion.1, bf16[2048,1280]{1,0:T(8,128)(2,1)} %all-gather.19.cloned.1.call-done), kind=kOutput, calls=%fused_computation.71 | convolution fusion | flops 6712524800 | bytes 13762560 | tf_op jit(solution)/shard_map/tf,td->fd/dot_general | solution.py:168
  586.3 11.8 %convolution_convert_fusion.4 = bf16[1280,1280]{1,0:T(8,128)(2,1)} fusion(bf16[2048,1280]{1,0:T(8,128)(2,1)} %all-gather.13.cloned.1.call-done, bf16[2048,1280]{1,0:T(8,128)(2,1)} %copy-done.62), kind=kOutput, calls=%fused_computation.72 | convolution fusion | flops 6712524800 | bytes 13762560 | tf_op jit(solution)/shard_map/td,tf->df/dot_general | solution.py:171
  598.2 5.5 all-gather.21.cloned.1.call-done
  603.7 4.4 convolution_convert_fusion.6
  610.6 118.6 %while.23 = (s32[]{:T(128)}, bf16[2,1024,3,5,64]{1,4,3,2,0:T(8,128)(2,1)}, bf16[2,1024,3,5,64]{1,4,3,2,0:T(8,128)(2,1)}, pred[2,1024]{1,0:T(4,128)(4,1)S(1)}, f3...) while((s32[]{:T(128)}, bf16[2,1024,3,5,64]{1,4,3,2,0:T(8,128)(2,1)}, ...), condition=%wide.region_15.16_spmd, body=%wide.region_13.15_spmd.sunk | while | flops 3441617920 | bytes 305546528 | solution.py:193
  614.9 2.9 fusion.131
  617.8 7.1 copy-done
  624.9 7.2 fusion.132
  632.1 15.0 %multiply_reduce_fusion.4 = (f32[5,1024]{1,0:T(8,128)S(1)}, f32[5,1024,1024]{1,2,0:T(8,128)}) fusion(f32[5,1024,1024]{1,2,0:T(8,128)} %copy-done, f32[5,1024]{1,0:T(8,128)S(1)} %dynamic-slice_bitcast_fusion.8, pred[1024]{0:T(1024)(128)(4,1)S(1)} %dynamic-slice_reduce_fusion.5, bf16[1024,3,5,64]{0,3,2,1:T(8,128)(2,1)} %copy-done.1, ...), kind=kOutput, calls=%fused_computation.20.clone.1 | convolution fusion | flops 697297920 | bytes 43295748 | tf_op jit(solution)/shard_map/while/body/eval_jaxpr/qhe,khe->hqk/dot_general | solution.py:70
  647.0 15.2 %multiply_convert_fusion.3 = bf16[5,1024,1024]{1,2,0:T(8,128)(2,1)S(1)} fusion(f32[5,1024,1024]{1,2,0:T(8,128)} %get-tuple-element.265, f32[5,1024,1024]{1,2,0:T(8,128)} %copy-done, f32[5,1024]{1,0:T(8,128)S(1)} %get-tuple-element.266, f32[5,1024]{1,0:T(8,128)S(1)} %dynamic-slice_bitcast_fusion.8, pred[1024]{0:T(1024)(128)(4,1)S(1)} %dynamic-slice_reduce_fusion.5), kind=kLoop, calls=%fused_computation.19.clone.1 | loop fusion | flops 31457280 | bytes 52470784 | tf_op jit(solution)/shard_map/while/body/eval_jaxpr/convert_element_type | solution.py:74
  664.2 3.3 fusion.133
  673.7 2.9 fusion.131
  676.7 7.1 copy-done
  683.8 7.2 fusion.132
  690.9 15.2 %multiply_reduce_fusion.4 = (f32[5,1024]{1,0:T(8,128)S(1)}, f32[5,1024,1024]{1,2,0:T(8,128)}) fusion(f32[5,1024,1024]{1,2,0:T(8,128)} %copy-done, f32[5,1024]{1,0:T(8,128)S(1)} %dynamic-slice_bitcast_fusion.8, pred[1024]{0:T(1024)(128)(4,1)S(1)} %dynamic-slice_reduce_fusion.5, bf16[1024,3,5,64]{0,3,2,1:T(8,128)(2,1)} %copy-done.1, ...), kind=kOutput, calls=%fused_computation.20.clone.1 | convolution fusion | flops 697297920 | bytes 43295748 | tf_op jit(solution)/shard_map/while/body/eval_jaxpr/qhe,khe->hqk/dot_general | solution.py:70
  706.1 15.4 %multiply_convert_fusion.3 = bf16[5,1024,1024]{1,2,0:T(8,128)(2,1)S(1)} fusion(f32[5,1024,1024]{1,2,0:T(8,128)} %get-tuple-element.265, f32[5,1024,1024]{1,2,0:T(8,128)} %copy-done, f32[5,1024]{1,0:T(8,128)S(1)} %get-tuple-element.266, f32[5,1024]{1,0:T(8,128)S(1)} %dynamic-slice_bitcast_fusion.8, pred[1024]{0:T(1024)(128)(4,1)S(1)} %dynamic-slice_reduce_fusion.5), kind=kLoop, calls=%fused_computation.19.clone.1 | loop fusion | flops 31457280 | bytes 52470784 | tf_op jit(solution)/shard_map/while/body/eval_jaxpr/convert_element_type | solution.py:74
  723.5 3.3 fusion.133
  729.2 8.1 copy.77
  737.3 10.0 reshape.180
  747.3 5.2 convolution_convert_fusion.5
  752.6 11.5 %fusion.43 = bf16[1280,3,320]{2,0,1:T(8,128)(2,1)} fusion(bf16[2048,3,320]{0,2,1:T(8,128)(2,1)} %reshape.180, bf16[2048,1280]{1,0:T(8,128)(2,1)} %all-gather.9.cloned.1.call-done), kind=kOutput, calls=%fused_computation.77 | convolution fusion | flops 5034393600 | bytes 11632640 | tf_op jit(solution)/shard_map/td,tcf->dcf/dot_general | solution.py:198
  764.2 10.6 bitcast_convert_fusion
  776.7 10.4 convolution_convert_fusion.1
  791.2 31.4 %reduce-scatter.22.cloned.1.call-done = bf16[40,1280]{1,0:T(8,128)(2,1)} async-done(((bf16[320,1280]{1,0:T(8,128)(2,1)}), bf16[40,1280]{1,0:T(8,128)(2,1)}) %reduce-scatter.22.cloned.1.call-update) | async-done | bytes 102416 | tf_op jit(solution)/shard_map/reduce_scatter | solution.py:221
  824.1 74.0 %reduce-scatter.20.cloned.1.call-done = bf16[160,3,320]{2,0,1:T(8,128)(2,1)} async-done(((bf16[1280,3,320]{2,0,1:T(8,128)(2,1)}), bf16[160,3,320]{2,0,1:T(8,128)(2,1)}) %reduce-scatter.20.cloned.1.call-update) | async-done | bytes 307216 | tf_op jit(solution)/shard_map/reduce_scatter | solution.py:218
  902.5 48.5 %reduce-scatter.18.cloned.1.call-done = bf16[512,1280]{1,0:T(8,128)(2,1)} async-done(((bf16[2048,1280]{1,0:T(8,128)(2,1)}), bf16[512,1280]{1,0:T(8,128)(2,1)}) %reduce-scatter.18.cloned.1.call-update) | async-done | bytes 1310736 | tf_op jit(solution)/shard_map/reduce_scatter | solution.py:202
  951.0 2.6 fusion.72
  953.6 10.3 psum.14
  964.9 40.1 %reduce-scatter.14.cloned.1.call-done = bf16[512,1280]{1,0:T(8,128)(2,1)} async-done(((bf16[2048,1280]{1,0:T(8,128)(2,1)}), bf16[512,1280]{1,0:T(8,128)(2,1)}) %reduce-scatter.14.cloned.1.call-update) | async-done | bytes 1310736 | tf_op jit(solution)/shard_map/reduce_scatter | solution.py:159
  1005.0 5.3 fusion.64
  1010.3 59.7 %reduce-scatter.28.cloned.1.call-done = bf16[160,4]{1,0:T(8,128)(2,1)} async-done(((bf16[1280,4]{1,0:T(8,128)(2,1)}), bf16[160,4]{1,0:T(8,128)(2,1)}) %reduce-scatter.28.cloned.1.call-update) | async-done | bytes 1296
  1072.1 40.2 %psum.15 = f32[]{:T(128)} all-reduce(f32[]{:T(128)S(6)} %add.190), channel_id=1, replica_groups=mesh['dp'=8,'tensor'=4] {'dp','tensor'}, use_global_device_ids=true, to_apply=%region_34.35 | all-reduce | flops 1 | bytes 8 | tf_op jit(solution)/shard_map/psum | solution.py:241
  1114.3 2.1 multiply_subtract_fusion.3
  1116.4 3.4 multiply_subtract_fusion.2
  (236 shorter events, 58.7 us)
Async XLA Ops:
  7.2 35.5 %copy-start.4 = (bf16[512,1280]{1,0:T(8,128)(2,1)S(1)}, bf16[512,1280]{1,0:T(8,128)(2,1)}, u32[]{:S(2)}) copy-start(bf16[512,1280]{1,0:T(8,128)(2,1)} %param.23) | copy-start | bytes 3932164
  7.2 37.2 %copy-start.23 = (f32[40,1280]{1,0:T(8,128)S(1)}, f32[40,1280]{1,0:T(8,128)}, u32[]{:S(2)}) copy-start(f32[40,1280]{1,0:T(8,128)} %param.28) | copy-start | bytes 614404
  7.2 77.8 %all-gather.11.cloned.1.call-start = ((), (), s32[]{:S(2)}) async-start(), calls=%async_computation.10 | async-start | bytes 3317760 | tf_op jit(solution)/shard_map/all_gather | solution.py:123
  9.3 35.2 %copy-start.55 = (s32[2,1024]{1,0:T(2,128)S(1)}, s32[2,1024]{1,0:T(2,128)}, u32[]{:S(2)}) copy-start(s32[2,1024]{1,0:T(2,128)} %param.26) | copy-start | bytes 24580
  9.3 35.2 %copy-start.58 = (s32[2]{0:T(128)S(1)}, s32[2]{0:T(128)}, u32[]{:S(2)}) copy-start(s32[2]{0:T(128)} %param.25) | copy-start | bytes 28
  9.3 117.7 %all-gather.9.cloned.1.call-start = ((), (), s32[]{:S(2)}) async-start(), calls=%async_computation.9 | async-start | bytes 6553600 | tf_op jit(solution)/shard_map/all_gather | solution.py:138
  44.3 204.0 %reduce-scatter.12.cloned.1.call-start = ((), (), s32[]{:S(2)}) async-start(), calls=%async_computation.11 | async-start | bytes 6553600 | tf_op jit(solution)/shard_map/reduce_scatter | solution.py:146
  153.5 4.0 copy-start.3
  157.5 5.0 copy-start.33
  171.4 4.0 copy-start.3
  175.4 5.0 copy-start.33
  187.5 9.2 copy-start.30
  187.5 4.2 copy-start.24
  196.8 51.6 %copy-start.5 = (bf16[512,1280]{1,0:T(8,128)(2,1)S(1)}, bf16[512,1280]{1,0:T(8,128)(2,1)}, u32[]{:S(2)}) copy-start(bf16[512,1280]{1,0:T(8,128)(2,1)} %param.23) | copy-start | bytes 3932164
  196.8 55.4 %copy-start.35 = (f32[1280]{0:T(1024)S(1)}, f32[1280]{0:T(1024)}, u32[]{:S(2)}) copy-start(f32[1280]{0:T(1024)} %get-tuple-element.136) | copy-start | bytes 15364
  196.8 55.4 %copy-start.47 = (f32[1280]{0:T(1024)S(1)}, f32[1280]{0:T(1024)}, u32[]{:S(2)}) copy-start(f32[1280]{0:T(1024)} %get-tuple-element.135) | copy-start | bytes 15364
  196.8 116.4 %all-gather.15.cloned.1.call-start = ((), (), s32[]{:S(2)}) async-start(), calls=%async_computation.13 | async-start | bytes 3686400 | tf_op jit(solution)/shard_map/all_gather | solution.py:125
  198.7 155.6 %all-gather.13.cloned.1.call-start = ((), (), s32[]{:S(2)}) async-start(), calls=%async_computation.12 | async-start | bytes 6553600 | tf_op jit(solution)/shard_map/all_gather | solution.py:153
  250.2 310.5 %copy-start.39 = (f32[512]{0:T(512)}, f32[512]{0:T(512)S(1)}, u32[]{:S(2)}) copy-start(f32[512]{0:T(512)S(1)} %broadcast_multiply_fusion.4) | copy-start | bytes 6148
  252.2 308.5 %copy-start.41 = (f32[512]{0:T(512)}, f32[512]{0:T(512)S(1)}, u32[]{:S(2)}) copy-start(f32[512]{0:T(512)S(1)} %add_rsqrt_fusion) | copy-start | bytes 6148
  254.0 165.2 %all-gather.17.cloned.1.call-start = ((), (), s32[]{:S(2)}) async-start(), calls=%async_computation.14 | async-start | bytes 3686400 | tf_op jit(solution)/shard_map/all_gather | solution.py:126
  254.9 205.0 %all-gather.19.cloned.1.call-start = ((), (), s32[]{:S(2)}) async-start(), calls=%async_computation.16 | async-start | bytes 6553600 | tf_op jit(solution)/shard_map/all_gather | solution.py:166
  255.6 301.7 %reduce-scatter.16.cloned.1.call-start = ((), (), s32[]{:S(2)}) async-start(), calls=%async_computation.17 | async-start | bytes 6553600 | tf_op jit(solution)/shard_map/reduce_scatter | solution.py:173
  459.9 37.2 %copy-start.60 = (bf16[1280,1280]{1,0:T(8,128)(2,1)S(1)}, bf16[1280,1280]{1,0:T(8,128)(2,1)}, u32[]{:S(2)}) copy-start(bf16[1280,1280]{1,0:T(8,128)(2,1)} %all-gather.15.cloned.1.call-done) | copy-start | bytes 9830404
  505.8 98.0 %all-gather.21.cloned.1.call-start = ((), (), s32[]{:S(2)}) async-start(), calls=%async_computation.18 | async-start | bytes 6553600 | tf_op jit(solution)/shard_map/all_gather | solution.py:186
  563.2 224.2 %reduce-scatter.26.cloned.1.call-start = ((), (), s32[]{:S(2)}) async-start(), calls=%async_computation.23 | async-start | bytes 3686400 | tf_op jit(solution)/shard_map/reduce_scatter | solution.py:227
  586.2 203.1 %reduce-scatter.24.cloned.1.call-start = ((), (), s32[]{:S(2)}) async-start(), calls=%async_computation.22 | async-start | bytes 3686400 | tf_op jit(solution)/shard_map/reduce_scatter | solution.py:224
  586.3 17.4 %copy-start.25 = (bf16[320,1280]{1,0:T(8,128)(2,1)S(1)}, bf16[320,1280]{1,0:T(8,128)(2,1)}, u32[]{:S(2)}) copy-start(bf16[320,1280]{1,0:T(8,128)(2,1)} %all_gather.30) | copy-start | bytes 2457604
  598.2 224.4 %reduce-scatter.22.cloned.1.call-start = ((), (), s32[]{:S(2)}) async-start(), calls=%async_computation.21 | async-start | bytes 921600 | tf_op jit(solution)/shard_map/reduce_scatter | solution.py:221
  617.8 7.1 copy-start
  647.0 15.2 %copy-start.2 = (bf16[1024,3,5,64]{0,3,2,1:T(8,128)(2,1)S(1)}, bf16[1024,3,5,64]{0,3,2,1:T(8,128)(2,1)}, u32[]{:S(2)}) copy-start(bf16[1024,3,5,64]{0,3,2,1:T(8,128)(2,1)} %copy-done.1) | copy-start | bytes 5898244 | tf_op jit(solution)/shard_map/while
  676.7 7.1 copy-start
  706.1 15.4 %copy-start.2 = (bf16[1024,3,5,64]{0,3,2,1:T(8,128)(2,1)S(1)}, bf16[1024,3,5,64]{0,3,2,1:T(8,128)(2,1)}, u32[]{:S(2)}) copy-start(bf16[1024,3,5,64]{0,3,2,1:T(8,128)(2,1)} %copy-done.1) | copy-start | bytes 5898244 | tf_op jit(solution)/shard_map/while
  737.3 10.0 copy-start.22
  752.6 11.6 %copy-start.61 = (bf16[1280,3,320]{2,0,1:T(8,128)(2,1)S(1)}, bf16[1280,3,320]{2,0,1:T(8,128)(2,1)}, u32[]{:S(2)}) copy-start(bf16[1280,3,320]{2,0,1:T(8,128)(2,1)} %all-gather.11.cloned.1.call-done) | copy-start | bytes 7372804
  752.6 145.5 %reduce-scatter.20.cloned.1.call-start = ((), (), s32[]{:S(2)}) async-start(), calls=%async_computation.20 | async-start | bytes 3317760 | tf_op jit(solution)/shard_map/reduce_scatter | solution.py:218
  764.1 186.8 %reduce-scatter.18.cloned.1.call-start = ((), (), s32[]{:S(2)}) async-start(), calls=%async_computation.19 | async-start | bytes 6553600 | tf_op jit(solution)/shard_map/reduce_scatter | solution.py:202
  774.8 230.1 %reduce-scatter.14.cloned.1.call-start = ((), (), s32[]{:S(2)}) async-start(), calls=%async_computation.15 | async-start | bytes 6553600 | tf_op jit(solution)/shard_map/reduce_scatter | solution.py:159
  787.1 4.0 copy-start.46
  787.1 4.0 copy-start.45
  787.1 163.8 %copy-start.6 = (bf16[512,1280]{1,0:T(8,128)(2,1)S(1)}, bf16[512,1280]{1,0:T(8,128)(2,1)}, u32[]{:S(2)}) copy-start(bf16[512,1280]{1,0:T(8,128)(2,1)} %param.23) | copy-start | bytes 3932164
  787.1 163.8 %copy-start.38 = (f32[1280]{0:T(1024)S(1)}, f32[1280]{0:T(1024)}, u32[]{:S(2)}) copy-start(f32[1280]{0:T(1024)} %copy-done.37) | copy-start | bytes 15364
  787.2 163.8 %copy-start.44 = (f32[512]{0:T(512)S(1)}, f32[512]{0:T(512)}, u32[]{:S(2)}) copy-start(f32[512]{0:T(512)} %copy-done.43) | copy-start | bytes 6148
  787.2 163.8 %copy-start.49 = (f32[512]{0:T(512)S(1)}, f32[512]{0:T(512)}, u32[]{:S(2)}) copy-start(f32[512]{0:T(512)} %copy-done.48) | copy-start | bytes 6148
  787.2 217.8 %copy-start.8 = (bf16[512,1280]{1,0:T(8,128)(2,1)S(1)}, bf16[512,1280]{1,0:T(8,128)(2,1)}, u32[]{:S(2)}) copy-start(bf16[512,1280]{1,0:T(8,128)(2,1)} %reduce-scatter.12.cloned.1.call-done) | copy-start | bytes 3932164
  787.2 217.7 %copy-start.36 = (f32[1280]{0:T(1024)S(1)}, f32[1280]{0:T(1024)}, u32[]{:S(2)}) copy-start(f32[1280]{0:T(1024)} %get-tuple-element.136) | copy-start | bytes 15364
  787.2 217.7 %copy-start.40 = (f32[512]{0:T(512)S(1)}, f32[512]{0:T(512)}, u32[]{:S(2)}) copy-start(f32[512]{0:T(512)} %copy-done.39) | copy-start | bytes 6148
  787.2 217.7 %copy-start.42 = (f32[512]{0:T(512)S(1)}, f32[512]{0:T(512)}, u32[]{:S(2)}) copy-start(f32[512]{0:T(512)} %copy-done.41) | copy-start | bytes 6148
  787.2 217.7 %copy-start.51 = (f32[512]{0:T(512)S(1)}, f32[512]{0:T(512)}, u32[]{:S(2)}) copy-start(f32[512]{0:T(512)} %copy-done.50) | copy-start | bytes 6148
  787.2 217.7 %copy-start.53 = (f32[512]{0:T(512)S(1)}, f32[512]{0:T(512)}, u32[]{:S(2)}) copy-start(f32[512]{0:T(512)} %copy-done.52) | copy-start | bytes 6148
  787.3 282.7 %reduce-scatter.28.cloned.1.call-start = ((), (), s32[]{:S(2)}) async-start(), calls=%async_computation.24 | async-start | bytes 368640
  964.8 148.9 %copy-start.54 = (f32[4,160]{1,0:T(4,128)S(1)}, f32[4,160]{1,0:T(4,128)}, u32[]{:S(2)}) copy-start(f32[4,160]{1,0:T(4,128)} %param.31) | copy-start | bytes 7684
  964.8 148.9 %copy-start.56 = (f32[4,160]{1,0:T(4,128)S(1)}, f32[4,160]{1,0:T(4,128)}, u32[]{:S(2)}) copy-start(f32[4,160]{1,0:T(4,128)} %param.40) | copy-start | bytes 7684
  964.8 148.9 %copy-start.57 = (f32[4,160]{1,0:T(4,128)S(1)}, f32[4,160]{1,0:T(4,128)}, u32[]{:S(2)}) copy-start(f32[4,160]{1,0:T(4,128)} %param.41) | copy-start | bytes 7684
  964.8 149.5 %copy-start.32 = (bf16[40,1280]{1,0:T(8,128)(2,1)S(1)}, bf16[40,1280]{1,0:T(8,128)(2,1)}, u32[]{:S(2)}) copy-start(bf16[40,1280]{1,0:T(8,128)(2,1)} %reduce-scatter.22.cloned.1.call-done) | copy-start | bytes 307204
  964.9 151.5 %copy-start.18 = (f32[160,3,320]{2,0,1:T(8,128)S(1)}, f32[160,3,320]{2,0,1:T(8,128)}, u32[]{:S(2)}) copy-start(f32[160,3,320]{2,0,1:T(8,128)} %param.27) | copy-start | bytes 1843204
  1010.3 109.5 %copy-start.15 = (f32[160,1280]{1,0:T(8,128)S(1)}, f32[160,1280]{1,0:T(8,128)}, u32[]{:S(2)}) copy-start(f32[160,1280]{1,0:T(8,128)} %param.30) | copy-start | bytes 2457604
  1010.3 109.5 %copy-start.19 = (bf16[160,1280]{1,0:T(8,128)(2,1)S(1)}, bf16[160,1280]{1,0:T(8,128)(2,1)}, u32[]{:S(2)}) copy-start(bf16[160,1280]{1,0:T(8,128)(2,1)} %reduce-scatter.26.cloned.1.call-done) | copy-start | bytes 1228804
  1010.3 109.5 %copy-start.26 = (f32[160,1280]{1,0:T(8,128)S(1)}, f32[160,1280]{1,0:T(8,128)}, u32[]{:S(2)}) copy-start(f32[160,1280]{1,0:T(8,128)} %param.38) | copy-start | bytes 2457604
  1113.1 6.7 copy-start.27
  1116.4 5.4 copy-start.17
  1116.4 5.4 copy-start.20
  1116.4 5.4 copy-start.28
  1116.4 5.4 copy-start.29
  (24 other events, 55.6 us)
Sparse Core Ops, SparseCore 0:
  10.8 74.1 all-gather.10
  87.1 39.8 all-gather.8
  196.9 51.3 reduce-scatter.11
  251.2 61.9 all-gather.14
  315.3 38.9 all-gather.12
  357.2 61.9 all-gather.16
  420.8 38.9 all-gather.18
  505.9 51.3 reduce-scatter.15
  563.3 40.4 all-gather.20
  607.2 76.2 reduce-scatter.25
  687.5 75.0 reduce-scatter.23
  766.3 56.1 reduce-scatter.21
  826.5 71.5 reduce-scatter.19
  900.5 50.4 reduce-scatter.17
  953.5 51.3 reduce-scatter.13
  1008.6 61.3 reduce-scatter.27
where the time goes:
time: 1140 us; the launch traced here: 1130 us
  waiting for transfers between devices  599 us (53%)
  matrix products  218 us (19%)
  blocking collectives  115 us (10%)
  other arithmetic  99.2 us (9%)
  local copies, waits for them, and re-layouts  79.2 us (7%)
  between operations  20 us (2%)
    reduce_scatter x1, waiting for transfers between devices, on_device(): lax.psum_scatter(grad_qkv.astype(jnp.bfloat16), 'dp', scatter_dimension=0...  74 us
    unnamed x17, waiting for transfers between devices  60.7 us
    all_gather x1, waiting for transfers between devices, on_device(): lax.all_gather(up_weight.astype(jnp.bfloat16), 'dp', axis=0, tiled=True)  57.5 us
    all_gather x1, waiting for transfers between devices, on_device(): lax.all_gather(down_weight.astype(jnp.bfloat16), 'dp', axis=0, tiled=True)  52.7 us
    reduce_scatter x1, waiting for transfers between devices, on_device(): lax.psum_scatter(jnp.einsum('tf,df->td', row_block, up_full, preferred_el...  51.3 us
    reduce_scatter x1, waiting for transfers between devices, on_device(): lax.psum_scatter(jnp.dot(row_block, out_full, preferred_element_type=jnp....  49.6 us
    reduce_scatter x1, waiting for transfers between devices, on_device(): lax.psum_scatter(jnp.einsum('tcf,dcf->td', row_block, qkv_full, preferred...  48.5 us
    all_gather x1, waiting for transfers between devices, on_device(): lax.all_gather(ln_one.astype(jnp.bfloat16), 'tensor', axis=0, tiled=True)  42 us
  transfers between devices with their start and end apart: 16, of which 14 were waited for; matrix products, arithmetic and copies ran while one was open for 21% of the time, Pallas kernels for 0%

commit v1 on v0

v1 whole, which is shorter than its diff:
```python
import functools

import jax
import jax.numpy as jnp
from jax import lax
from jax.experimental import pallas as pl
from jax.experimental.pallas import tpu as pltpu
from jax.sharding import PartitionSpec as P

HD = 64
STEP = 5

NORM_EPS = 1e-05
CLIP_LIMIT = 1.0
BETA_FIRST = 0.5
BETA_SECOND = 0.5
ADAM_EPS = 1e-08
DECAY_RATE = 0.01
RATE_QKV = 0.03
RATE_OUT = 0.5
RATE_UP = 0.03
RATE_DOWN = 0.015
RATE_NORM = 0.2

F32 = jnp.float32
BF16 = jnp.bfloat16
NN = (((1,), (0,)), ((), ()))
NT = (((1,), (1,)), ((), ()))
TN = (((0,), (0,)), ((), ()))
VMEM = pl.BlockSpec(memory_space=pltpu.VMEM)


def dot(left, right, dims=NN):
    return lax.dot_general(left, right, dims, preferred_element_type=F32)


def widen(block, columns, lane):
    rows = block.shape[0]
    wide = jnp.concatenate([block.astype(F32), jnp.zeros((rows, HD), F32)], axis=1)
    for n, column in enumerate(columns):
        wide = jnp.where(lane == HD + n, column, wide)
    return wide.astype(BF16)


def minus_parts(column):
    high = column.astype(BF16).astype(F32)
    rest = column - high
    middle = rest.astype(BF16).astype(F32)
    return [-high, -middle, middle - rest]


def attend_kernel(heads, step, qkv_ref, bias_ref, ctx_ref, lse_ref, keys):
    tokens = qkv_ref.shape[0]
    width = heads * HD
    lane = lax.broadcasted_iota(jnp.int32, (1, 2 * HD), 1)
    for h in range(heads):
        keys[h] = widen(qkv_ref[:, width + h * HD : width + (h + 1) * HD], [bias_ref[...]], lane)

    def block(n, _):
        rows = pl.ds(pl.multiple_of(n * step, step), step)
        outs = []
        stat = jnp.zeros((step, 2 * HD), F32)
        for h in range(heads):
            query = qkv_ref[rows, h * HD : (h + 1) * HD].astype(F32) * HD ** (-0.5)
            scores = dot(widen(query, [jnp.ones((step, 1), F32)], lane), keys[h], NT)
            top = jnp.max(scores, axis=1, keepdims=True)
            weights = jnp.exp(scores - top)
            total = jnp.sum(weights, axis=1, keepdims=True)
            values = qkv_ref[:, 2 * width + h * HD : 2 * width + (h + 1) * HD]
            outs.append((dot(weights.astype(BF16), values) / total).astype(BF16))
            stat = jnp.where(lane == h, top + jnp.log(total), stat)
        ctx_ref[rows, :] = jnp.concatenate(outs, axis=1)
        lse_ref[rows, :] = stat
        return 0

    lax.fori_loop(0, tokens // step, block, 0)


def attend(qkv, bias, heads, step=512):
    tokens = qkv.shape[0]
    return pl.pallas_call(
        functools.partial(attend_kernel, heads, step),
        out_shape=(
            jax.ShapeDtypeStruct((tokens, heads * HD), BF16),
            jax.ShapeDtypeStruct((tokens, 2 * HD), F32),
        ),
        in_specs=[VMEM] * 2,
        out_specs=[VMEM] * 2,
        scratch_shapes=[pltpu.VMEM((heads, tokens, 2 * HD), BF16)],
        compiler_params=pltpu.CompilerParams(vmem_limit_bytes=48 * 2**20),
        cost_estimate=pl.CostEstimate(
            flops=16 * heads * tokens * tokens * HD,
            bytes_accessed=10 * tokens * heads * HD,
            transcendentals=heads * tokens * tokens,
        ),
        name="attend",
    )(qkv, bias)


def attend_back_kernel(
    heads, step, qkv_ref, bias_ref, ctx_ref, lse_ref, grad_ref, out_ref, keys, values, dk, dv
):
    tokens = qkv_ref.shape[0]
    width = heads * HD
    scale = HD ** (-0.5)
    lane = lax.broadcasted_iota(jnp.int32, (1, 2 * HD), 1)
    one = jnp.ones((tokens, 1), F32)
    for h in range(heads):
        key = qkv_ref[:, width + h * HD : width + (h + 1) * HD]
        value = qkv_ref[:, 2 * width + h * HD : 2 * width + (h + 1) * HD]
        keys[h] = widen(key, [bias_ref[...], one, one, one], lane)
        values[h] = widen(value, [one, one, one], lane)
    dk[...] = jnp.zeros_like(dk)
    dv[...] = jnp.zeros_like(dv)

    def block(n, _):
        rows = pl.ds(pl.multiple_of(n * step, step), step)
        outs = []
        ones = jnp.ones((step, 1), F32)
        for h in range(heads):
            cols = slice(h * HD, (h + 1) * HD)
            query = qkv_ref[rows, cols].astype(F32) * scale
            grad = grad_ref[rows, cols].astype(F32)
            delta = jnp.sum(grad * ctx_ref[rows, cols].astype(F32), axis=1, keepdims=True)
            lse = lse_ref[rows, h : h + 1]
            weights = jnp.exp(dot(widen(query, [ones] + minus_parts(lse), lane), keys[h], NT))
            slopes = dot(widen(grad, minus_parts(delta), lane), values[h], NT)
            slopes = (weights * slopes).astype(BF16)
            weights = weights.astype(BF16)
            key = qkv_ref[:, width + h * HD : width + (h + 1) * HD]
            outs.append((dot(slopes, key) * scale).astype(BF16))
            dk[h] += dot(query.T.astype(BF16), slopes)
            dv[h] += dot(grad.T.astype(BF16), weights)
        out_ref[rows, :width] = jnp.concatenate(outs, axis=1)
        return 0

    lax.fori_loop(0, tokens // step, block, 0)
    for place, total in ((1, dk), (2, dv)):
        turned = jnp.concatenate([total[h].T for h in range(heads)], axis=1)
        out_ref[:, place * width : (place + 1) * width] = turned.astype(BF16)


def attend_back(qkv, bias, ctx, lse, grad, heads, step=256):
    tokens = qkv.shape[0]
    return pl.pallas_call(
        functools.partial(attend_back_kernel, heads, step),
        out_shape=jax.ShapeDtypeStruct((tokens, 3 * heads * HD), BF16),
        in_specs=[VMEM] * 5,
        out_specs=VMEM,
        scratch_shapes=[pltpu.VMEM((heads, tokens, 2 * HD), BF16)] * 2
        + [pltpu.VMEM((heads, HD, tokens), F32)] * 2,
        compiler_params=pltpu.CompilerParams(vmem_limit_bytes=48 * 2**20),
        cost_estimate=pl.CostEstimate(
            flops=40 * heads * tokens * tokens * HD,
            bytes_accessed=20 * tokens * heads * HD,
            transcendentals=heads * tokens * tokens,
        ),
        name="attend_back",
    )(qkv, bias, ctx, lse, grad)


def swap(value, axis, bits):
    size = lax.axis_size(axis)
    return lax.ppermute(value, axis, [(i, i ^ bits) for i in range(size)])


def core_swap(value):
    return swap(value, "tensor", 1)


def side_swap(value):
    return swap(value, "tensor", 2)


def dp_split(size):
    fast = 2 if size < 16 else 4
    return size // fast, fast


def gather_rows(shard):
    slow, fast = dp_split(lax.axis_size("dp"))
    blocks = []
    for k in range(slow):
        block = swap(shard, "dp", k * fast) if k else shard
        blocks.append([swap(block, "dp", j) if j else block for j in range(fast)])
    return assemble(blocks, slow, fast)


def assemble(blocks, slow, fast):
    rows, columns = blocks[0][0].shape
    index = lax.axis_index("dp")
    place = jnp.stack([index // fast, index % fast]).astype(jnp.int32)
    flat = [b for line in blocks for b in line]

    def kernel(place_ref, *refs):
        ins, out, sems = refs[: slow * fast], refs[-2], refs[-1]
        copies = []
        for n, source in enumerate(ins):
            k, j = n // fast, n % fast
            target = (place_ref[0] ^ k) * fast + (place_ref[1] ^ j)
            copies.append(pltpu.make_async_copy(source, out.at[target], sems.at[n]))
        for copy in copies:
            copy.start()
        for copy in copies:
            copy.wait()

    out = pl.pallas_call(
        kernel,
        out_shape=jax.ShapeDtypeStruct((slow * fast, rows, columns), shard_type(flat[0])),
        in_specs=[pl.BlockSpec(memory_space=pltpu.SMEM)] + [pl.BlockSpec(memory_space=pl.ANY)] * len(flat),
        out_specs=pl.BlockSpec(memory_space=pl.ANY),
        scratch_shapes=[pltpu.SemaphoreType.DMA((slow * fast,))],
        name="assemble",
    )(place, *flat)
    return out.reshape(slow * fast * rows, columns)


def shard_type(value):
    return value.dtype


def scatter_rows(total):
    slow, fast = dp_split(lax.axis_size("dp"))
    rows = total.shape[0] // (slow * fast)
    index = lax.axis_index("dp")
    high, low = index // fast, index % fast

    def part(k, j):
        start = ((high ^ k) * fast + (low ^ j)) * rows
        return lax.dynamic_slice_in_dim(total, start, rows, 0)

    result = None
    for k in list(range(1, slow)) + [0]:
        line = part(k, 0).astype(F32)
        for j in range(1, fast):
            line = line + swap(part(k, j), "dp", j).astype(F32)
        if k:
            line = swap(line.astype(BF16), "dp", k * fast).astype(F32)
        result = line if result is None else result + line
    return result


def gather_tokens(own):
    near = jnp.concatenate([own, core_swap(own)])
    side = side_swap(own)
    far = jnp.concatenate([side, core_swap(side)])
    return near, far


def half_sum(partial):
    half = partial.shape[0] // 2
    return partial[:half].astype(F32) + core_swap(partial[half:]).astype(F32)


def send_far(partial):
    return side_swap(half_sum(partial).astype(BF16)).astype(F32)


def sum_all(value):
    for axis in ("tensor", "dp"):
        bits = 1
        while bits < lax.axis_size(axis):
            value = value + swap(value, axis, bits)
            bits *= 2
    return value


def layer_norm_parts(values, gain_row, shift_row):
    centered = values - jnp.mean(values, axis=-1, keepdims=True)
    inverse = lax.rsqrt(jnp.mean(centered * centered, axis=-1, keepdims=True) + NORM_EPS)
    normed = centered * inverse
    return (normed * gain_row + shift_row, normed, inverse)


def layer_norm_back(grad_normed, normed, inverse, gain_row):
    scaled = grad_normed * gain_row
    return inverse * (
        scaled
        - jnp.mean(scaled, axis=-1, keepdims=True)
        - normed * jnp.mean(scaled * normed, axis=-1, keepdims=True)
    )


def adam_update(master, grad_sum, moment_one, moment_two, step_rate, clip_factor):
    clipped = grad_sum * clip_factor
    one_new = BETA_FIRST * moment_one + (1.0 - BETA_FIRST) * clipped
    two_new = BETA_SECOND * moment_two + (1.0 - BETA_SECOND) * clipped * clipped
    one_hat = one_new / (1.0 - BETA_FIRST**STEP)
    two_hat = two_new / (1.0 - BETA_SECOND**STEP)
    master_new = master - step_rate * (
        one_hat / (jnp.sqrt(two_hat) + ADAM_EPS) + DECAY_RATE * master
    )
    return (master_new, one_new, two_new)


def gelu_parts(value):
    share = 0.5 * lax.erfc(value * -(0.5**0.5))
    slope = share + value * jnp.exp(-0.5 * value * value) * (0.5 / jnp.pi) ** 0.5
    return (value * share).astype(BF16), slope.astype(BF16)


def on_device(
    tokens,
    cotangent,
    lengths,
    key_mask,
    qkv_weight,
    out_weight,
    up_weight,
    down_weight,
    norm_params,
    qkv_first,
    qkv_second,
    out_first,
    out_second,
    up_first,
    up_second,
    down_first,
    down_second,
    norm_first,
    norm_second,
):
    own, width = tokens.shape
    cell = 2 * own
    heads = qkv_weight.shape[2] // HD
    dp, tensor = lax.axis_index("dp"), lax.axis_index("tensor")
    side, core = tensor // 2, tensor % 2

    norm_rows = norm_params.shape[1]
    norm_low = lax.all_gather(norm_params.astype(BF16), "dp", axis=1, tiled=True)
    norm_values = norm_low.astype(F32)

    positions = jnp.arange(cell, dtype=jnp.int32)
    key_valid = (positions[None, :] < lengths[:, None]) & (
        (key_mask == 1) | (positions[None, :] == 0)
    )
    bias = jnp.where(key_valid, 0.0, -1e30).astype(F32)
    bias = jnp.where(side == 0, bias, bias[::-1])
    bias = jnp.where(core == 0, bias, jnp.roll(bias, own, axis=1))
    bias_near, bias_far = bias[0][:, None], bias[1][:, None]

    qkv_full = gather_rows(qkv_weight.astype(BF16).reshape(qkv_weight.shape[0], -1))
    out_full = gather_rows(out_weight.astype(BF16))
    up_full = gather_rows(up_weight.astype(BF16))
    down_full = gather_rows(down_weight.astype(BF16))

    stream_in = tokens.astype(F32)
    ln_one, normed_one, inverse_one = layer_norm_parts(stream_in, norm_values[0], norm_values[1])
    one_near, one_far = gather_tokens(ln_one.astype(BF16))
    qkv_far = dot(one_far, qkv_full).astype(BF16)
    ctx_far, lse_far = attend(qkv_far, bias_far, heads)
    out_far = send_far(dot(ctx_far, out_full).astype(BF16))
    qkv_near = dot(one_near, qkv_full).astype(BF16)
    ctx_near, lse_near = attend(qkv_near, bias_near, heads)
    out_near = half_sum(dot(ctx_near, out_full).astype(BF16))
    residual = stream_in + (out_near + out_far)

    ln_two, normed_two, inverse_two = layer_norm_parts(residual, norm_values[2], norm_values[3])
    two_near, two_far = gather_tokens(ln_two.astype(BF16))
    grad_near, grad_far = gather_tokens(cotangent)
    hid_near, slope_near = gelu_parts(dot(two_near, up_full))
    hid_far, slope_far = gelu_parts(dot(two_far, up_full))
    pre_far = (dot(grad_far, down_full, NT) * slope_far.astype(F32)).astype(BF16)
    back_far = send_far(dot(pre_far, up_full, NT).astype(BF16))
    pre_near = (dot(grad_near, down_full, NT) * slope_near.astype(F32)).astype(BF16)
    back_near = half_sum(dot(pre_near, up_full, NT).astype(BF16))
    grad_ln_two = back_near + back_far

    hid = jnp.concatenate([hid_near, hid_far])
    grad_group = jnp.concatenate([grad_near, grad_far])
    two_group = jnp.concatenate([two_near, two_far])
    pre = jnp.concatenate([pre_near, pre_far])
    grad_down = dot(hid, grad_group, TN).astype(BF16)
    summed_down = scatter_rows(grad_down)
    grad_up = dot(two_group, pre, TN).astype(BF16)
    summed_up = scatter_rows(grad_up)

    last_far = send_far(dot(hid_far, down_full).astype(BF16))
    last_near = half_sum(dot(hid_near, down_full).astype(BF16))
    layer_out = (residual + (last_near + last_far)).astype(BF16)

    grad_residual = cotangent.astype(F32) + layer_norm_back(
        grad_ln_two, normed_two, inverse_two, norm_values[2]
    )
    gain_two = jnp.sum(grad_ln_two * normed_two, axis=0)
    shift_two = jnp.sum(grad_ln_two, axis=0)

    res_near, res_far = gather_tokens(grad_residual.astype(BF16))
    dctx_near = dot(res_near, out_full, NT).astype(BF16)
    dqkv_near = attend_back(qkv_near, bias_near, ctx_near, lse_near, dctx_near, heads)
    dctx_far = dot(res_far, out_full, NT).astype(BF16)
    dqkv_far = attend_back(qkv_far, bias_far, ctx_far, lse_far, dctx_far, heads)
    first_far = send_far(dot(dqkv_far, qkv_full, NT).astype(BF16))
    first_near = half_sum(dot(dqkv_near, qkv_full, NT).astype(BF16))
    one_group = jnp.concatenate([one_near, one_far])
    dqkv = jnp.concatenate([dqkv_near, dqkv_far])
    grad_qkv = dot(one_group, dqkv, TN).astype(BF16)
    summed_qkv = scatter_rows(grad_qkv)
    res_group = jnp.concatenate([res_near, res_far])
    ctx = jnp.concatenate([ctx_near, ctx_far])
    grad_out = dot(ctx, res_group, TN).astype(BF16)
    summed_out = scatter_rows(grad_out)

    grad_ln_one = first_near + first_far
    input_grad = (
        grad_residual + layer_norm_back(grad_ln_one, normed_one, inverse_one, norm_values[0])
    ).astype(BF16)
    gain_one = jnp.sum(grad_ln_one * normed_one, axis=0)
    shift_one = jnp.sum(grad_ln_one, axis=0)

    local_squares = (
        jnp.sum(summed_qkv * summed_qkv)
        + jnp.sum(summed_out * summed_out)
        + jnp.sum(summed_up * summed_up)
        + jnp.sum(summed_down * summed_down)
    )
    rows = jnp.stack([gain_one, shift_one, gain_two, shift_two])
    packed = jnp.concatenate([rows, jnp.full((4, 128), local_squares, F32)], axis=1)
    packed = sum_all(packed)
    norm_grad = packed[:, :width]
    squares_total = packed[0, width] + jnp.sum(norm_grad * norm_grad)
    summed_norm = lax.dynamic_slice_in_dim(norm_grad, dp * norm_rows, norm_rows, 1)
    grad_norm = jnp.sqrt(squares_total)
    clip_factor = jnp.minimum(1.0, CLIP_LIMIT / grad_norm)

    qkv_new, qkv_one, qkv_two = adam_update(
        qkv_weight,
        summed_qkv.reshape(qkv_weight.shape),
        qkv_first,
        qkv_second,
        RATE_QKV,
        clip_factor,
    )
    out_new, out_one, out_two = adam_update(
        out_weight, summed_out, out_first, out_second, RATE_OUT, clip_factor
    )
    up_new, up_one, up_two = adam_update(
        up_weight, summed_up, up_first, up_second, RATE_UP, clip_factor
    )
    down_new, down_one, down_two = adam_update(
        down_weight, summed_down, down_first, down_second, RATE_DOWN, clip_factor
    )
    norm_new, norm_one, norm_two = adam_update(
        norm_params, summed_norm, norm_first, norm_second, RATE_NORM, clip_factor
    )
    shift_grad = clip_factor * summed_norm[3]
    return (
        layer_out,
        input_grad,
        grad_norm,
        qkv_new,
        qkv_one,
        qkv_two,
        out_new,
        out_one,
        out_two,
        up_new,
        up_one,
        up_two,
        down_new,
        down_one,
        down_two,
        norm_new,
        norm_one,
        norm_two,
        shift_grad,
    )


def solution(mesh):
    tokens = P(("dp", "tensor"), None)
    columns = P("dp", None, "tensor")
    rows = P(("tensor", "dp"), None)
    both = P("dp", "tensor")
    norms = P(None, "dp")
    return jax.shard_map(
        on_device,
        mesh=mesh,
        in_specs=(tokens, tokens, P("dp"), P("dp", None), columns, rows, both, rows, norms)
        + (columns,) * 2
        + (rows,) * 2
        + (both,) * 2
        + (rows,) * 2
        + (norms,) * 2,
        out_specs=(tokens, tokens, P())
        + (columns,) * 3
        + (rows,) * 3
        + (both,) * 3
        + (rows,) * 3
        + (norms,) * 3
        + (P("dp"),),
        check_vma=False,
    )
```

time: 1140 us -> 984 us (0.86)
  Pallas kernels: 0 us -> 366 us
  waiting for transfers between devices: 599 us -> 270 us
  starting transfers between devices: 0.84 us -> 92.2 us
  blocking collectives: 115 us -> 27.8 us
  matrix products: 218 us -> 133 us
  local copies, waits for them, and re-layouts: 79.2 us -> 22.4 us
  other arithmetic: 99.2 us -> 53.8 us
  between operations: 20 us -> 7.9 us
    pallas_call x0 -> x8, Pallas kernels: none -> 366 us  [the longest x4 310 us: assemble(): pl.pallas_call(kernel, out_shape=jax.ShapeDtypeStruct((slow * fast, rows,...]
    reduce_scatter x8 -> x0, waiting for transfers between devices: 295 us -> none  [the longest x1 74 us: on_device(): lax.psum_scatter(grad_qkv.astype(jnp.bfloat16), 'dp', scatter_dimension=0...]
    ppermute x0 -> x85, waiting for transfers between devices: none -> 270 us  [swap(): return lax.ppermute(value, axis, [(i, i ^ bits) for i in range(size)])]
    all_gather x7 -> x0, waiting for transfers between devices: 244 us -> none  [the longest x1 57.5 us: on_device(): lax.all_gather(up_weight.astype(jnp.bfloat16), 'dp', axis=0, tiled=True)]
    ppermute x0 -> x85, starting transfers between devices: none -> 92.2 us  [swap(): return lax.ppermute(value, axis, [(i, i ^ bits) for i in range(size)])]
    dot_general x26 -> x20, matrix products: 218 us -> 133 us  [dot(): return lax.dot_general(left, right, dims, preferred_element_type=F32)]
    unnamed x17 -> x0, waiting for transfers between devices: 60.7 us -> none
    psum x2 -> x0, blocking collectives: 50.5 us -> none  [the longest x1 40.2 us: on_device(): squares_total = lax.psum(local_squares, ('dp', 'tensor'))]
  transfers between devices with their start and end apart: 16 -> 85, of which waited for: 14 -> 28; matrix products, arithmetic and copies ran while one was open for 21% -> 18% of each run, Pallas kernels for 0% -> 38%
where the time goes in v1:
time: 984 us; the launch traced here: 974 us
  Pallas kernels  366 us (37%)
  waiting for transfers between devices  270 us (27%)
  matrix products  133 us (14%)
  starting transfers between devices  92.2 us (9%)
  other arithmetic  53.8 us (5%)
  blocking collectives  27.8 us (3%)
  local copies, waits for them, and re-layouts  22.4 us (2%)
    pallas_call x4, Pallas kernels, assemble(): pl.pallas_call(kernel, out_shape=jax.ShapeDtypeStruct((slow * fast, rows,...  310 us
    ppermute x85, waiting for transfers between devices, swap(): return lax.ppermute(value, axis, [(i, i ^ bits) for i in range(size)])  270 us
    dot_general x20, matrix products, dot(): return lax.dot_general(left, right, dims, preferred_element_type=F32)  133 us
    ppermute x85, starting transfers between devices, swap(): return lax.ppermute(value, axis, [(i, i ^ bits) for i in range(size)])  92.2 us
    pallas_call x2, Pallas kernels, attend_back(): pl.pallas_call(functools.partial(attend_back_kernel, heads, step), out_sh...  38.4 us
    all_gather x1, blocking collectives, on_device(): lax.all_gather(norm_params.astype(BF16), 'dp', axis=1, tiled=True)  27.8 us
  transfers between devices with their start and end apart: 85, of which 28 were waited for; matrix products, arithmetic and copies ran while one was open for 18% of the time, Pallas kernels for 38%

profile of v1, /device:TPU:0, one launch (start us, length us, event | category | flops | bytes accessed | tf_op | source)
XLA Modules:
  0.0 973.6 jit_solution(7620368211871422581)
XLA Ops:
  1.5 27.8 %all-gather = bf16[8,160,4]{1,2,0:T(4,128)(2,1)S(1)} all-gather(bf16[1,160,4]{1,2,0:T(4,128)(2,1)S(1)} %convert_bitcast_fusion), channel_id=1, replica_groups=mesh['dp'=8,'tensor'=4] {'dp'}, dimensions={0}, use_global_device_ids=true | all-gather | bytes 11520 | tf_op jit(solution)/shard_map/all_gather | solution.py:330
  41.1 18.5 %collective-permute-done.16 = bf16[512,1280]{1,0:T(8,128)(2,1)} collective-permute-done((bf16[512,1280]{1,0:T(8,128)(2,1)S(1)}, bf16[512,1280]{1,0:T(8,128)(2,1)}, u32[]{:S(2)}, u32[]{:S(2)}) %collective-permute-start.16) | collective-permute-done | bytes 1310752 | tf_op jit(solution)/shard_map/ppermute | solution.py:164
  62.5 2.9 collective-permute-start.4
  67.3 4.2 collective-permute-done.12.refs_5_
  72.0 4.1 collective-permute-done.14.refs_7_
  79.2 9.0 collective-permute-done.4.refs_4_
  91.5 26.7 %assemble.5 = bf16[8,40,1280]{2,1,0:T(8,128)(2,1)} custom-call(s32[2]{0:T(128)} %pad_add_fusion.place_ref, bf16[40,1280]{1,0:T(8,128)(2,1)} %copy-done.55, bf16[40,1280]{1,0:T(8,128)(2,1)} %copy-done.76, bf16[40,1280]{1,0:T(8,128)(2,1)} %copy-done.77, bf16[40,1280]{1,0:T(8,128)(2,1)} %collective-permute-done.10.refs_3_, bf16[40,1280]{1,0:T(8,128)(2,1)} %copy-done.78, ...), custom_call_target="tpu_custom_call" | custom-call | tf_op jit(solution)/shard_map/assemble/pallas_call | solution.py:207
  118.3 81.3 %assemble.4 = bf16[8,160,960]{2,1,0:T(8,128)(2,1)} custom-call(s32[2]{0:T(128)} %pad_add_fusion.place_ref, bf16[160,960]{1,0:T(8,128)(2,1)} %copy-done.44, bf16[160,960]{1,0:T(8,128)(2,1)} %collective-permute-done.1.refs_1_, bf16[160,960]{1,0:T(8,128)(2,1)} %copy-done.69, bf16[160,960]{1,0:T(8,128)(2,1)} %collective-permute-done.3.refs_3_, ...), custom_call_target="tpu_custom_call" | custom-call | tf_op jit(solution)/shard_map/assemble/pallas_call | solution.py:207
  199.6 5.4 fusion.118.qkv_ref
  205.0 8.8 attend.3
  217.1 4.4 fusion.121.qkv_ref
  221.5 9.0 attend.2
  235.2 6.4 collective-permute-start.29
  244.1 19.7 %collective-permute-done.19 = bf16[512,1280]{1,0:T(8,128)(2,1)S(1)} collective-permute-done((bf16[512,1280]{1,0:T(8,128)(2,1)S(1)}, bf16[512,1280]{1,0:T(8,128)(2,1)S(1)}, u32[]{:S(2)}, u32[]{:S(2)}) %collective-permute-start.19) | collective-permute-done | bytes 1310752 | tf_op jit(solution)/shard_map/ppermute | solution.py:164
  265.7 6.4 collective-permute-start.22
  278.5 5.1 collective-permute-done.22.refs_2_
  283.6 24.1 %collective-permute-done.24.refs_4_ = bf16[160,1280]{1,0:T(8,128)(2,1)} collective-permute-done((bf16[160,1280]{1,0:T(8,128)(2,1)S(1)}, bf16[160,1280]{1,0:T(8,128)(2,1)}, u32[]{:S(2)}, u32[]{:S(2)}) %collective-permute-start.24) | collective-permute-done | bytes 409632 | tf_op jit(solution)/shard_map/ppermute | solution.py:164
  309.7 10.4 %collective-permute-done.30.refs_3_ = bf16[160,1280]{1,0:T(8,128)(2,1)S(1)} collective-permute-done((bf16[160,1280]{1,0:T(8,128)(2,1)S(1)}, bf16[160,1280]{1,0:T(8,128)(2,1)S(1)}, u32[]{:S(2)}, u32[]{:S(2)}) %collective-permute-start.30) | collective-permute-done | bytes 409632 | tf_op jit(solution)/shard_map/ppermute | solution.py:164
  320.6 8.4 collective-permute-done.32.refs_5_
  329.4 8.2 collective-permute-done.34.refs_7_
  338.1 8.3 collective-permute-done.23.refs_3_
  347.0 101.1 %assemble.7 = bf16[8,160,1280]{2,1,0:T(8,128)(2,1)} custom-call(s32[2]{0:T(128)} %pad_add_fusion.place_ref, bf16[160,1280]{1,0:T(8,128)(2,1)} %copy-done.40, bf16[160,1280]{1,0:T(8,128)(2,1)} %copy-done.60, bf16[160,1280]{1,0:T(8,128)(2,1)} %copy-done.61, bf16[160,1280]{1,0:T(8,128)(2,1)} %copy-done.66, bf16[160,1280]{1,0:T(8,128)(2,1)} %copy-done.63, ...), custom_call_target="tpu_custom_call" | custom-call | tf_op jit(solution)/shard_map/assemble/pallas_call | solution.py:207
  448.2 101.1 %assemble.6 = bf16[8,160,1280]{2,1,0:T(8,128)(2,1)} custom-call(s32[2]{0:T(128)} %pad_add_fusion.place_ref, bf16[160,1280]{1,0:T(8,128)(2,1)} %copy-done.39, bf16[160,1280]{1,0:T(8,128)(2,1)} %copy-done.62, bf16[160,1280]{1,0:T(8,128)(2,1)} %copy-done.65, bf16[160,1280]{1,0:T(8,128)(2,1)} %copy-done.67, bf16[160,1280]{1,0:T(8,128)(2,1)} %collective-permute-done.24.refs_4_, ...), custom_call_target="tpu_custom_call" | custom-call | tf_op jit(solution)/shard_map/assemble/pallas_call | solution.py:207
  550.0 18.6 %multiply_convert_fusion.3 = (bf16[1024,1280]{1,0:T(8,128)(2,1)}, f32[1024,1280]{1,0:T(8,128)S(1)}, f32[1024,1280]{1,0:T(8,128)}) fusion(bf16[1280,1280]{1,0:T(8,128)(2,1)} %bitcast.49, bf16[512,1280]{1,0:T(8,128)(2,1)} %collective-permute-done.20, bf16[512,1280]{1,0:T(8,128)(2,1)} %add_convert_fusion.4), kind=kOutput, calls=%fused_computation.71 | convolution fusion | flops 3444572160 | bytes 19005440 | tf_op jit(solution)/shard_map/dot_general | solution.py:34
  568.6 8.3 multiply_convert_fusion.1
  577.0 5.3 convolution_convert_fusion.3
  584.5 3.7 convolution_convert_fusion.5
  589.8 18.1 %multiply_convert_fusion.2 = (bf16[1024,1280]{1,0:T(8,128)(2,1)}, f32[1024,1280]{1,0:T(8,128)}, f32[1024,1280]{1,0:T(8,128)}) fusion(bf16[1280,1280]{1,0:T(8,128)(2,1)S(1)} %bitcast.51, bf16[512,1280]{1,0:T(8,128)(2,1)S(1)} %collective-permute-done.37, bf16[512,1280]{1,0:T(8,128)(2,1)} %collective-permute-done.36), kind=kOutput, calls=%fused_computation.58 | convolution fusion | flops 3444572160 | bytes 19005440 | tf_op jit(solution)/shard_map/dot_general | solution.py:34
  608.0 9.3 multiply_convert_fusion
  617.3 5.3 convolution_convert_fusion.2
  625.8 4.0 convolution_convert_fusion.4
  631.0 10.8 %convolution_convert_fusion.1 = bf16[1280,1280]{1,0:T(8,128)(2,1)S(1)} fusion(bf16[512,1280]{1,0:T(8,128)(2,1)S(1)} %copy-done.99, bf16[512,1280]{1,0:T(8,128)(2,1)} %collective-permute-done.36, bf16[512,1280]{1,0:T(8,128)(2,1)} %collective-permute-done.20, bf16[512,1280]{1,0:T(8,128)(2,1)} %add_convert_fusion.4, ...), kind=kOutput, calls=%fused_computation.5 | convolution fusion | flops 6743982080 | bytes 13762560 | tf_op jit(solution)/shard_map/dot_general | solution.py:34
  645.0 2.7 add_convert_fusion.1
  648.3 2.7 add_convert_fusion.3
  652.6 11.1 %convolution_convert_fusion = bf16[1280,1280]{1,0:T(8,128)(2,1)S(1)} fusion(bf16[1024,1280]{1,0:T(8,128)(2,1)} %get-tuple-element.64, bf16[1024,1280]{1,0:T(8,128)(2,1)} %get-tuple-element.62, bf16[512,1280]{1,0:T(8,128)(2,1)} %copy-done.97, bf16[512,1280]{1,0:T(8,128)(2,1)} %collective-permute-done.42, bf16[512,1280]{1,0:T(8,128)(2,1)} %collective-permute-done.40, ...), kind=kOutput, calls=%fused_computation.4 | convolution fusion | flops 6743982080 | bytes 13762560 | tf_op jit(solution)/shard_map/dot_general | solution.py:34
  665.3 14.2 %collective-permute-done.45 = bf16[512,1280]{1,0:T(8,128)(2,1)S(1)} collective-permute-done((bf16[512,1280]{1,0:T(8,128)(2,1)}, bf16[512,1280]{1,0:T(8,128)(2,1)S(1)}, u32[]{:S(2)}, u32[]{:S(2)}) %collective-permute-start.45) | collective-permute-done | bytes 1310752 | tf_op jit(solution)/shard_map/ppermute | solution.py:164
  682.6 24.7 %collective-permute-done.39 = bf16[512,1280]{1,0:T(8,128)(2,1)} collective-permute-done((bf16[512,1280]{1,0:T(8,128)(2,1)}, bf16[512,1280]{1,0:T(8,128)(2,1)}, u32[]{:S(2)}, u32[]{:S(2)}) %collective-permute-start.39) | collective-permute-done | bytes 1310752 | tf_op jit(solution)/shard_map/ppermute | solution.py:164
  707.3 5.0 fusion.159
  718.4 7.0 collective-permute-done.73
  726.9 7.2 collective-permute-done.77
  735.7 7.2 collective-permute-done.75
  747.4 3.2 fusion.130
  752.1 19.2 %attend_back.2 = bf16[1024,960]{1,0:T(8,128)(2,1)S(1)} custom-call(bf16[1024,960]{1,0:T(8,128)(2,1)} %copy-done.9, f32[1024,1]{1,0:T(8,128)S(1)} %copy-done.3, bf16[1024,320]{1,0:T(8,128)(2,1)S(1)} %copy-done.7, f32[1024,128]{1,0:T(8,128)S(1)} %get-tuple-element.25.lse_ref, bf16[1024,320]{1,0:T(8,128)(2,1)S(1)} %copy.76.grad_ref), custom_call_target="tpu_custom_call" | custom-call | flops 13421772800 | bytes 6553600 | tf_op jit(solution)/shard_map/attend_back/pallas_call | solution.py:145
  771.3 3.2 convolution_convert_fusion.9
  777.5 3.2 fusion.127
  782.2 19.2 %attend_back.3 = bf16[1024,960]{1,0:T(8,128)(2,1)S(1)} custom-call(bf16[1024,960]{1,0:T(8,128)(2,1)} %copy-done.8, f32[1024,1]{1,0:T(8,128)S(1)} %copy-done.1, bf16[1024,320]{1,0:T(8,128)(2,1)S(1)} %copy-done.5, f32[1024,128]{1,0:T(8,128)S(1)} %get-tuple-element.26.lse_ref, bf16[1024,320]{1,0:T(8,128)(2,1)S(1)} %copy.78.grad_ref), custom_call_target="tpu_custom_call" | custom-call | flops 13421772800 | bytes 6553600 | tf_op jit(solution)/shard_map/attend_back/pallas_call | solution.py:145
  801.5 3.2 convolution_convert_fusion.8
  805.3 8.6 fusion.65
  813.9 4.5 fusion.76
  829.0 16.6 %collective-permute-done.67 = bf16[160,1280]{1,0:T(8,128)(2,1)S(1)} collective-permute-done((bf16[160,1280]{1,0:T(8,128)(2,1)S(1)}, bf16[160,1280]{1,0:T(8,128)(2,1)S(1)}, u32[]{:S(2)}, u32[]{:S(2)}) %collective-permute-start.67) | collective-permute-done | bytes 409632 | tf_op jit(solution)/shard_map/ppermute | solution.py:164
  847.7 13.7 %collective-permute-done.76 = bf16[160,1280]{1,0:T(8,128)(2,1)S(1)} collective-permute-done((bf16[160,1280]{1,0:T(8,128)(2,1)S(1)}, bf16[160,1280]{1,0:T(8,128)(2,1)S(1)}, u32[]{:S(2)}, u32[]{:S(2)}) %collective-permute-start.76) | collective-permute-done | bytes 409632 | tf_op jit(solution)/shard_map/ppermute | solution.py:164
  866.5 8.0 collective-permute-done.65
  877.7 4.7 collective-permute-start.62
  883.3 4.3 collective-permute-done.62
  889.6 2.5 collective-permute-start.53
  892.1 2.9 multiply_reduce_fusion.6
  896.4 7.3 collective-permute-done.57
  903.7 26.7 %collective-permute-done.55 = bf16[160,960]{0,1:T(8,128)(2,1)S(1)} collective-permute-done((bf16[160,960]{0,1:T(8,128)(2,1)S(1)}, bf16[160,960]{0,1:T(8,128)(2,1)S(1)}, u32[]{:S(2)}, u32[]{:S(2)}) %collective-permute-start.55) | collective-permute-done | bytes 307232 | tf_op jit(solution)/shard_map/ppermute | solution.py:164
  934.2 3.3 fusion.86
  940.4 2.4 collective-permute-done.81
  944.1 3.3 collective-permute-done.82
  947.5 3.8 collective-permute-done.83
  952.4 4.3 fusion.85
  963.2 3.2 multiply_subtract_fusion.2
  (426 shorter events, 128.0 us)
Async XLA Ops:
  33.6 26.1 %collective-permute-start.16 = (bf16[512,1280]{1,0:T(8,128)(2,1)S(1)}, bf16[512,1280]{1,0:T(8,128)(2,1)}, u32[]{:S(2)}, u32[]{:S(2)}) collective-permute-start(bf16[512,1280]{1,0:T(8,128)(2,1)S(1)} %fusion.80), channel_id=1, source_target_pairs={{0,2},{1,3},{2,0},{3,1},{4,6},{5,7},{6,4},{7,5},{8,10},{9,11},{10,... | collective-permute-start | bytes 3932168 | tf_op jit(solution)/shard_map/ppermute | solution.py:164
  35.2 27.2 %collective-permute-start.8 = (bf16[40,1280]{1,0:T(8,128)(2,1)S(1)}, bf16[40,1280]{1,0:T(8,128)(2,1)S(1)}, u32[]{:S(2)}, u32[]{:S(2)}) collective-permute-start(bf16[40,1280]{1,0:T(8,128)(2,1)S(1)} %convert_element_type.357.refs_0_), channel_id=1, source_target_pairs={{0,4},{4,0},{8,12},{12,8},{16,20},{20,16},{24,28},{28,24},{1,5},{5... | collective-permute-start | bytes 307208 | tf_op jit(solution)/shard_map/ppermute | solution.py:164
  36.7 23.2 %collective-permute-start.9 = (bf16[40,1280]{1,0:T(8,128)(2,1)S(1)}, bf16[40,1280]{1,0:T(8,128)(2,1)S(1)}, u32[]{:S(2)}, u32[]{:S(2)}) collective-permute-start(bf16[40,1280]{1,0:T(8,128)(2,1)S(1)} %convert_element_type.357.refs_0_), channel_id=1, source_target_pairs={{0,8},{4,12},{8,0},{12,4},{16,24},{20,28},{24,16},{28,20},{1,9},{5... | collective-permute-start | bytes 307208 | tf_op jit(solution)/shard_map/ppermute | solution.py:164
  37.0 25.5 %collective-permute-start.11 = (bf16[40,1280]{1,0:T(8,128)(2,1)S(1)}, bf16[40,1280]{1,0:T(8,128)(2,1)S(1)}, u32[]{:S(2)}, u32[]{:S(2)}) collective-permute-start(bf16[40,1280]{1,0:T(8,128)(2,1)S(1)} %convert_element_type.357.refs_0_), channel_id=1, source_target_pairs={{0,16},{4,20},{8,24},{12,28},{16,0},{20,4},{24,8},{28,12},{1,17},{... | collective-permute-start | bytes 307208 | tf_op jit(solution)/shard_map/ppermute | solution.py:164
  39.1 26.3 %collective-permute-start.13 = (bf16[40,1280]{1,0:T(8,128)(2,1)S(1)}, bf16[40,1280]{1,0:T(8,128)(2,1)S(1)}, u32[]{:S(2)}, u32[]{:S(2)}) collective-permute-start(bf16[40,1280]{1,0:T(8,128)(2,1)S(1)} %convert_element_type.357.refs_0_), channel_id=1, source_target_pairs={{0,24},{4,28},{8,16},{12,20},{16,8},{20,12},{24,0},{28,4},{1,25},{... | collective-permute-start | bytes 307208 | tf_op jit(solution)/shard_map/ppermute | solution.py:164
  59.7 139.9 %collective-permute-start.17 = (bf16[512,1280]{1,0:T(8,128)(2,1)}, bf16[512,1280]{1,0:T(8,128)(2,1)}, u32[]{:S(2)}, u32[]{:S(2)}) collective-permute-start(bf16[512,1280]{1,0:T(8,128)(2,1)} %collective-permute-done.16), channel_id=1, source_target_pairs={{0,1},{1,0},{2,3},{3,2},{4,5},{5,4},{6,7},{7,6},{8,9},{9,8},{10,11... | collective-permute-start | bytes 3932168 | tf_op jit(solution)/shard_map/ppermute | solution.py:164
  62.4 16.4 %collective-permute-start.2 = (bf16[160,960]{1,0:T(8,128)(2,1)S(1)}, bf16[160,960]{1,0:T(8,128)(2,1)S(1)}, u32[]{:S(2)}, u32[]{:S(2)}) collective-permute-start(bf16[160,960]{1,0:T(8,128)(2,1)S(1)} %reshape.104.refs_0_), channel_id=1, source_target_pairs={{0,8},{4,12},{8,0},{12,4},{16,24},{20,28},{24,16},{28,20},{1,9},{5... | collective-permute-start | bytes 921608 | tf_op jit(solution)/shard_map/ppermute | solution.py:164
  62.5 25.7 %collective-permute-start.4 = (bf16[160,960]{1,0:T(8,128)(2,1)S(1)}, bf16[160,960]{1,0:T(8,128)(2,1)}, u32[]{:S(2)}, u32[]{:S(2)}) collective-permute-start(bf16[160,960]{1,0:T(8,128)(2,1)S(1)} %reshape.104.refs_0_), channel_id=1, source_target_pairs={{0,16},{4,20},{8,24},{12,28},{16,0},{20,4},{24,8},{28,12},{1,17},{... | collective-permute-start | bytes 921608 | tf_op jit(solution)/shard_map/ppermute | solution.py:164
  65.4 23.3 %collective-permute-start.6 = (bf16[160,960]{1,0:T(8,128)(2,1)S(1)}, bf16[160,960]{1,0:T(8,128)(2,1)}, u32[]{:S(2)}, u32[]{:S(2)}) collective-permute-start(bf16[160,960]{1,0:T(8,128)(2,1)S(1)} %reshape.104.refs_0_), channel_id=1, source_target_pairs={{0,24},{4,28},{8,16},{12,20},{16,8},{20,12},{24,0},{28,4},{1,25},{... | collective-permute-start | bytes 921608 | tf_op jit(solution)/shard_map/ppermute | solution.py:164
  76.2 42.0 %collective-permute-start.1 = (bf16[160,960]{1,0:T(8,128)(2,1)S(1)}, bf16[160,960]{1,0:T(8,128)(2,1)}, u32[]{:S(2)}, u32[]{:S(2)}) collective-permute-start(bf16[160,960]{1,0:T(8,128)(2,1)S(1)} %reshape.104.refs_0_), channel_id=1, source_target_pairs={{0,4},{4,0},{8,12},{12,8},{16,20},{20,16},{24,28},{28,24},{1,5},{5... | collective-permute-start | bytes 921608 | tf_op jit(solution)/shard_map/ppermute | solution.py:164
  78.8 39.5 %collective-permute-start.3 = (bf16[160,960]{1,0:T(8,128)(2,1)S(1)}, bf16[160,960]{1,0:T(8,128)(2,1)}, u32[]{:S(2)}, u32[]{:S(2)}) collective-permute-start(bf16[160,960]{1,0:T(8,128)(2,1)S(1)} %collective-permute-done.2.refs_2_), channel_id=1, source_target_pairs={{0,4},{4,0},{8,12},{12,8},{16,20},{20,16},{24,28},{28,24},{1,5},{5... | collective-permute-start | bytes 921608 | tf_op jit(solution)/shard_map/ppermute | solution.py:164
  88.2 30.1 %collective-permute-start.5 = (bf16[160,960]{1,0:T(8,128)(2,1)}, bf16[160,960]{1,0:T(8,128)(2,1)}, u32[]{:S(2)}, u32[]{:S(2)}) collective-permute-start(bf16[160,960]{1,0:T(8,128)(2,1)} %collective-permute-done.4.refs_4_), channel_id=1, source_target_pairs={{0,4},{4,0},{8,12},{12,8},{16,20},{20,16},{24,28},{28,24},{1,5},{5... | collective-permute-start | bytes 921608 | tf_op jit(solution)/shard_map/ppermute | solution.py:164
  88.7 29.6 %collective-permute-start.7 = (bf16[160,960]{1,0:T(8,128)(2,1)}, bf16[160,960]{1,0:T(8,128)(2,1)}, u32[]{:S(2)}, u32[]{:S(2)}) collective-permute-start(bf16[160,960]{1,0:T(8,128)(2,1)} %collective-permute-done.6.refs_6_), channel_id=1, source_target_pairs={{0,4},{4,0},{8,12},{12,8},{16,20},{20,16},{24,28},{28,24},{1,5},{5... | collective-permute-start | bytes 921608 | tf_op jit(solution)/shard_map/ppermute | solution.py:164
  118.2 97.8 %collective-permute-start = (bf16[512,1280]{1,0:T(8,128)(2,1)S(1)}, bf16[512,1280]{1,0:T(8,128)(2,1)}, u32[]{:S(2)}, u32[]{:S(2)}) collective-permute-start(bf16[512,1280]{1,0:T(8,128)(2,1)S(1)} %fusion.80), channel_id=1, source_target_pairs={{0,1},{1,0},{2,3},{3,2},{4,5},{5,4},{6,7},{7,6},{8,9},{9,8},{10,11... | collective-permute-start | bytes 3932168 | tf_op jit(solution)/shard_map/ppermute | solution.py:164
  215.4 17.3 %collective-permute-start.18 = (bf16[512,1280]{1,0:T(8,128)(2,1)S(1)}, bf16[512,1280]{1,0:T(8,128)(2,1)S(1)}, u32[]{:S(2)}, u32[]{:S(2)}) collective-permute-start(bf16[512,1280]{1,0:T(8,128)(2,1)S(1)} %slice.121), channel_id=1, source_target_pairs={{0,1},{1,0},{2,3},{3,2},{4,5},{5,4},{6,7},{7,6},{8,9},{9,8},{10,11... | collective-permute-start | bytes 3932168 | tf_op jit(solution)/shard_map/ppermute | solution.py:164
  233.0 30.8 %collective-permute-start.19 = (bf16[512,1280]{1,0:T(8,128)(2,1)S(1)}, bf16[512,1280]{1,0:T(8,128)(2,1)S(1)}, u32[]{:S(2)}, u32[]{:S(2)}) collective-permute-start(bf16[512,1280]{1,0:T(8,128)(2,1)S(1)} %add_convert_fusion.5), channel_id=1, source_target_pairs={{0,2},{1,3},{2,0},{3,1},{4,6},{5,7},{6,4},{7,5},{8,10},{9,11},{10,... | collective-permute-start | bytes 3932168 | tf_op jit(solution)/shard_map/ppermute | solution.py:164
  234.6 31.0 %collective-permute-start.28 = (bf16[160,1280]{1,0:T(8,128)(2,1)S(1)}, bf16[160,1280]{1,0:T(8,128)(2,1)S(1)}, u32[]{:S(2)}, u32[]{:S(2)}) collective-permute-start(bf16[160,1280]{1,0:T(8,128)(2,1)S(1)} %convert_element_type.370.refs_0_), channel_id=1, source_target_pairs={{0,4},{4,0},{8,12},{12,8},{16,20},{20,16},{24,28},{28,24},{1,5},{5... | collective-permute-start | bytes 1228808 | tf_op jit(solution)/shard_map/ppermute | solution.py:164
  235.2 36.9 %collective-permute-start.29 = (bf16[160,1280]{1,0:T(8,128)(2,1)S(1)}, bf16[160,1280]{1,0:T(8,128)(2,1)S(1)}, u32[]{:S(2)}, u32[]{:S(2)}) collective-permute-start(bf16[160,1280]{1,0:T(8,128)(2,1)S(1)} %convert_element_type.370.refs_0_), channel_id=1, source_target_pairs={{0,8},{4,12},{8,0},{12,4},{16,24},{20,28},{24,16},{28,20},{1,9},{5... | collective-permute-start | bytes 1228808 | tf_op jit(solution)/shard_map/ppermute | solution.py:164
  241.6 31.5 %collective-permute-start.31 = (bf16[160,1280]{1,0:T(8,128)(2,1)S(1)}, bf16[160,1280]{1,0:T(8,128)(2,1)S(1)}, u32[]{:S(2)}, u32[]{:S(2)}) collective-permute-start(bf16[160,1280]{1,0:T(8,128)(2,1)S(1)} %convert_element_type.370.refs_0_), channel_id=1, source_target_pairs={{0,16},{4,20},{8,24},{12,28},{16,0},{20,4},{24,8},{28,12},{1,17},{... | collective-permute-start | bytes 1228808 | tf_op jit(solution)/shard_map/ppermute | solution.py:164
  242.6 33.8 %collective-permute-start.33 = (bf16[160,1280]{1,0:T(8,128)(2,1)S(1)}, bf16[160,1280]{1,0:T(8,128)(2,1)S(1)}, u32[]{:S(2)}, u32[]{:S(2)}) collective-permute-start(bf16[160,1280]{1,0:T(8,128)(2,1)S(1)} %convert_element_type.370.refs_0_), channel_id=1, source_target_pairs={{0,24},{4,28},{8,16},{12,20},{16,8},{20,12},{24,0},{28,4},{1,25},{... | collective-permute-start | bytes 1228808 | tf_op jit(solution)/shard_map/ppermute | solution.py:164
  265.7 17.9 %collective-permute-start.22 = (bf16[160,1280]{1,0:T(8,128)(2,1)S(1)}, bf16[160,1280]{1,0:T(8,128)(2,1)S(1)}, u32[]{:S(2)}, u32[]{:S(2)}) collective-permute-start(bf16[160,1280]{1,0:T(8,128)(2,1)S(1)} %convert_element_type.368.refs_0_), channel_id=1, source_target_pairs={{0,8},{4,12},{8,0},{12,4},{16,24},{20,28},{24,16},{28,20},{1,9},{5... | collective-permute-start | bytes 1228808 | tf_op jit(solution)/shard_map/ppermute | solution.py:164
  272.1 35.6 %collective-permute-start.24 = (bf16[160,1280]{1,0:T(8,128)(2,1)S(1)}, bf16[160,1280]{1,0:T(8,128)(2,1)}, u32[]{:S(2)}, u32[]{:S(2)}) collective-permute-start(bf16[160,1280]{1,0:T(8,128)(2,1)S(1)} %convert_element_type.368.refs_0_), channel_id=1, source_target_pairs={{0,16},{4,20},{8,24},{12,28},{16,0},{20,4},{24,8},{28,12},{1,17},{... | collective-permute-start | bytes 1228808 | tf_op jit(solution)/shard_map/ppermute | solution.py:164
  273.1 35.0 %collective-permute-start.26 = (bf16[160,1280]{1,0:T(8,128)(2,1)S(1)}, bf16[160,1280]{1,0:T(8,128)(2,1)}, u32[]{:S(2)}, u32[]{:S(2)}) collective-permute-start(bf16[160,1280]{1,0:T(8,128)(2,1)S(1)} %convert_element_type.368.refs_0_), channel_id=1, source_target_pairs={{0,24},{4,28},{8,16},{12,20},{16,8},{20,12},{24,0},{28,4},{1,25},{... | collective-permute-start | bytes 1228808 | tf_op jit(solution)/shard_map/ppermute | solution.py:164
  276.4 272.9 %collective-permute-start.42 = (bf16[512,1280]{1,0:T(8,128)(2,1)S(1)}, bf16[512,1280]{1,0:T(8,128)(2,1)}, u32[]{:S(2)}, u32[]{:S(2)}) collective-permute-start(bf16[512,1280]{1,0:T(8,128)(2,1)S(1)} %copy-done.41), channel_id=1, source_target_pairs={{0,2},{1,3},{2,0},{3,1},{4,6},{5,7},{6,4},{7,5},{8,10},{9,11},{10,... | collective-permute-start | bytes 3932168 | tf_op jit(solution)/shard_map/ppermute | solution.py:164
  277.8 272.1 %collective-permute-start.36 = (bf16[512,1280]{1,0:T(8,128)(2,1)}, bf16[512,1280]{1,0:T(8,128)(2,1)}, u32[]{:S(2)}, u32[]{:S(2)}) collective-permute-start(bf16[512,1280]{1,0:T(8,128)(2,1)} %add_convert_fusion.4), channel_id=1, source_target_pairs={{0,2},{1,3},{2,0},{3,1},{4,6},{5,7},{6,4},{7,5},{8,10},{9,11},{10,... | collective-permute-start | bytes 3932168 | tf_op jit(solution)/shard_map/ppermute | solution.py:164
  283.6 266.4 %collective-permute-start.20 = (bf16[512,1280]{1,0:T(8,128)(2,1)}, bf16[512,1280]{1,0:T(8,128)(2,1)}, u32[]{:S(2)}, u32[]{:S(2)}) collective-permute-start(bf16[512,1280]{1,0:T(8,128)(2,1)} %add_convert_fusion.4), channel_id=1, source_target_pairs={{0,1},{1,0},{2,3},{3,2},{4,5},{5,4},{6,7},{7,6},{8,9},{9,8},{10,11... | collective-permute-start | bytes 3932168 | tf_op jit(solution)/shard_map/ppermute | solution.py:164
  308.2 20.8 %collective-permute-start.32 = (bf16[160,1280]{1,0:T(8,128)(2,1)S(1)}, bf16[160,1280]{1,0:T(8,128)(2,1)}, u32[]{:S(2)}, u32[]{:S(2)}) collective-permute-start(bf16[160,1280]{1,0:T(8,128)(2,1)S(1)} %collective-permute-done.31.refs_4_), channel_id=1, source_target_pairs={{0,4},{4,0},{8,12},{12,8},{16,20},{20,16},{24,28},{28,24},{1,5},{5... | collective-permute-start | bytes 1228808 | tf_op jit(solution)/shard_map/ppermute | solution.py:164
  320.1 17.6 %collective-permute-start.34 = (bf16[160,1280]{1,0:T(8,128)(2,1)S(1)}, bf16[160,1280]{1,0:T(8,128)(2,1)S(1)}, u32[]{:S(2)}, u32[]{:S(2)}) collective-permute-start(bf16[160,1280]{1,0:T(8,128)(2,1)S(1)} %collective-permute-done.33.refs_6_), channel_id=1, source_target_pairs={{0,4},{4,0},{8,12},{12,8},{16,20},{20,16},{24,28},{28,24},{1,5},{5... | collective-permute-start | bytes 1228808 | tf_op jit(solution)/shard_map/ppermute | solution.py:164
  328.9 17.4 %collective-permute-start.23 = (bf16[160,1280]{1,0:T(8,128)(2,1)S(1)}, bf16[160,1280]{1,0:T(8,128)(2,1)S(1)}, u32[]{:S(2)}, u32[]{:S(2)}) collective-permute-start(bf16[160,1280]{1,0:T(8,128)(2,1)S(1)} %collective-permute-done.22.refs_2_), channel_id=1, source_target_pairs={{0,4},{4,0},{8,12},{12,8},{16,20},{20,16},{24,28},{28,24},{1,5},{5... | collective-permute-start | bytes 1228808 | tf_op jit(solution)/shard_map/ppermute | solution.py:164
  337.6 110.5 %collective-permute-start.25 = (bf16[160,1280]{1,0:T(8,128)(2,1)}, bf16[160,1280]{1,0:T(8,128)(2,1)}, u32[]{:S(2)}, u32[]{:S(2)}) collective-permute-start(bf16[160,1280]{1,0:T(8,128)(2,1)} %collective-permute-done.24.refs_4_), channel_id=1, source_target_pairs={{0,4},{4,0},{8,12},{12,8},{16,20},{20,16},{24,28},{28,24},{1,5},{5... | collective-permute-start | bytes 1228808 | tf_op jit(solution)/shard_map/ppermute | solution.py:164
  346.4 101.8 %collective-permute-start.27 = (bf16[160,1280]{1,0:T(8,128)(2,1)}, bf16[160,1280]{1,0:T(8,128)(2,1)}, u32[]{:S(2)}, u32[]{:S(2)}) collective-permute-start(bf16[160,1280]{1,0:T(8,128)(2,1)} %collective-permute-done.26.refs_6_), channel_id=1, source_target_pairs={{0,4},{4,0},{8,12},{12,8},{16,20},{20,16},{24,28},{28,24},{1,5},{5... | collective-permute-start | bytes 1228808 | tf_op jit(solution)/shard_map/ppermute | solution.py:164
  448.1 120.5 %collective-permute-start.40 = (bf16[512,1280]{1,0:T(8,128)(2,1)S(1)}, bf16[512,1280]{1,0:T(8,128)(2,1)}, u32[]{:S(2)}, u32[]{:S(2)}) collective-permute-start(bf16[512,1280]{1,0:T(8,128)(2,1)S(1)} %copy-done.41), channel_id=1, source_target_pairs={{0,1},{1,0},{2,3},{3,2},{4,5},{5,4},{6,7},{7,6},{8,9},{9,8},{10,11... | collective-permute-start | bytes 3932168 | tf_op jit(solution)/shard_map/ppermute | solution.py:164
  549.3 58.7 %collective-permute-start.43 = (bf16[512,1280]{1,0:T(8,128)(2,1)}, bf16[512,1280]{1,0:T(8,128)(2,1)S(1)}, u32[]{:S(2)}, u32[]{:S(2)}) collective-permute-start(bf16[512,1280]{1,0:T(8,128)(2,1)} %collective-permute-done.42), channel_id=1, source_target_pairs={{0,1},{1,0},{2,3},{3,2},{4,5},{5,4},{6,7},{7,6},{8,9},{9,8},{10,11... | collective-permute-start | bytes 3932168 | tf_op jit(solution)/shard_map/ppermute | solution.py:164
  549.9 40.0 %collective-permute-start.37 = (bf16[512,1280]{1,0:T(8,128)(2,1)}, bf16[512,1280]{1,0:T(8,128)(2,1)S(1)}, u32[]{:S(2)}, u32[]{:S(2)}) collective-permute-start(bf16[512,1280]{1,0:T(8,128)(2,1)} %collective-permute-done.36), channel_id=1, source_target_pairs={{0,1},{1,0},{2,3},{3,2},{4,5},{5,4},{6,7},{7,6},{8,9},{9,8},{10,11... | collective-permute-start | bytes 3932168 | tf_op jit(solution)/shard_map/ppermute | solution.py:164
  583.5 80.3 %collective-permute-start.41 = (bf16[512,1280]{1,0:T(8,128)(2,1)}, bf16[512,1280]{1,0:T(8,128)(2,1)S(1)}, u32[]{:S(2)}, u32[]{:S(2)}) collective-permute-start(bf16[512,1280]{1,0:T(8,128)(2,1)} %slice.129), channel_id=1, source_target_pairs={{0,1},{1,0},{2,3},{3,2},{4,5},{5,4},{6,7},{7,6},{8,9},{9,8},{10,11... | collective-permute-start | bytes 3932168 | tf_op jit(solution)/shard_map/ppermute | solution.py:164
  589.4 93.2 %collective-permute-start.35 = (bf16[512,1280]{1,0:T(8,128)(2,1)}, bf16[512,1280]{1,0:T(8,128)(2,1)}, u32[]{:S(2)}, u32[]{:S(2)}) collective-permute-start(bf16[512,1280]{1,0:T(8,128)(2,1)} %slice.125), channel_id=1, source_target_pairs={{0,1},{1,0},{2,3},{3,2},{4,5},{5,4},{6,7},{7,6},{8,9},{9,8},{10,11... | collective-permute-start | bytes 3932168 | tf_op jit(solution)/shard_map/ppermute | solution.py:164
  623.8 20.6 %collective-permute-start.44 = (bf16[512,1280]{1,0:T(8,128)(2,1)}, bf16[512,1280]{1,0:T(8,128)(2,1)}, u32[]{:S(2)}, u32[]{:S(2)}) collective-permute-start(bf16[512,1280]{1,0:T(8,128)(2,1)} %slice.131), channel_id=1, source_target_pairs={{0,1},{1,0},{2,3},{3,2},{4,5},{5,4},{6,7},{7,6},{8,9},{9,8},{10,11... | collective-permute-start | bytes 3932168 | tf_op jit(solution)/shard_map/ppermute | solution.py:164
  630.9 17.4 %collective-permute-start.38 = (bf16[512,1280]{1,0:T(8,128)(2,1)}, bf16[512,1280]{1,0:T(8,128)(2,1)}, u32[]{:S(2)}, u32[]{:S(2)}) collective-permute-start(bf16[512,1280]{1,0:T(8,128)(2,1)} %slice.127), channel_id=1, source_target_pairs={{0,1},{1,0},{2,3},{3,2},{4,5},{5,4},{6,7},{7,6},{8,9},{9,8},{10,11... | collective-permute-start | bytes 3932168 | tf_op jit(solution)/shard_map/ppermute | solution.py:164
  642.8 71.8 %collective-permute-start.66 = (bf16[160,1280]{1,0:T(8,128)(2,1)}, bf16[160,1280]{1,0:T(8,128)(2,1)S(1)}, u32[]{:S(2)}, u32[]{:S(2)}) collective-permute-start(bf16[160,1280]{1,0:T(8,128)(2,1)} %get-tuple-element.78), channel_id=1, source_target_pairs={{0,4},{4,0},{8,12},{12,8},{16,20},{20,16},{24,28},{28,24},{1,5},{5... | collective-permute-start | bytes 1228808 | tf_op jit(solution)/shard_map/ppermute | solution.py:164
  647.7 31.8 %collective-permute-start.45 = (bf16[512,1280]{1,0:T(8,128)(2,1)}, bf16[512,1280]{1,0:T(8,128)(2,1)S(1)}, u32[]{:S(2)}, u32[]{:S(2)}) collective-permute-start(bf16[512,1280]{1,0:T(8,128)(2,1)} %add_convert_fusion.1), channel_id=1, source_target_pairs={{0,2},{1,3},{2,0},{3,1},{4,6},{5,7},{6,4},{7,5},{8,10},{9,11},{10,... | collective-permute-start | bytes 3932168 | tf_op jit(solution)/shard_map/ppermute | solution.py:164
  651.0 56.2 %collective-permute-start.39 = (bf16[512,1280]{1,0:T(8,128)(2,1)}, bf16[512,1280]{1,0:T(8,128)(2,1)}, u32[]{:S(2)}, u32[]{:S(2)}) collective-permute-start(bf16[512,1280]{1,0:T(8,128)(2,1)} %add_convert_fusion.3), channel_id=1, source_target_pairs={{0,2},{1,3},{2,0},{3,1},{4,6},{5,7},{6,4},{7,5},{8,10},{9,11},{10,... | collective-permute-start | bytes 3932168 | tf_op jit(solution)/shard_map/ppermute | solution.py:164
  663.7 51.4 %collective-permute-start.70 = (bf16[160,1280]{1,0:T(8,128)(2,1)S(1)}, bf16[160,1280]{1,0:T(8,128)(2,1)S(1)}, u32[]{:S(2)}, u32[]{:S(2)}) collective-permute-start(bf16[160,1280]{1,0:T(8,128)(2,1)S(1)} %get-tuple-element.80), channel_id=1, source_target_pairs={{0,4},{4,0},{8,12},{12,8},{16,20},{20,16},{24,28},{28,24},{1,5},{5... | collective-permute-start | bytes 1228808 | tf_op jit(solution)/shard_map/ppermute | solution.py:164
  679.5 37.1 %collective-permute-start.68 = (bf16[160,1280]{1,0:T(8,128)(2,1)S(1)}, bf16[160,1280]{1,0:T(8,128)(2,1)S(1)}, u32[]{:S(2)}, u32[]{:S(2)}) collective-permute-start(bf16[160,1280]{1,0:T(8,128)(2,1)S(1)} %get-tuple-element.81), channel_id=1, source_target_pairs={{0,4},{4,0},{8,12},{12,8},{16,20},{20,16},{24,28},{28,24},{1,5},{5... | collective-permute-start | bytes 1228808 | tf_op jit(solution)/shard_map/ppermute | solution.py:164
  712.3 34.1 %collective-permute-start.46 = (bf16[512,1280]{1,0:T(8,128)(2,1)}, bf16[512,1280]{1,0:T(8,128)(2,1)S(1)}, u32[]{:S(2)}, u32[]{:S(2)}) collective-permute-start(bf16[512,1280]{1,0:T(8,128)(2,1)} %get-tuple-element.60), channel_id=1, source_target_pairs={{0,1},{1,0},{2,3},{3,2},{4,5},{5,4},{6,7},{7,6},{8,9},{9,8},{10,11... | collective-permute-start | bytes 3932168 | tf_op jit(solution)/shard_map/ppermute | solution.py:164
  714.6 19.5 %collective-permute-start.77 = (bf16[160,1280]{1,0:T(8,128)(2,1)S(1)}, bf16[160,1280]{1,0:T(8,128)(2,1)S(1)}, u32[]{:S(2)}, u32[]{:S(2)}) collective-permute-start(bf16[160,1280]{1,0:T(8,128)(2,1)S(1)} %get-tuple-element.73), channel_id=1, source_target_pairs={{0,4},{4,0},{8,12},{12,8},{16,20},{20,16},{24,28},{28,24},{1,5},{5... | collective-permute-start | bytes 1228808 | tf_op jit(solution)/shard_map/ppermute | solution.py:164
  715.1 27.8 %collective-permute-start.75 = (bf16[160,1280]{1,0:T(8,128)(2,1)S(1)}, bf16[160,1280]{1,0:T(8,128)(2,1)S(1)}, u32[]{:S(2)}, u32[]{:S(2)}) collective-permute-start(bf16[160,1280]{1,0:T(8,128)(2,1)S(1)} %get-tuple-element.74), channel_id=1, source_target_pairs={{0,4},{4,0},{8,12},{12,8},{16,20},{20,16},{24,28},{28,24},{1,5},{5... | collective-permute-start | bytes 1228808 | tf_op jit(solution)/shard_map/ppermute | solution.py:164
  716.7 35.3 %collective-permute-start.48 = (bf16[512,1280]{1,0:T(8,128)(2,1)}, bf16[512,1280]{1,0:T(8,128)(2,1)}, u32[]{:S(2)}, u32[]{:S(2)}) collective-permute-start(bf16[512,1280]{1,0:T(8,128)(2,1)} %get-tuple-element.60), channel_id=1, source_target_pairs={{0,2},{1,3},{2,0},{3,1},{4,6},{5,7},{6,4},{7,5},{8,10},{9,11},{10,... | collective-permute-start | bytes 3932168 | tf_op jit(solution)/shard_map/ppermute | solution.py:164
  725.4 93.1 %collective-permute-start.72 = (bf16[160,1280]{1,0:T(8,128)(2,1)}, bf16[160,1280]{1,0:T(8,128)(2,1)}, u32[]{:S(2)}, u32[]{:S(2)}) collective-permute-start(bf16[160,1280]{1,0:T(8,128)(2,1)} %get-tuple-element.79), channel_id=1, source_target_pairs={{0,4},{4,0},{8,12},{12,8},{16,20},{20,16},{24,28},{28,24},{1,5},{5... | collective-permute-start | bytes 1228808 | tf_op jit(solution)/shard_map/ppermute | solution.py:164
  734.2 86.2 %collective-permute-start.79 = (bf16[160,1280]{1,0:T(8,128)(2,1)}, bf16[160,1280]{1,0:T(8,128)(2,1)}, u32[]{:S(2)}, u32[]{:S(2)}) collective-permute-start(bf16[160,1280]{1,0:T(8,128)(2,1)} %get-tuple-element.72), channel_id=1, source_target_pairs={{0,4},{4,0},{8,12},{12,8},{16,20},{20,16},{24,28},{28,24},{1,5},{5... | collective-permute-start | bytes 1228808 | tf_op jit(solution)/shard_map/ppermute | solution.py:164
  742.9 77.7 %collective-permute-start.71 = (bf16[160,1280]{1,0:T(8,128)(2,1)}, bf16[160,1280]{1,0:T(8,128)(2,1)}, u32[]{:S(2)}, u32[]{:S(2)}) collective-permute-start(bf16[160,1280]{1,0:T(8,128)(2,1)} %get-tuple-element.76), channel_id=1, source_target_pairs={{0,24},{4,28},{8,16},{12,20},{16,8},{20,12},{24,0},{28,4},{1,25},{... | collective-permute-start | bytes 1228808 | tf_op jit(solution)/shard_map/ppermute | solution.py:164
  746.3 77.0 %collective-permute-start.69 = (bf16[160,1280]{1,0:T(8,128)(2,1)}, bf16[160,1280]{1,0:T(8,128)(2,1)}, u32[]{:S(2)}, u32[]{:S(2)}) collective-permute-start(bf16[160,1280]{1,0:T(8,128)(2,1)} %get-tuple-element.77), channel_id=1, source_target_pairs={{0,16},{4,20},{8,24},{12,28},{16,0},{20,4},{24,8},{28,12},{1,17},{... | collective-permute-start | bytes 1228808 | tf_op jit(solution)/shard_map/ppermute | solution.py:164
  752.0 23.8 %collective-permute-start.49 = (bf16[512,1280]{1,0:T(8,128)(2,1)}, bf16[512,1280]{1,0:T(8,128)(2,1)S(1)}, u32[]{:S(2)}, u32[]{:S(2)}) collective-permute-start(bf16[512,1280]{1,0:T(8,128)(2,1)} %collective-permute-done.48), channel_id=1, source_target_pairs={{0,1},{1,0},{2,3},{3,2},{4,5},{5,4},{6,7},{7,6},{8,9},{9,8},{10,11... | collective-permute-start | bytes 3932168 | tf_op jit(solution)/shard_map/ppermute | solution.py:164
  804.7 58.7 %collective-permute-start.50 = (bf16[512,1280]{1,0:T(8,128)(2,1)S(1)}, bf16[512,1280]{1,0:T(8,128)(2,1)S(1)}, u32[]{:S(2)}, u32[]{:S(2)}) collective-permute-start(bf16[512,1280]{1,0:T(8,128)(2,1)S(1)} %slice.135), channel_id=1, source_target_pairs={{0,1},{1,0},{2,3},{3,2},{4,5},{5,4},{6,7},{7,6},{8,9},{9,8},{10,11... | collective-permute-start | bytes 3932168 | tf_op jit(solution)/shard_map/ppermute | solution.py:164
  823.3 22.3 %collective-permute-start.67 = (bf16[160,1280]{1,0:T(8,128)(2,1)S(1)}, bf16[160,1280]{1,0:T(8,128)(2,1)S(1)}, u32[]{:S(2)}, u32[]{:S(2)}) collective-permute-start(bf16[160,1280]{1,0:T(8,128)(2,1)S(1)} %copy-done.56), channel_id=1, source_target_pairs={{0,8},{4,12},{8,0},{12,4},{16,24},{20,28},{24,16},{28,20},{1,9},{5... | collective-permute-start | bytes 1228808 | tf_op jit(solution)/shard_map/ppermute | solution.py:164
  824.4 21.6 %collective-permute-start.78 = (bf16[160,1280]{1,0:T(8,128)(2,1)S(1)}, bf16[160,1280]{1,0:T(8,128)(2,1)S(1)}, u32[]{:S(2)}, u32[]{:S(2)}) collective-permute-start(bf16[160,1280]{1,0:T(8,128)(2,1)S(1)} %copy-done.59), channel_id=1, source_target_pairs={{0,24},{4,28},{8,16},{12,20},{16,8},{20,12},{24,0},{28,4},{1,25},{... | collective-permute-start | bytes 1228808 | tf_op jit(solution)/shard_map/ppermute | solution.py:164
  826.8 34.6 %collective-permute-start.76 = (bf16[160,1280]{1,0:T(8,128)(2,1)S(1)}, bf16[160,1280]{1,0:T(8,128)(2,1)S(1)}, u32[]{:S(2)}, u32[]{:S(2)}) collective-permute-start(bf16[160,1280]{1,0:T(8,128)(2,1)S(1)} %copy-done.58), channel_id=1, source_target_pairs={{0,16},{4,20},{8,24},{12,28},{16,0},{20,4},{24,8},{28,12},{1,17},{... | collective-permute-start | bytes 1228808 | tf_op jit(solution)/shard_map/ppermute | solution.py:164
  828.3 34.0 %collective-permute-start.74 = (bf16[160,1280]{1,0:T(8,128)(2,1)S(1)}, bf16[160,1280]{1,0:T(8,128)(2,1)S(1)}, u32[]{:S(2)}, u32[]{:S(2)}) collective-permute-start(bf16[160,1280]{1,0:T(8,128)(2,1)S(1)} %copy-done.57), channel_id=1, source_target_pairs={{0,8},{4,12},{8,0},{12,4},{16,24},{20,28},{24,16},{28,20},{1,9},{5... | collective-permute-start | bytes 1228808 | tf_op jit(solution)/shard_map/ppermute | solution.py:164
  845.6 29.2 %collective-permute-start.52 = (bf16[160,960]{0,1:T(8,128)(2,1)S(1)}, bf16[160,960]{0,1:T(8,128)(2,1)S(1)}, u32[]{:S(2)}, u32[]{:S(2)}) collective-permute-start(bf16[160,960]{0,1:T(8,128)(2,1)S(1)} %get-tuple-element.86), channel_id=1, source_target_pairs={{0,4},{4,0},{8,12},{12,8},{16,20},{20,16},{24,28},{28,24},{1,5},{5... | collective-permute-start | bytes 921608 | tf_op jit(solution)/shard_map/ppermute | solution.py:164
  846.1 31.6 %collective-permute-start.56 = (bf16[160,960]{0,1:T(8,128)(2,1)S(1)}, bf16[160,960]{0,1:T(8,128)(2,1)S(1)}, u32[]{:S(2)}, u32[]{:S(2)}) collective-permute-start(bf16[160,960]{0,1:T(8,128)(2,1)S(1)} %get-tuple-element.88), channel_id=1, source_target_pairs={{0,4},{4,0},{8,12},{12,8},{16,20},{20,16},{24,28},{28,24},{1,5},{5... | collective-permute-start | bytes 921608 | tf_op jit(solution)/shard_map/ppermute | solution.py:164
  861.4 20.9 %collective-permute-start.54 = (bf16[160,960]{0,1:T(8,128)(2,1)S(1)}, bf16[160,960]{0,1:T(8,128)(2,1)S(1)}, u32[]{:S(2)}, u32[]{:S(2)}) collective-permute-start(bf16[160,960]{0,1:T(8,128)(2,1)S(1)} %get-tuple-element.89), channel_id=1, source_target_pairs={{0,4},{4,0},{8,12},{12,8},{16,20},{20,16},{24,28},{28,24},{1,5},{5... | collective-permute-start | bytes 921608 | tf_op jit(solution)/shard_map/ppermute | solution.py:164
  874.6 59.6 %collective-permute-start.47 = (bf16[512,1280]{1,0:T(8,128)(2,1)}, bf16[512,1280]{1,0:T(8,128)(2,1)S(1)}, u32[]{:S(2)}, u32[]{:S(2)}) collective-permute-start(bf16[512,1280]{1,0:T(8,128)(2,1)} %slice.133), channel_id=1, source_target_pairs={{0,1},{1,0},{2,3},{3,2},{4,5},{5,4},{6,7},{7,6},{8,9},{9,8},{10,11... | collective-permute-start | bytes 3932168 | tf_op jit(solution)/shard_map/ppermute | solution.py:164
  874.9 59.3 %collective-permute-start.51 = (bf16[512,1280]{1,0:T(8,128)(2,1)}, bf16[512,1280]{1,0:T(8,128)(2,1)}, u32[]{:S(2)}, u32[]{:S(2)}) collective-permute-start(bf16[512,1280]{1,0:T(8,128)(2,1)} %add_convert_fusion), channel_id=1, source_target_pairs={{0,2},{1,3},{2,0},{3,1},{4,6},{5,7},{6,4},{7,5},{8,10},{9,11},{10,... | collective-permute-start | bytes 3932168 | tf_op jit(solution)/shard_map/ppermute | solution.py:164
  887.8 42.6 %collective-permute-start.55 = (bf16[160,960]{0,1:T(8,128)(2,1)S(1)}, bf16[160,960]{0,1:T(8,128)(2,1)S(1)}, u32[]{:S(2)}, u32[]{:S(2)}) collective-permute-start(bf16[160,960]{0,1:T(8,128)(2,1)S(1)} %get-tuple-element.85), channel_id=1, source_target_pairs={{0,16},{4,20},{8,24},{12,28},{16,0},{20,4},{24,8},{28,12},{1,17},{... | collective-permute-start | bytes 921608 | tf_op jit(solution)/shard_map/ppermute | solution.py:164
  889.6 40.8 %collective-permute-start.53 = (bf16[160,960]{0,1:T(8,128)(2,1)S(1)}, bf16[160,960]{0,1:T(8,128)(2,1)S(1)}, u32[]{:S(2)}, u32[]{:S(2)}) collective-permute-start(bf16[160,960]{0,1:T(8,128)(2,1)S(1)} %get-tuple-element.83), channel_id=1, source_target_pairs={{0,8},{4,12},{8,0},{12,4},{16,24},{20,28},{24,16},{28,20},{1,9},{5... | collective-permute-start | bytes 921608 | tf_op jit(solution)/shard_map/ppermute | solution.py:164
  (125 other events, 2885.9 us)

commit v2 on v1

--- a/solution.py
+++ b/solution.py
@@ -4,6 +4,7 @@
 import jax.numpy as jnp
 from jax import lax
 from jax.experimental import pallas as pl
+from jax.experimental.layout import Layout, with_layout_constraint
 from jax.experimental.pallas import tpu as pltpu
 from jax.sharding import PartitionSpec as P
 
@@ -88,11 +89,7 @@
         out_specs=[VMEM] * 2,
         scratch_shapes=[pltpu.VMEM((heads, tokens, 2 * HD), BF16)],
         compiler_params=pltpu.CompilerParams(vmem_limit_bytes=48 * 2**20),
-        cost_estimate=pl.CostEstimate(
-            flops=16 * heads * tokens * tokens * HD,
-            bytes_accessed=10 * tokens * heads * HD,
-            transcendentals=heads * tokens * tokens,
-        ),
+        cost_estimate=pl.CostEstimate(flops=0, bytes_accessed=1, transcendentals=0),
         name="attend",
     )(qkv, bias)
 
@@ -150,11 +147,7 @@
         scratch_shapes=[pltpu.VMEM((heads, tokens, 2 * HD), BF16)] * 2
         + [pltpu.VMEM((heads, HD, tokens), F32)] * 2,
         compiler_params=pltpu.CompilerParams(vmem_limit_bytes=48 * 2**20),
-        cost_estimate=pl.CostEstimate(
-            flops=40 * heads * tokens * tokens * HD,
-            bytes_accessed=20 * tokens * heads * HD,
-            transcendentals=heads * tokens * tokens,
-        ),
+        cost_estimate=pl.CostEstimate(flops=0, bytes_accessed=1, transcendentals=0),
         name="attend_back",
     )(qkv, bias, ctx, lse, grad)
 
@@ -172,88 +165,229 @@
     return swap(value, "tensor", 2)
 
 
+def tie(*values):
+    return lax.optimization_barrier(values)
+
+
 def dp_split(size):
     fast = 2 if size < 16 else 4
     return size // fast, fast
 
 
-def gather_rows(shard):
+def high_swap(value, k):
+    return swap(value, "dp", k * dp_split(lax.axis_size("dp"))[1])
+
+
+def gather_small(shard):
+    size = lax.axis_size("dp")
+    blocks = shard[None]
+    bits = 1
+    while bits < size:
+        blocks = jnp.concatenate([blocks, swap(blocks, "dp", bits)])
+        bits *= 2
+    index = lax.axis_index("dp")
+    return jnp.stack([blocks[index ^ n] for n in range(size)])
+
+
+def spread(block):
+    _, fast = dp_split(lax.axis_size("dp"))
+    return [block] + [swap(block, "dp", j) for j in range(1, fast)]
+
+
+def entries(k, line, at=None):
+    return [(k, j, block, at if j else None) for j, block in enumerate(line)]
+
+
+def joined_entries(ks, blocks, others):
+    return [
+        entry
+        for n, (k, block) in enumerate(zip(ks, blocks, strict=True))
+        for entry in entries(k, [block, *others], n)
+    ]
+
+
+def pack_kernel(qkv_ref, out_ref, packed_ref):
+    rows, width = out_ref.shape
+    step = width * rows // qkv_ref.shape[0]
+    parts = [qkv_ref[:, n, :] for n in range(qkv_ref.shape[1])]
+    turned = [out_ref[:, n : n + step] for n in range(0, width, step)]
+    packed = jnp.concatenate([*parts, jnp.concatenate(turned, axis=0)], axis=1)
+    packed_ref[...] = packed.astype(BF16)
+
+
+def pack_first(qkv, out):
+    shape = (qkv.shape[0], qkv.shape[1] * qkv.shape[2] + out.size // qkv.shape[0])
+    if out.shape[0] % 8:
+        step = out.shape[1] * out.shape[0] // qkv.shape[0]
+        turned = jnp.concatenate([out[:, n : n + step] for n in range(0, out.shape[1], step)])
+        packed = jnp.concatenate([qkv.reshape(qkv.shape[0], -1), turned], axis=1)
+        return packed.astype(BF16)
+    return pl.pallas_call(
+        pack_kernel,
+        out_shape=jax.ShapeDtypeStruct(shape, BF16),
+        in_specs=[VMEM] * 2,
+        out_specs=VMEM,
+        compiler_params=pltpu.CompilerParams(vmem_limit_bytes=16 * 2**20),
+        cost_estimate=pl.CostEstimate(flops=0, bytes_accessed=1, transcendentals=0),
+        name="pack_first",
+    )(qkv, out)
+
+
+def assemble(blocks, cut=None):
     slow, fast = dp_split(lax.axis_size("dp"))
-    blocks = []
-    for k in range(slow):
-        block = swap(shard, "dp", k * fast) if k else shard
-        blocks.append([swap(block, "dp", j) if j else block for j in range(fast)])
-    return assemble(blocks, slow, fast)
-
-
-def assemble(blocks, slow, fast):
-    rows, columns = blocks[0][0].shape
+    rows, columns = blocks[0][2].shape[-2:]
+    kind = blocks[0][2].dtype
     index = lax.axis_index("dp")
     place = jnp.stack([index // fast, index % fast]).astype(jnp.int32)
-    flat = [b for line in blocks for b in line]
+    where = [(k, j, at) for k, j, _, at in blocks]
+    out_rows = rows * (columns - cut) // columns if cut else 0
 
     def kernel(place_ref, *refs):
-        ins, out, sems = refs[: slow * fast], refs[-2], refs[-1]
+        ins, outs = refs[: len(where)], refs[len(where) : -2]
+        whole, sems = refs[-2:] if cut else (outs[0], refs[-1])
         copies = []
-        for n, source in enumerate(ins):
-            k, j = n // fast, n % fast
+        for n, (source, (k, j, at)) in enumerate(zip(ins, where, strict=True)):
             target = (place_ref[0] ^ k) * fast + (place_ref[1] ^ j)
-            copies.append(pltpu.make_async_copy(source, out.at[target], sems.at[n]))
+            source = source if at is None else source.at[at]
+            copies.append(pltpu.make_async_copy(source, whole.at[target], sems.at[n]))
         for copy in copies:
             copy.start()
         for copy in copies:
             copy.wait()
-
-    out = pl.pallas_call(
+        if cut:
+            outs[0][...] = whole[:, :, :cut]
+            if out_rows % 8:
+                outs[1][...] = whole[:, :, cut:]
+            else:
+                turned = []
+                for n in range(slow * fast):
+                    block = whole[n, :, cut:].astype(F32)
+                    parts = [block[m : m + out_rows] for m in range(0, rows, out_rows)]
+                    turned.append(jnp.concatenate(parts, axis=1))
+                outs[1][...] = jnp.concatenate(turned, axis=0).astype(kind)
+
+    size = slow * fast
+    full = (size, rows, columns)
+    if not cut:
+        shapes = [full]
+    elif out_rows % 8:
+        shapes = [(size, rows, cut), (size, rows, columns - cut)]
+    else:
+        shapes = [(size, rows, cut), (size * out_rows, columns)]
+    outs = pl.pallas_call(
         kernel,
-        out_shape=jax.ShapeDtypeStruct((slow * fast, rows, columns), shard_type(flat[0])),
-        in_specs=[pl.BlockSpec(memory_space=pltpu.SMEM)] + [pl.BlockSpec(memory_space=pl.ANY)] * len(flat),
-        out_specs=pl.BlockSpec(memory_space=pl.ANY),
-        scratch_shapes=[pltpu.SemaphoreType.DMA((slow * fast,))],
+        out_shape=[jax.ShapeDtypeStruct(shape, kind) for shape in shapes],
+        in_specs=[pl.BlockSpec(memory_space=pltpu.SMEM)]
+        + [pl.BlockSpec(memory_space=pltpu.HBM)] * len(where),
+        out_specs=[VMEM] * len(shapes),
+        scratch_shapes=[
+            pltpu.VMEM(full if cut else (8, 16, 128), kind),
+            pltpu.SemaphoreType.DMA((len(where),)),
+        ],
+        compiler_params=pltpu.CompilerParams(vmem_limit_bytes=24 * 2**20),
+        cost_estimate=pl.CostEstimate(flops=0, bytes_accessed=1, transcendentals=0),
         name="assemble",
-    )(place, *flat)
-    return out.reshape(slow * fast * rows, columns)
-
-
-def shard_type(value):
-    return value.dtype
-
-
-def scatter_rows(total):
+    )(place, *[array for _, _, array, _ in blocks])
+    outs = list(outs)
+    if cut and out_rows % 8:
+        turned = outs[1].reshape(size, rows // out_rows, out_rows, columns - cut)
+        outs[1] = turned.transpose(0, 2, 1, 3).reshape(size * out_rows, columns)
+    return [out.reshape(-1, out.shape[-1]) for out in outs]
+
+
+def pick(total, k, j):
     slow, fast = dp_split(lax.axis_size("dp"))
     rows = total.shape[0] // (slow * fast)
     index = lax.axis_index("dp")
-    high, low = index // fast, index % fast
-
-    def part(k, j):
-        start = ((high ^ k) * fast + (low ^ j)) * rows
-        return lax.dynamic_slice_in_dim(total, start, rows, 0)
-
-    result = None
-    for k in list(range(1, slow)) + [0]:
-        line = part(k, 0).astype(F32)
-        for j in range(1, fast):
-            line = line + swap(part(k, j), "dp", j).astype(F32)
-        if k:
-            line = swap(line.astype(BF16), "dp", k * fast).astype(F32)
-        result = line if result is None else result + line
-    return result
-
-
-def gather_tokens(own):
-    near = jnp.concatenate([own, core_swap(own)])
-    side = side_swap(own)
-    far = jnp.concatenate([side, core_swap(side)])
-    return near, far
-
-
-def half_sum(partial):
-    half = partial.shape[0] // 2
-    return partial[:half].astype(F32) + core_swap(partial[half:]).astype(F32)
-
-
-def send_far(partial):
-    return side_swap(half_sum(partial).astype(BF16)).astype(F32)
+    start = (((index // fast) ^ k) * fast + ((index % fast) ^ j)) * rows
+    return lax.dynamic_slice_in_dim(total, start, rows, 0)
+
+
+def rows_first(value):
+    return with_layout_constraint(value, Layout(tuple(range(value.ndim))))
+
+
+def scatter_send(total, ks):
+    _, fast = dp_split(lax.axis_size("dp"))
+    return [
+        swap(jnp.concatenate([rows_first(pick(total, k, j)) for k in ks]), "dp", j)
+        for j in range(1, fast)
+    ]
+
+
+def scatter_lines(total, ks, received):
+    lines = {}
+    for n, k in enumerate(ks):
+        line = pick(total, k, 0).astype(F32)
+        rows = line.shape[0]
+        for part in received:
+            line = line + part[n * rows : (n + 1) * rows].astype(F32)
+        lines[k] = rows_first(line.astype(BF16))
+    return lines
+
+
+def scatter_last(lines):
+    return [high_swap(line, k) if k else line for k, line in lines.items()]
+
+
+def scatter_order():
+    slow, _ = dp_split(lax.axis_size("dp"))
+    order = list(range(2, slow, 2)) + list(range(1, slow, 2)) + [0]
+    return order[: slow // 2], order[slow // 2 :]
+
+
+def parts_sum(parts):
+    return functools.reduce(jnp.add, [part.astype(F32) for part in parts])
+
+
+def cores_sum(left, right, dims=NN):
+    return own_sum(left, right, mates_part(left, right, dims), dims)
+
+
+def mates_part(left, right, dims=NN):
+    return core_swap(dot(left[left.shape[0] // 2 :], right, dims).astype(BF16))
+
+
+def own_sum(left, right, mate, dims=NN):
+    return dot(left[: left.shape[0] // 2], right, dims) + mate.astype(F32)
+
+
+def side_send(value):
+    half = value.shape[0] // 2
+    return [side_swap(value[:half]), side_swap(value[half:])]
+
+
+def join(parts):
+    return jnp.concatenate(parts)
+
+
+def with_mate(own):
+    return jnp.concatenate([own, core_swap(own)])
+
+
+def norm_kernel(top_ref, rest_ref, rows_ref, out_ref):
+    gain, shift = rows_ref[0:1, :], rows_ref[1:2, :]
+    for n, ref in enumerate((top_ref, rest_ref)):
+        values = ref[...].astype(F32)
+        centered = values - jnp.mean(values, axis=-1, keepdims=True)
+        inverse = lax.rsqrt(jnp.mean(centered * centered, axis=-1, keepdims=True) + NORM_EPS)
+        out_ref[n] = (centered * inverse * gain + shift).astype(BF16)
+
+
+def norm_tokens(top, rest, rows, step=128):
+    half, width = top.shape
+    block = pl.BlockSpec((step, width), lambda i: (i, 0))
+    out = pl.pallas_call(
+        norm_kernel,
+        grid=(half // step,),
+        out_shape=jax.ShapeDtypeStruct((2, half, width), BF16),
+        in_specs=[block, block, pl.BlockSpec((2, width), lambda i: (0, 0))],
+        out_specs=pl.BlockSpec((2, step, width), lambda i: (0, i, 0)),
+        compiler_params=pltpu.CompilerParams(vmem_limit_bytes=24 * 2**20),
+        cost_estimate=pl.CostEstimate(flops=0, bytes_accessed=1, transcendentals=0),
+        name="norm_tokens",
+    )(top, rest, rows)
+    return out.reshape(2 * half, width)
 
 
 def sum_all(value):
@@ -294,7 +428,7 @@
 
 
 def gelu_parts(value):
-    share = 0.5 * lax.erfc(value * -(0.5**0.5))
+    share = 0.5 + 0.5 * lax.erf(value * 0.5**0.5)
     slope = share + value * jnp.exp(-0.5 * value * value) * (0.5 / jnp.pi) ** 0.5
     return (value * share).astype(BF16), slope.astype(BF16)
 
@@ -327,8 +461,6 @@
     side, core = tensor // 2, tensor % 2
 
     norm_rows = norm_params.shape[1]
-    norm_low = lax.all_gather(norm_params.astype(BF16), "dp", axis=1, tiled=True)
-    norm_values = norm_low.astype(F32)
 
     positions = jnp.arange(cell, dtype=jnp.int32)
     key_valid = (positions[None, :] < lengths[:, None]) & (
@@ -339,82 +471,198 @@
     bias = jnp.where(core == 0, bias, jnp.roll(bias, own, axis=1))
     bias_near, bias_far = bias[0][:, None], bias[1][:, None]
 
-    qkv_full = gather_rows(qkv_weight.astype(BF16).reshape(qkv_weight.shape[0], -1))
-    out_full = gather_rows(out_weight.astype(BF16))
-    up_full = gather_rows(up_weight.astype(BF16))
-    down_full = gather_rows(down_weight.astype(BF16))
-
-    stream_in = tokens.astype(F32)
-    ln_one, normed_one, inverse_one = layer_norm_parts(stream_in, norm_values[0], norm_values[1])
-    one_near, one_far = gather_tokens(ln_one.astype(BF16))
+    slow, _ = dp_split(lax.axis_size("dp"))
+    odds, evens = list(range(1, slow, 2)), list(range(2, slow, 2))
+    qkv_width = 3 * heads * HD
+    first_low = pack_first(qkv_weight, out_weight)
+    first_odd = [high_swap(first_low, k) for k in odds]
+    first_own = spread(first_low)
+    mate_tokens = core_swap(tokens)
+    norm_low, mate_tokens = tie(norm_params.astype(BF16), mate_tokens)
+    norm_low = gather_small(norm_low)
+    side_tokens = side_swap(tokens)
+    first_low, first_odd, first_own, up_low, down_low = tie(
+        first_low, first_odd, first_own, up_weight, down_weight
+    )
+    first_even = [high_swap(first_low, k) for k in evens]
+    first_odd = [spread(block) for block in first_odd]
+    up_low, down_low = up_low.astype(BF16), down_low.astype(BF16)
+    norm_values = jnp.moveaxis(norm_low, 0, 1).reshape(4, width).astype(F32)
+    one_near = norm_tokens(tokens, mate_tokens, norm_values[:2])
+    first_even, first_odd, one_near, side_tokens, up_low, down_low, cotangent = tie(
+        first_even, first_odd, one_near, side_tokens, up_low, down_low, cotangent
+    )
+    first_even = [spread(block) for block in first_even]
+    one_far = norm_tokens(side_tokens, core_swap(side_tokens), norm_values[:2])
+    lines = odds + evens
+    up_lines = [high_swap(up_low, k) for k in lines]
+    both_own = spread(jnp.stack([up_low, down_low]))[1:]
+    cot_side = side_swap(cotangent)
+    first_even, one_far = tie(first_even, one_far)
+
+    qkv_full, out_full = assemble(
+        sum(
+            [entries(k, line) for k, line in zip(odds + evens, first_odd + first_even, strict=True)],
+            entries(0, first_own),
+        ),
+        qkv_width,
+    )
     qkv_far = dot(one_far, qkv_full).astype(BF16)
     ctx_far, lse_far = attend(qkv_far, bias_far, heads)
-    out_far = send_far(dot(ctx_far, out_full).astype(BF16))
+    ctx_far, up_lines, both_own, cot_side, down_low = tie(
+        ctx_far, up_lines, both_own, cot_side, down_low
+    )
+    up_others = spread(jnp.stack(up_lines))[1:]
+    down_odd = [high_swap(down_low, k) for k in odds]
+    far_sum = cores_sum(ctx_far, out_full).astype(BF16)
+    far_sum, one_near, qkv_full = tie(far_sum, one_near, qkv_full)
+    out_far = side_swap(far_sum)
     qkv_near = dot(one_near, qkv_full).astype(BF16)
     ctx_near, lse_near = attend(qkv_near, bias_near, heads)
-    out_near = half_sum(dot(ctx_near, out_full).astype(BF16))
-    residual = stream_in + (out_near + out_far)
+    ctx_near, out_far, up_others, down_odd, down_low, cotangent, cot_side = tie(
+        ctx_near, out_far, up_others, down_odd, down_low, cotangent, cot_side
+    )
+    down_even = [high_swap(down_low, k) for k in evens]
+    odd_others = spread(jnp.stack(down_odd))[1:]
+    grad_near = with_mate(cotangent)
+    grad_far = with_mate(cot_side)
+    out_near = cores_sum(ctx_near, out_full)
+    stream_in = tokens.astype(F32)
+    residual = stream_in + (out_near + out_far.astype(F32))
 
     ln_two, normed_two, inverse_two = layer_norm_parts(residual, norm_values[2], norm_values[3])
-    two_near, two_far = gather_tokens(ln_two.astype(BF16))
-    grad_near, grad_far = gather_tokens(cotangent)
+    ln_two = ln_two.astype(BF16)
+    two_near = with_mate(ln_two)
+    two_side = side_swap(ln_two)
+    two_near, up_lines, up_others, both_own, down_low = tie(
+        two_near, up_lines, up_others, both_own, down_low
+    )
+    (up_full,) = assemble(
+        [(0, 0, up_low, None)]
+        + [(0, j + 1, block, 0) for j, block in enumerate(both_own)]
+        + joined_entries(lines, up_lines, up_others)
+    )
     hid_near, slope_near = gelu_parts(dot(two_near, up_full))
+    hid_near, down_even, odd_others, grad_near, grad_far = tie(
+        hid_near, down_even, odd_others, grad_near, grad_far
+    )
+    even_others = [spread(block) for block in down_even]
+    hid_near, even_others = tie(hid_near, even_others)
+    (down_full,) = assemble(
+        sum(
+            [entries(k, line) for k, line in zip(evens, even_others, strict=True)],
+            [(0, 0, down_low, None)] + [(0, j + 1, block, 1) for j, block in enumerate(both_own)],
+        )
+        + joined_entries(odds, down_odd, odd_others)
+    )
+    pre_near = (dot(grad_near, down_full, NT) * slope_near.astype(F32)).astype(BF16)
+    pre_near, hid_near, two_side = tie(pre_near, hid_near, two_side)
+    two_far = with_mate(two_side)
     hid_far, slope_far = gelu_parts(dot(two_far, up_full))
     pre_far = (dot(grad_far, down_full, NT) * slope_far.astype(F32)).astype(BF16)
-    back_far = send_far(dot(pre_far, up_full, NT).astype(BF16))
-    pre_near = (dot(grad_near, down_full, NT) * slope_near.astype(F32)).astype(BF16)
-    back_near = half_sum(dot(pre_near, up_full, NT).astype(BF16))
-    grad_ln_two = back_near + back_far
-
-    hid = jnp.concatenate([hid_near, hid_far])
-    grad_group = jnp.concatenate([grad_near, grad_far])
-    two_group = jnp.concatenate([two_near, two_far])
-    pre = jnp.concatenate([pre_near, pre_far])
-    grad_down = dot(hid, grad_group, TN).astype(BF16)
-    summed_down = scatter_rows(grad_down)
-    grad_up = dot(two_group, pre, TN).astype(BF16)
-    summed_up = scatter_rows(grad_up)
-
-    last_far = send_far(dot(hid_far, down_full).astype(BF16))
-    last_near = half_sum(dot(hid_near, down_full).astype(BF16))
-    layer_out = (residual + (last_near + last_far)).astype(BF16)
-
+    far_sum = cores_sum(pre_far, up_full, NT).astype(BF16)
+    far_sum, pre_near, pre_far, hid_near, hid_far = tie(
+        far_sum, pre_near, pre_far, hid_near, hid_far
+    )
+    back_far = side_swap(far_sum)
+    back_near = cores_sum(pre_near, up_full, NT)
+    back_near, hid_near, hid_far, grad_near, grad_far = tie(
+        back_near, hid_near, hid_far, grad_near, grad_far
+    )
+    heavy, light = scatter_order()
+    order = heavy + light
+    grad_down = dot(join([hid_near, hid_far]), join([grad_near, grad_far]), TN).astype(BF16)
+    half = own
+    last_terms = [dot(v[half:], down_full).astype(BF16) for v in (hid_far, hid_near)]
+    last_terms, grad_down, back_far, pre_near, pre_far = tie(
+        last_terms, grad_down, back_far, pre_near, pre_far
+    )
+    down_received = scatter_send(grad_down, order)
+    grad_ln_two = back_near + back_far.astype(F32)
     grad_residual = cotangent.astype(F32) + layer_norm_back(
         grad_ln_two, normed_two, inverse_two, norm_values[2]
     )
     gain_two = jnp.sum(grad_ln_two * normed_two, axis=0)
     shift_two = jnp.sum(grad_ln_two, axis=0)
 
-    res_near, res_far = gather_tokens(grad_residual.astype(BF16))
+    res_low = grad_residual.astype(BF16)
+    res_side = side_swap(res_low)
+    res_near = with_mate(res_low)
+    last_mates = [core_swap(v) for v in last_terms]
+    res_near, last_mates, pre_near, pre_far = tie(res_near, last_mates, pre_near, pre_far)
+    grad_up = dot(join([two_near, two_far]), join([pre_near, pre_far]), TN).astype(BF16)
+    grad_up, res_near, grad_down, down_received = tie(grad_up, res_near, grad_down, down_received)
+    up_received = scatter_send(grad_up, order)
+    down_lines = scatter_lines(grad_down, order, down_received)
+    down_parts = {k: high_swap(down_lines[k], k) for k in heavy}
     dctx_near = dot(res_near, out_full, NT).astype(BF16)
     dqkv_near = attend_back(qkv_near, bias_near, ctx_near, lse_near, dctx_near, heads)
+    dqkv_near, res_side, up_received, grad_up, down_parts, down_lines, last_mates, hid_far = tie(
+        dqkv_near, res_side, up_received, grad_up, down_parts, down_lines, last_mates, hid_far
+    )
+    for k in light:
+        down_parts[k] = high_swap(down_lines[k], k) if k else down_lines[k]
+    last_far = own_sum(hid_far, down_full, last_mates[0]).astype(BF16)
+    last_side = side_swap(last_far)
+    up_lines = scatter_lines(grad_up, order, up_received)
+    up_parts = {k: high_swap(up_lines[k], k) for k in heavy}
+    res_far = with_mate(res_side)
+    grad_out = dot(join([ctx_near, ctx_far]), join([res_near, res_far]), TN).astype(BF16)
     dctx_far = dot(res_far, out_full, NT).astype(BF16)
+    dctx_far, grad_out = tie(dctx_far, grad_out)
     dqkv_far = attend_back(qkv_far, bias_far, ctx_far, lse_far, dctx_far, heads)
-    first_far = send_far(dot(dqkv_far, qkv_full, NT).astype(BF16))
-    first_near = half_sum(dot(dqkv_near, qkv_full, NT).astype(BF16))
-    one_group = jnp.concatenate([one_near, one_far])
-    dqkv = jnp.concatenate([dqkv_near, dqkv_far])
-    grad_qkv = dot(one_group, dqkv, TN).astype(BF16)
-    summed_qkv = scatter_rows(grad_qkv)
-    res_group = jnp.concatenate([res_near, res_far])
-    ctx = jnp.concatenate([ctx_near, ctx_far])
-    grad_out = dot(ctx, res_group, TN).astype(BF16)
-    summed_out = scatter_rows(grad_out)
-
-    grad_ln_one = first_near + first_far
+    dqkv_far, up_parts, up_lines, down_parts, last_side, grad_out = tie(
+        dqkv_far, up_parts, up_lines, down_parts, last_side, grad_out
+    )
+
+    for k in light:
+        up_parts[k] = high_swap(up_lines[k], k) if k else up_lines[k]
+    out_received = scatter_send(grad_out, order)
+    grad_qkv = dot(join([one_near, one_far]), join([dqkv_near, dqkv_far]), TN).astype(BF16)
+    grad_qkv, dqkv_far, dqkv_near = tie(rows_first(grad_qkv), dqkv_far, dqkv_near)
+    received = {k: scatter_send(grad_qkv, [k]) for k in order}
+    mate = mates_part(dqkv_far, qkv_full, NT)
+    first_lines = {}
+    for k in evens:
+        first_lines.update(scatter_lines(grad_qkv, [k], received[k]))
+    first_lines, mate, grad_qkv, dqkv_far, out_received, grad_out = tie(
+        first_lines, mate, grad_qkv, dqkv_far, out_received, grad_out
+    )
+    qkv_parts = scatter_last(first_lines)
+    out_parts = scatter_last(scatter_lines(grad_out, order, out_received))
+    far_sum = own_sum(dqkv_far, qkv_full, mate, NT).astype(BF16)
+    far_sum, dqkv_near = tie(far_sum, dqkv_near)
+    first_far = side_swap(far_sum)
+    first_near = cores_sum(dqkv_near, qkv_full, NT)
+    odd_lines = {}
+    for k in odds:
+        odd_lines.update(scatter_lines(grad_qkv, [k], received[k]))
+    odd_lines, grad_qkv, first_near = tie(odd_lines, grad_qkv, first_near)
+    qkv_parts = qkv_parts + scatter_last(odd_lines)
+    qkv_parts = qkv_parts + scatter_last(scatter_lines(grad_qkv, [0], received[0]))
+
+    last_near = own_sum(hid_near, down_full, last_mates[1])
+    layer_out = (residual + (last_near + last_side.astype(F32))).astype(BF16)
+    summed_up, summed_down = parts_sum(up_parts.values()), parts_sum(down_parts.values())
+    summed_out = parts_sum(out_parts)
+    early_squares = (
+        jnp.sum(summed_up * summed_up)
+        + jnp.sum(summed_down * summed_down)
+        + jnp.sum(summed_out * summed_out)
+    )
+    _, normed_one, inverse_one = layer_norm_parts(stream_in, norm_values[0], norm_values[1])
+    layer_out, first_far, early_squares = tie(layer_out, first_far, early_squares)
+    grad_ln_one = first_near + first_far.astype(F32)
     input_grad = (
         grad_residual + layer_norm_back(grad_ln_one, normed_one, inverse_one, norm_values[0])
     ).astype(BF16)
     gain_one = jnp.sum(grad_ln_one * normed_one, axis=0)
     shift_one = jnp.sum(grad_ln_one, axis=0)
-
-    local_squares = (
-        jnp.sum(summed_qkv * summed_qkv)
-        + jnp.sum(summed_out * summed_out)
-        + jnp.sum(summed_up * summed_up)
-        + jnp.sum(summed_down * summed_down)
-    )
     rows = jnp.stack([gain_one, shift_one, gain_two, shift_two])
+    qkv_parts, rows, input_grad, early_squares = tie(qkv_parts, rows, input_grad, early_squares)
+    summed_qkv = parts_sum(qkv_parts)
+
+    local_squares = early_squares + jnp.sum(summed_qkv * summed_qkv)
     packed = jnp.concatenate([rows, jnp.full((4, 128), local_squares, F32)], axis=1)
     packed = sum_all(packed)
     norm_grad = packed[:, :width]

time: 984 us -> 514 us (0.52)
  Pallas kernels: 366 us -> 71.2 us
  waiting for transfers between devices: 270 us -> 159 us
  blocking collectives: 27.8 us -> 0 us
  starting transfers between devices: 92.2 us -> 72 us
  matrix products: 133 us -> 114 us
    pallas_call x4 -> x6, Pallas kernels: 310 us -> 14.7 us  [the longest x3 8.67 us: assemble(): pl.pallas_call(kernel, out_shape=[jax.ShapeDtypeStruct(shape, kind) for s...]
    ppermute x85 -> x68, waiting for transfers between devices: 270 us -> 159 us  [swap(): return lax.ppermute(value, axis, [(i, i ^ bits) for i in range(size)])]
    all_gather x1 -> x0, blocking collectives: 27.8 us -> none  [on_device(): lax.all_gather(norm_params.astype(BF16), 'dp', axis=1, tiled=True)]
    ppermute x85 -> x68, starting transfers between devices: 92.2 us -> 72 us  [swap(): return lax.ppermute(value, axis, [(i, i ^ bits) for i in range(size)])]
    dot_general x20 -> x28, matrix products: 133 us -> 114 us  [dot(): return lax.dot_general(left, right, dims, preferred_element_type=F32)]
    convert_element_type x16 -> x13, other arithmetic: 17.8 us -> 20.5 us  [the longest x6 11.5 us: scatter_lines(): lines[k] = rows_first(line.astype(BF16))]
  transfers between devices with their start and end apart: 85 -> 68, of which waited for: 28 -> 30; matrix products, arithmetic and copies ran while one was open for 18% -> 26% of each run, Pallas kernels for 38% -> 14%
where the time goes in v2:
time: 514 us; the launch traced here: 505 us
  waiting for transfers between devices  159 us (31%)
  matrix products  114 us (22%)
  starting transfers between devices  72 us (14%)
  Pallas kernels  71.2 us (14%)
  other arithmetic  58.3 us (11%)
  local copies, waits for them, and re-layouts  23.2 us (5%)
  between operations  7.84 us (2%)
    ppermute x68, waiting for transfers between devices, swap(): return lax.ppermute(value, axis, [(i, i ^ bits) for i in range(size)])  159 us
    dot_general x28, matrix products, dot(): return lax.dot_general(left, right, dims, preferred_element_type=F32)  114 us
    ppermute x68, starting transfers between devices, swap(): return lax.ppermute(value, axis, [(i, i ^ bits) for i in range(size)])  72 us
    pallas_call x2, Pallas kernels, attend_back(): pl.pallas_call(functools.partial(attend_back_kernel, heads, step), out_sh...  38.4 us
    pallas_call x2, Pallas kernels, attend(): pl.pallas_call(functools.partial(attend_kernel, heads, step), out_shape=(...  18.2 us
    unnamed x222, local copies, waits for them, and re-layouts  15.4 us
    convert_element_type x6, other arithmetic, scatter_lines(): lines[k] = rows_first(line.astype(BF16))  11.5 us
  transfers between devices with their start and end apart: 68, of which 30 were waited for; matrix products, arithmetic and copies ran while one was open for 26% of the time, Pallas kernels for 14%

profile of v2, /device:TPU:0, one launch (start us, length us, event | category | flops | bytes accessed | tf_op | source)
XLA Modules:
  0.0 505.2 jit_solution(621609223050865632)
XLA Ops:
  4.0 2.7 collective-permute-start
  6.7 2.5 collective-permute-start.1
  12.3 8.2 %collective-permute-done.7 = bf16[1,4,160]{2,1,0:T(4,128)(2,1)S(1)} collective-permute-done((bf16[1,4,160]{2,1,0:T(4,128)(2,1)S(1)}, bf16[1,4,160]{2,1,0:T(4,128)(2,1)S(1)}, u32[]{:S(2)}, u32[]{:S(2)}) %collective-permute-start.7) | collective-permute-done | bytes 1312 | tf_op jit(solution)/shard_map/ppermute | solution.py:157
  25.0 3.6 collective-permute-start.9
  40.3 9.7 %collective-permute-done.3.refs_6_ = bf16[160,1280]{1,0:T(8,128)(2,1)} collective-permute-done((bf16[160,1280]{1,0:T(8,128)(2,1)S(1)}, bf16[160,1280]{1,0:T(8,128)(2,1)}, u32[]{:S(2)}, u32[]{:S(2)}) %collective-permute-start.3) | collective-permute-done | bytes 409632 | tf_op jit(solution)/shard_map/ppermute | solution.py:157
  58.8 3.7 norm_tokens.3
  62.5 2.8 collective-permute-done.11.refs_7_
  68.2 4.5 assemble.3
  72.7 4.8 convolution_convert_fusion.11.qkv_ref
  77.6 9.0 %attend.2 = (bf16[1024,320]{1,0:T(8,128)(2,1)S(1)}, f32[1024,128]{1,0:T(8,128)S(1)}) custom-call(bf16[1024,960]{1,0:T(8,128)(2,1)S(1)} %convolution_convert_fusion.11.qkv_ref, f32[1024,1]{1,0:T(8,128)S(1)} %copy.66.bias_ref), custom_call_target="tpu_custom_call" | custom-call | bytes 1 | tf_op jit(solution)/shard_map/attend/pallas_call | solution.py:82
  86.6 8.1 %collective-permute-done.15.refs_6_ = bf16[160,1280]{1,0:T(8,128)(2,1)S(1)} collective-permute-done((bf16[160,1280]{1,0:T(8,128)(2,1)S(1)}, bf16[160,1280]{1,0:T(8,128)(2,1)S(1)}, u32[]{:S(2)}, u32[]{:S(2)}) %collective-permute-start.15) | collective-permute-done | bytes 409632 | tf_op jit(solution)/shard_map/ppermute | solution.py:157
  95.7 3.0 collective-permute-done.18
  107.2 5.4 %convolution_convert_fusion.10.qkv_ref = bf16[1024,960]{1,0:T(8,128)(2,1)S(1)} fusion(bf16[1024,1280]{1,0:T(8,128)(2,1)} %bitcast.67, bf16[1280,960]{1,0:T(8,128)(2,1)} %bitcast.6), kind=kOutput, calls=%fused_computation.106 | convolution fusion | flops 2517565440 | bytes 7045120 | tf_op jit(solution)/shard_map/dot_general | solution.py:35
  112.7 9.2 %attend.3 = (bf16[1024,320]{1,0:T(8,128)(2,1)S(1)}, f32[1024,128]{1,0:T(8,128)S(1)}) custom-call(bf16[1024,960]{1,0:T(8,128)(2,1)S(1)} %convolution_convert_fusion.10.qkv_ref, f32[1024,1]{1,0:T(8,128)S(1)} %copy-done.5), custom_call_target="tpu_custom_call" | custom-call | bytes 1 | tf_op jit(solution)/shard_map/attend/pallas_call | solution.py:82
  121.9 3.6 collective-permute-done.22.refs_6_
  125.5 5.8 %collective-permute-done.20.refs_3_.refs_5_.refs_7_ = bf16[3,160,1280]{2,1,0:T(8,128)(2,1)S(1)} collective-permute-done((bf16[3,160,1280]{2,1,0:T(8,128)(2,1)}, bf16[3,160,1280]{2,1,0:T(8,128)(2,1)S(1)}, u32[]{:S(2)}, u32[]{:S(2)}) %collective-permute-start.20) | collective-permute-done | bytes 1228832 | tf_op jit(solution)/shard_map/ppermute | solution.py:157
  134.5 2.5 collective-permute-done.23
  137.1 2.9 fusion.123
  149.0 5.5 %multiply_convert_fusion.3 = (bf16[1024,1280]{1,0:T(8,128)(2,1)S(1)}, f32[1024,1280]{1,0:T(8,128)}) fusion(bf16[1024,1280]{1,0:T(8,128)(2,1)S(1)} %pad_maximum_fusion, bf16[1280,1280]{1,0:T(8,128)(2,1)S(1)} %bitcast.55), kind=kOutput, calls=%fused_computation.42 | convolution fusion | flops 3361996800 | bytes 13762560 | tf_op jit(solution)/shard_map/dot_general | solution.py:35
  154.4 8.1 %collective-permute-done.25.refs_2_ = bf16[160,1280]{1,0:T(8,128)(2,1)S(1)} collective-permute-done((bf16[160,1280]{1,0:T(8,128)(2,1)S(1)}, bf16[160,1280]{1,0:T(8,128)(2,1)S(1)}, u32[]{:S(2)}, u32[]{:S(2)}) %collective-permute-start.25) | collective-permute-done | bytes 409632 | tf_op jit(solution)/shard_map/ppermute | solution.py:157
  165.2 8.8 %collective-permute-done.29.refs_3_ = bf16[160,1280]{1,0:T(8,128)(2,1)S(1)} collective-permute-done((bf16[160,1280]{1,0:T(8,128)(2,1)S(1)}, bf16[160,1280]{1,0:T(8,128)(2,1)S(1)}, u32[]{:S(2)}, u32[]{:S(2)}) %collective-permute-start.29) | collective-permute-done | bytes 409632 | tf_op jit(solution)/shard_map/ppermute | solution.py:157
  176.1 7.2 %multiply_convert_fusion.2 = bf16[1024,1280]{1,0:T(8,128)(2,1)S(1)} fusion(bf16[1024,1280]{1,0:T(8,128)(2,1)S(1)} %pad_maximum_fusion.1, bf16[1280,1280]{1,0:T(8,128)(2,1)S(1)} %bitcast.61, f32[1024,1280]{1,0:T(8,128)} %get-tuple-element.382), kind=kOutput, calls=%fused_computation.41 | convolution fusion | flops 3371171840 | bytes 13762560 | tf_op jit(solution)/shard_map/dot_general | solution.py:35
  183.2 11.3 %collective-permute-done.30 = bf16[512,1280]{1,0:T(8,128)(2,1)S(1)} collective-permute-done((bf16[512,1280]{1,0:T(8,128)(2,1)S(1)}, bf16[512,1280]{1,0:T(8,128)(2,1)S(1)}, u32[]{:S(2)}, u32[]{:S(2)}) %collective-permute-start.30) | collective-permute-done | bytes 1310752 | tf_op jit(solution)/shard_map/ppermute | solution.py:157
  194.5 3.0 collective-permute-done.31
  197.5 6.1 %multiply_convert_fusion = (bf16[1024,1280]{1,0:T(8,128)(2,1)S(1)}, f32[1024,1280]{1,0:T(8,128)}) fusion(bf16[1280,1280]{1,0:T(8,128)(2,1)S(1)} %bitcast.56, bf16[512,1280]{1,0:T(8,128)(2,1)S(1)} %collective-permute-done.31, bf16[512,1280]{1,0:T(8,128)(2,1)S(1)} %collective-permute-done.30), kind=kOutput, calls=%fused_computation.38 | convolution fusion | flops 3367239680 | bytes 13762560 | tf_op jit(solution)/shard_map/dot_general | solution.py:35
  203.7 7.1 %multiply_convert_fusion.1 = bf16[1024,1280]{1,0:T(8,128)(2,1)S(1)} fusion(bf16[1024,1280]{1,0:T(8,128)(2,1)S(1)} %pad_maximum_fusion.2, bf16[1280,1280]{1,0:T(8,128)(2,1)S(1)} %bitcast.62, f32[1024,1280]{1,0:T(8,128)} %get-tuple-element.384), kind=kOutput, calls=%fused_computation.39 | convolution fusion | flops 3371171840 | bytes 13762560 | tf_op jit(solution)/shard_map/dot_general | solution.py:35
  212.9 2.9 collective-permute-done.32
  224.6 2.9 convolution_convert_fusion.5
  227.5 2.9 convolution_convert_fusion.4
  230.5 8.6 %convolution_convert_fusion.1 = bf16[1280,1280]{1,0:T(8,128)(2,1)} fusion(bf16[1024,1280]{1,0:T(8,128)(2,1)S(1)} %get-tuple-element.255, bf16[1024,1280]{1,0:T(8,128)(2,1)S(1)} %get-tuple-element.222, bf16[1024,1280]{1,0:T(8,128)(2,1)S(1)} %pad_maximum_fusion.2, bf16[1024,1280]{1,0:T(8,128)(2,1)S(1)} %pad_maximum_fusion.1), kind=kOutput, calls=%fused_computation.3 | convolution fusion | flops 6733496320 | bytes 13762560 | tf_op jit(solution)/shard_map/dot_general | solution.py:35
  239.0 11.8 %collective-permute-done.34 = bf16[512,1280]{1,0:T(8,128)(2,1)S(1)} collective-permute-done((bf16[512,1280]{1,0:T(8,128)(2,1)S(1)}, bf16[512,1280]{1,0:T(8,128)(2,1)S(1)}, u32[]{:S(2)}, u32[]{:S(2)}) %collective-permute-start.34) | collective-permute-done | bytes 1310752 | tf_op jit(solution)/shard_map/ppermute | solution.py:157
  252.1 3.0 fusion.120
  258.5 3.8 pad_maximum_fusion.3
  262.4 7.2 %convolution_convert_fusion = bf16[1280,1280]{1,0:T(8,128)(2,1)S(1)} fusion(bf16[512,1280]{1,0:T(8,128)(2,1)S(1)} %copy-done.98, bf16[512,1280]{1,0:T(8,128)(2,1)S(1)} %copy-done.96, bf16[1024,1280]{1,0:T(8,128)(2,1)S(1)} %copy-done.64, bf16[1024,1280]{1,0:T(8,128)(2,1)S(1)} %copy-done.106, bf16[1024,1280]{1,0:T(8,128)(2,1)S(1)} %copy-done.104), kind=kOutput, calls=%fused_computation.2 | convolution fusion | flops 6738739200 | bytes 13762560 | tf_op jit(solution)/shard_map/dot_general | solution.py:35
  269.7 26.1 %collective-permute-done.38 = bf16[640,1280]{1,0:T(8,128)(2,1)S(1)} collective-permute-done((bf16[640,1280]{1,0:T(8,128)(2,1)S(1)}, bf16[640,1280]{1,0:T(8,128)(2,1)S(1)}, u32[]{:S(2)}, u32[]{:S(2)}) %collective-permute-start.38) | collective-permute-done | bytes 1638432 | tf_op jit(solution)/shard_map/ppermute | solution.py:157
  299.8 3.3 add_convert_fusion.7
  305.4 3.7 convolution_convert_fusion.12
  313.5 19.2 %attend_back.2 = bf16[1024,960]{1,0:T(8,128)(2,1)S(1)} custom-call(bf16[1024,960]{1,0:T(8,128)(2,1)} %copy-done.2, f32[1024,1]{1,0:T(8,128)S(1)} %copy-done.6, bf16[1024,320]{1,0:T(8,128)(2,1)S(1)} %copy-done.14, f32[1024,128]{1,0:T(8,128)S(1)} %copy-done.41, bf16[1024,320]{1,0:T(8,128)(2,1)S(1)} %copy-done.17), custom_call_target="tpu_custom_call" | custom-call | bytes 1 | tf_op jit(solution)/shard_map/attend_back/pallas_call | solution.py:142
  332.8 2.4 collective-permute-done.40
  335.2 3.4 fusion.83
  338.6 4.4 fusion.50
  344.1 2.6 add_convert_fusion.3
  351.1 4.1 fusion.51
  355.2 2.9 fusion.72.grad_ref
  358.2 19.2 %attend_back.3 = bf16[1024,960]{1,0:T(8,128)(2,1)S(1)} custom-call(bf16[1024,960]{1,0:T(8,128)(2,1)} %copy-done.1, f32[1024,1]{1,0:T(8,128)S(1)} %copy-done.4, bf16[1024,320]{1,0:T(8,128)(2,1)S(1)} %copy-done.16, f32[1024,128]{1,0:T(8,128)S(1)} %copy-done.39, bf16[1024,320]{1,0:T(8,128)(2,1)S(1)} %fusion.72.grad_ref), custom_call_target="tpu_custom_call" | custom-call | bytes 1 | tf_op jit(solution)/shard_map/attend_back/pallas_call | solution.py:142
  378.9 6.1 %fusion.37 = bf16[1280,960]{1,0:T(8,128)(2,1)S(1)} fusion(bf16[1024,960]{1,0:T(8,128)(2,1)S(1)} %attend_back.3, bf16[1024,960]{1,0:T(8,128)(2,1)S(1)} %attend_back.2, bf16[1024,1280]{1,0:T(8,128)(2,1)S(1)} %bitcast.70, bf16[1024,1280]{1,0:T(8,128)(2,1)S(1)} %bitcast.68), kind=kOutput, calls=%fused_computation.50 | convolution fusion | flops 5052743680 | bytes 11632640 | tf_op jit(solution)/shard_map/dot_general | solution.py:35
  386.6 3.7 convolution_convert_fusion.3
  394.1 3.0 add_convert_fusion
  399.2 4.5 collective-permute-done.50
  403.7 4.6 fusion.48
  409.5 4.4 convolution_convert_fusion.2
  421.8 9.1 %collective-permute-start.54 = (bf16[40,1280]{1,0:T(8,128)(2,1)S(1)}, bf16[40,1280]{1,0:T(8,128)(2,1)S(1)}, u32[]{:S(2)}, u32[]{:S(2)}) collective-permute-start(bf16[40,1280]{1,0:T(8,128)(2,1)S(1)} %get-tuple-element.368), channel_id=1, source_target_pairs={{0,8},{4,12},{8,0},{12,4},{16,24},{20,28},{24,16},{28,20},{1,9},{5... | collective-permute-start | bytes 307208 | tf_op jit(solution)/shard_map/ppermute | solution.py:157
  431.8 2.3 add_convert_fusion.12
  434.2 3.3 collective-permute-start.56
  437.5 9.3 %collective-permute-done.53 = bf16[40,1280]{1,0:T(8,128)(2,1)S(1)} collective-permute-done((bf16[40,1280]{1,0:T(8,128)(2,1)S(1)}, bf16[40,1280]{1,0:T(8,128)(2,1)S(1)}, u32[]{:S(2)}, u32[]{:S(2)}) %collective-permute-start.53) | collective-permute-done | bytes 102432 | tf_op jit(solution)/shard_map/ppermute | solution.py:157
  449.8 3.7 convert_add_fusion.2
  455.6 2.7 fusion.55
  458.3 3.5 fusion.59
  463.1 4.4 collective-permute-done.60
  472.2 3.0 collective-permute-done.64
  475.7 3.6 collective-permute-done.65
  480.0 3.2 collective-permute-done.66
  484.1 4.2 collective-permute-done.67
  492.5 4.0 multiply_subtract_fusion
  (419 shorter events, 131.2 us)
Async XLA Ops:
  0.7 10.1 %collective-permute-start.6 = (bf16[512,1280]{1,0:T(8,128)(2,1)}, bf16[512,1280]{1,0:T(8,128)(2,1)S(1)}, u32[]{:S(2)}, u32[]{:S(2)}) collective-permute-start(bf16[512,1280]{1,0:T(8,128)(2,1)} %top_ref.1), channel_id=1, source_target_pairs={{0,1},{1,0},{2,3},{3,2},{4,5},{5,4},{6,7},{7,6},{8,9},{9,8},{10,11... | collective-permute-start | bytes 3932168 | tf_op jit(solution)/shard_map/ppermute | solution.py:157
  4.0 24.6 %collective-permute-start = (bf16[160,1280]{1,0:T(8,128)(2,1)S(1)}, bf16[160,1280]{1,0:T(8,128)(2,1)S(1)}, u32[]{:S(2)}, u32[]{:S(2)}) collective-permute-start(bf16[160,1280]{1,0:T(8,128)(2,1)S(1)} %pack_first.1.refs_0_), channel_id=1, source_target_pairs={{0,8},{4,12},{8,0},{12,4},{16,24},{20,28},{24,16},{28,20},{1,9},{5... | collective-permute-start | bytes 1228808 | tf_op jit(solution)/shard_map/ppermute | solution.py:157
  6.7 21.9 %collective-permute-start.1 = (bf16[160,1280]{1,0:T(8,128)(2,1)S(1)}, bf16[160,1280]{1,0:T(8,128)(2,1)}, u32[]{:S(2)}, u32[]{:S(2)}) collective-permute-start(bf16[160,1280]{1,0:T(8,128)(2,1)S(1)} %pack_first.1.refs_0_), channel_id=1, source_target_pairs={{0,24},{4,28},{8,16},{12,20},{16,8},{20,12},{24,0},{28,4},{1,25},{... | collective-permute-start | bytes 1228808 | tf_op jit(solution)/shard_map/ppermute | solution.py:157
  9.2 19.4 %collective-permute-start.2 = (bf16[160,1280]{1,0:T(8,128)(2,1)S(1)}, bf16[160,1280]{1,0:T(8,128)(2,1)S(1)}, u32[]{:S(2)}, u32[]{:S(2)}) collective-permute-start(bf16[160,1280]{1,0:T(8,128)(2,1)S(1)} %pack_first.1.refs_0_), channel_id=1, source_target_pairs={{0,4},{4,0},{8,12},{12,8},{16,20},{20,16},{24,28},{28,24},{1,5},{5... | collective-permute-start | bytes 1228808 | tf_op jit(solution)/shard_map/ppermute | solution.py:157
  11.8 8.7 %collective-permute-start.7 = (bf16[1,4,160]{2,1,0:T(4,128)(2,1)S(1)}, bf16[1,4,160]{2,1,0:T(4,128)(2,1)S(1)}, u32[]{:S(2)}, u32[]{:S(2)}) collective-permute-start(bf16[1,4,160]{2,1,0:T(4,128)(2,1)S(1)} %bitcast.76), channel_id=1, source_target_pairs={{0,4},{4,0},{8,12},{12,8},{16,20},{20,16},{24,28},{28,24},{1,5},{5... | collective-permute-start | bytes 3848 | tf_op jit(solution)/shard_map/ppermute | solution.py:157
  20.5 4.5 collective-permute-start.8
  21.2 29.6 %collective-permute-start.10 = (bf16[512,1280]{1,0:T(8,128)(2,1)S(1)}, bf16[512,1280]{1,0:T(8,128)(2,1)}, u32[]{:S(2)}, u32[]{:S(2)}) collective-permute-start(bf16[512,1280]{1,0:T(8,128)(2,1)S(1)} %copy-done), channel_id=1, source_target_pairs={{0,2},{1,3},{2,0},{3,1},{4,6},{5,7},{6,4},{7,5},{8,10},{9,11},{10,... | collective-permute-start | bytes 3932168 | tf_op jit(solution)/shard_map/ppermute | solution.py:157
  25.0 10.1 %collective-permute-start.9 = (bf16[4,4,160]{2,1,0:T(4,128)(2,1)S(1)}, bf16[4,4,160]{2,1,0:T(4,128)(2,1)S(1)}, u32[]{:S(2)}, u32[]{:S(2)}) collective-permute-start(bf16[4,4,160]{2,1,0:T(4,128)(2,1)S(1)} %pad_maximum_fusion.12), channel_id=1, source_target_pairs={{0,16},{4,20},{8,24},{12,28},{16,0},{20,4},{24,8},{28,12},{1,17},{... | collective-permute-start | bytes 15368 | tf_op jit(solution)/shard_map/ppermute | solution.py:157
  29.4 20.6 %collective-permute-start.3 = (bf16[160,1280]{1,0:T(8,128)(2,1)S(1)}, bf16[160,1280]{1,0:T(8,128)(2,1)}, u32[]{:S(2)}, u32[]{:S(2)}) collective-permute-start(bf16[160,1280]{1,0:T(8,128)(2,1)S(1)} %pack_first.1.refs_0_), channel_id=1, source_target_pairs={{0,16},{4,20},{8,24},{12,28},{16,0},{20,4},{24,8},{28,12},{1,17},{... | collective-permute-start | bytes 1228808 | tf_op jit(solution)/shard_map/ppermute | solution.py:157
  30.5 19.5 %collective-permute-start.4 = (bf16[160,1280]{1,0:T(8,128)(2,1)S(1)}, bf16[160,1280]{1,0:T(8,128)(2,1)}, u32[]{:S(2)}, u32[]{:S(2)}) collective-permute-start(bf16[160,1280]{1,0:T(8,128)(2,1)S(1)} %collective-permute-done.refs_2_), channel_id=1, source_target_pairs={{0,4},{4,0},{8,12},{12,8},{16,20},{20,16},{24,28},{28,24},{1,5},{5... | collective-permute-start | bytes 1228808 | tf_op jit(solution)/shard_map/ppermute | solution.py:157
  32.0 18.0 %collective-permute-start.5 = (bf16[160,1280]{1,0:T(8,128)(2,1)}, bf16[160,1280]{1,0:T(8,128)(2,1)}, u32[]{:S(2)}, u32[]{:S(2)}) collective-permute-start(bf16[160,1280]{1,0:T(8,128)(2,1)} %collective-permute-done.1.refs_4_), channel_id=1, source_target_pairs={{0,4},{4,0},{8,12},{12,8},{16,20},{20,16},{24,28},{28,24},{1,5},{5... | collective-permute-start | bytes 1228808 | tf_op jit(solution)/shard_map/ppermute | solution.py:157
  50.9 6.6 %collective-permute-start.12 = (bf16[512,1280]{1,0:T(8,128)(2,1)}, bf16[512,1280]{1,0:T(8,128)(2,1)}, u32[]{:S(2)}, u32[]{:S(2)}) collective-permute-start(bf16[512,1280]{1,0:T(8,128)(2,1)} %collective-permute-done.10.top_ref), channel_id=1, source_target_pairs={{0,1},{1,0},{2,3},{3,2},{4,5},{5,4},{6,7},{7,6},{8,9},{9,8},{10,11... | collective-permute-start | bytes 3932168 | tf_op jit(solution)/shard_map/ppermute | solution.py:157
  51.3 43.5 %collective-permute-start.17 = (bf16[512,1280]{1,0:T(8,128)(2,1)}, bf16[512,1280]{1,0:T(8,128)(2,1)}, u32[]{:S(2)}, u32[]{:S(2)}) collective-permute-start(bf16[512,1280]{1,0:T(8,128)(2,1)} %param.20), channel_id=1, source_target_pairs={{0,2},{1,3},{2,0},{3,1},{4,6},{5,7},{6,4},{7,5},{8,10},{9,11},{10,... | collective-permute-start | bytes 3932168 | tf_op jit(solution)/shard_map/ppermute | solution.py:157
  52.8 12.5 %collective-permute-start.11 = (bf16[160,1280]{1,0:T(8,128)(2,1)}, bf16[160,1280]{1,0:T(8,128)(2,1)S(1)}, u32[]{:S(2)}, u32[]{:S(2)}) collective-permute-start(bf16[160,1280]{1,0:T(8,128)(2,1)} %collective-permute-done.3.refs_6_), channel_id=1, source_target_pairs={{0,4},{4,0},{8,12},{12,8},{16,20},{20,16},{24,28},{28,24},{1,5},{5... | collective-permute-start | bytes 1228808 | tf_op jit(solution)/shard_map/ppermute | solution.py:157
  55.3 39.4 %collective-permute-start.16 = (bf16[2,160,1280]{2,1,0:T(8,128)(2,1)}, bf16[2,160,1280]{2,1,0:T(8,128)(2,1)}, u32[]{:S(2)}, u32[]{:S(2)}) collective-permute-start(bf16[2,160,1280]{2,1,0:T(8,128)(2,1)} %pad_maximum_fusion.7), channel_id=1, source_target_pairs={{0,4},{4,0},{8,12},{12,8},{16,20},{20,16},{24,28},{28,24},{1,5},{5... | collective-permute-start | bytes 2457608 | tf_op jit(solution)/shard_map/ppermute | solution.py:157
  56.2 30.4 %collective-permute-start.13 = (bf16[160,1280]{1,0:T(8,128)(2,1)S(1)}, bf16[160,1280]{1,0:T(8,128)(2,1)S(1)}, u32[]{:S(2)}, u32[]{:S(2)}) collective-permute-start(bf16[160,1280]{1,0:T(8,128)(2,1)S(1)} %convert_element_type.350.refs_0_), channel_id=1, source_target_pairs={{0,8},{4,12},{8,0},{12,4},{16,24},{20,28},{24,16},{28,20},{1,9},{5... | collective-permute-start | bytes 1228808 | tf_op jit(solution)/shard_map/ppermute | solution.py:157
  57.4 29.2 %collective-permute-start.14 = (bf16[160,1280]{1,0:T(8,128)(2,1)S(1)}, bf16[160,1280]{1,0:T(8,128)(2,1)S(1)}, u32[]{:S(2)}, u32[]{:S(2)}) collective-permute-start(bf16[160,1280]{1,0:T(8,128)(2,1)S(1)} %convert_element_type.350.refs_0_), channel_id=1, source_target_pairs={{0,24},{4,28},{8,16},{12,20},{16,8},{20,12},{24,0},{28,4},{1,25},{... | collective-permute-start | bytes 1228808 | tf_op jit(solution)/shard_map/ppermute | solution.py:157
  66.1 28.6 %collective-permute-start.15 = (bf16[160,1280]{1,0:T(8,128)(2,1)S(1)}, bf16[160,1280]{1,0:T(8,128)(2,1)S(1)}, u32[]{:S(2)}, u32[]{:S(2)}) collective-permute-start(bf16[160,1280]{1,0:T(8,128)(2,1)S(1)} %convert_element_type.350.refs_0_), channel_id=1, source_target_pairs={{0,16},{4,20},{8,24},{12,28},{16,0},{20,4},{24,8},{28,12},{1,17},{... | collective-permute-start | bytes 1228808 | tf_op jit(solution)/shard_map/ppermute | solution.py:157
  100.6 31.2 %collective-permute-start.19 = (bf16[512,1280]{1,0:T(8,128)(2,1)}, bf16[512,1280]{1,0:T(8,128)(2,1)}, u32[]{:S(2)}, u32[]{:S(2)}) collective-permute-start(bf16[512,1280]{1,0:T(8,128)(2,1)} %fusion.49), channel_id=1, source_target_pairs={{0,2},{1,3},{2,0},{3,1},{4,6},{5,7},{6,4},{7,5},{8,10},{9,11},{10,... | collective-permute-start | bytes 3932168 | tf_op jit(solution)/shard_map/ppermute | solution.py:157
  102.4 29.0 %collective-permute-start.20 = (bf16[3,160,1280]{2,1,0:T(8,128)(2,1)}, bf16[3,160,1280]{2,1,0:T(8,128)(2,1)S(1)}, u32[]{:S(2)}, u32[]{:S(2)}) collective-permute-start(bf16[3,160,1280]{2,1,0:T(8,128)(2,1)} %pad_maximum_fusion.6), channel_id=1, source_target_pairs={{0,4},{4,0},{8,12},{12,8},{16,20},{20,16},{24,28},{28,24},{1,5},{5... | collective-permute-start | bytes 3686408 | tf_op jit(solution)/shard_map/ppermute | solution.py:157
  104.9 16.9 %collective-permute-start.21 = (bf16[160,1280]{1,0:T(8,128)(2,1)}, bf16[160,1280]{1,0:T(8,128)(2,1)S(1)}, u32[]{:S(2)}, u32[]{:S(2)}) collective-permute-start(bf16[160,1280]{1,0:T(8,128)(2,1)} %copy-done.7), channel_id=1, source_target_pairs={{0,8},{4,12},{8,0},{12,4},{16,24},{20,28},{24,16},{28,20},{1,9},{5... | collective-permute-start | bytes 1228808 | tf_op jit(solution)/shard_map/ppermute | solution.py:157
  104.9 20.6 %collective-permute-start.22 = (bf16[160,1280]{1,0:T(8,128)(2,1)}, bf16[160,1280]{1,0:T(8,128)(2,1)S(1)}, u32[]{:S(2)}, u32[]{:S(2)}) collective-permute-start(bf16[160,1280]{1,0:T(8,128)(2,1)} %copy-done.7), channel_id=1, source_target_pairs={{0,24},{4,28},{8,16},{12,20},{16,8},{20,12},{24,0},{28,4},{1,25},{... | collective-permute-start | bytes 1228808 | tf_op jit(solution)/shard_map/ppermute | solution.py:157
  133.7 3.4 collective-permute-start.23
  133.9 9.9 %collective-permute-start.27 = (bf16[512,1280]{1,0:T(8,128)(2,1)}, bf16[512,1280]{1,0:T(8,128)(2,1)S(1)}, u32[]{:S(2)}, u32[]{:S(2)}) collective-permute-start(bf16[512,1280]{1,0:T(8,128)(2,1)} %param.20), channel_id=1, source_target_pairs={{0,1},{1,0},{2,3},{3,2},{4,5},{5,4},{6,7},{7,6},{8,9},{9,8},{10,11... | collective-permute-start | bytes 3932168 | tf_op jit(solution)/shard_map/ppermute | solution.py:157
  134.4 9.6 %collective-permute-start.28 = (bf16[512,1280]{1,0:T(8,128)(2,1)}, bf16[512,1280]{1,0:T(8,128)(2,1)S(1)}, u32[]{:S(2)}, u32[]{:S(2)}) collective-permute-start(bf16[512,1280]{1,0:T(8,128)(2,1)} %collective-permute-done.17), channel_id=1, source_target_pairs={{0,1},{1,0},{2,3},{3,2},{4,5},{5,4},{6,7},{7,6},{8,9},{9,8},{10,11... | collective-permute-start | bytes 3932168 | tf_op jit(solution)/shard_map/ppermute | solution.py:157
  140.9 4.6 collective-permute-start.24
  141.7 20.8 %collective-permute-start.25 = (bf16[160,1280]{1,0:T(8,128)(2,1)S(1)}, bf16[160,1280]{1,0:T(8,128)(2,1)S(1)}, u32[]{:S(2)}, u32[]{:S(2)}) collective-permute-start(bf16[160,1280]{1,0:T(8,128)(2,1)S(1)} %copy-done.8), channel_id=1, source_target_pairs={{0,16},{4,20},{8,24},{12,28},{16,0},{20,4},{24,8},{28,12},{1,17},{... | collective-permute-start | bytes 1228808 | tf_op jit(solution)/shard_map/ppermute | solution.py:157
  142.2 20.3 %collective-permute-start.26 = (bf16[2,160,1280]{2,1,0:T(8,128)(2,1)S(1)}, bf16[2,160,1280]{2,1,0:T(8,128)(2,1)S(1)}, u32[]{:S(2)}, u32[]{:S(2)}) collective-permute-start(bf16[2,160,1280]{2,1,0:T(8,128)(2,1)S(1)} %pad_maximum_fusion.8), channel_id=1, source_target_pairs={{0,4},{4,0},{8,12},{12,8},{16,20},{20,16},{24,28},{28,24},{1,5},{5... | collective-permute-start | bytes 2457608 | tf_op jit(solution)/shard_map/ppermute | solution.py:157
  162.6 11.4 %collective-permute-start.29 = (bf16[160,1280]{1,0:T(8,128)(2,1)S(1)}, bf16[160,1280]{1,0:T(8,128)(2,1)S(1)}, u32[]{:S(2)}, u32[]{:S(2)}) collective-permute-start(bf16[160,1280]{1,0:T(8,128)(2,1)S(1)} %collective-permute-done.25.refs_2_), channel_id=1, source_target_pairs={{0,4},{4,0},{8,12},{12,8},{16,20},{20,16},{24,28},{28,24},{1,5},{5... | collective-permute-start | bytes 1228808 | tf_op jit(solution)/shard_map/ppermute | solution.py:157
  164.1 30.4 %collective-permute-start.30 = (bf16[512,1280]{1,0:T(8,128)(2,1)S(1)}, bf16[512,1280]{1,0:T(8,128)(2,1)S(1)}, u32[]{:S(2)}, u32[]{:S(2)}) collective-permute-start(bf16[512,1280]{1,0:T(8,128)(2,1)S(1)} %add_convert_fusion.2), channel_id=1, source_target_pairs={{0,2},{1,3},{2,0},{3,1},{4,6},{5,7},{6,4},{7,5},{8,10},{9,11},{10,... | collective-permute-start | bytes 3932168 | tf_op jit(solution)/shard_map/ppermute | solution.py:157
  212.7 3.1 collective-permute-start.32
  219.8 31.0 %collective-permute-start.34 = (bf16[512,1280]{1,0:T(8,128)(2,1)S(1)}, bf16[512,1280]{1,0:T(8,128)(2,1)S(1)}, u32[]{:S(2)}, u32[]{:S(2)}) collective-permute-start(bf16[512,1280]{1,0:T(8,128)(2,1)S(1)} %add_convert_fusion.1), channel_id=1, source_target_pairs={{0,2},{1,3},{2,0},{3,1},{4,6},{5,7},{6,4},{7,5},{8,10},{9,11},{10,... | collective-permute-start | bytes 3932168 | tf_op jit(solution)/shard_map/ppermute | solution.py:157
  255.1 3.4 collective-permute-start.35
  255.2 7.2 %collective-permute-start.36 = (bf16[512,1280]{1,0:T(8,128)(2,1)}, bf16[512,1280]{1,0:T(8,128)(2,1)}, u32[]{:S(2)}, u32[]{:S(2)}) collective-permute-start(bf16[512,1280]{1,0:T(8,128)(2,1)} %convolution_convert_fusion.5), channel_id=1, source_target_pairs={{0,1},{1,0},{2,3},{3,2},{4,5},{5,4},{6,7},{7,6},{8,9},{9,8},{10,11... | collective-permute-start | bytes 3932168 | tf_op jit(solution)/shard_map/ppermute | solution.py:157
  255.7 6.7 %collective-permute-start.37 = (bf16[512,1280]{1,0:T(8,128)(2,1)}, bf16[512,1280]{1,0:T(8,128)(2,1)S(1)}, u32[]{:S(2)}, u32[]{:S(2)}) collective-permute-start(bf16[512,1280]{1,0:T(8,128)(2,1)} %convolution_convert_fusion.4), channel_id=1, source_target_pairs={{0,1},{1,0},{2,3},{3,2},{4,5},{5,4},{6,7},{7,6},{8,9},{9,8},{10,11... | collective-permute-start | bytes 3932168 | tf_op jit(solution)/shard_map/ppermute | solution.py:157
  257.5 38.2 %collective-permute-start.38 = (bf16[640,1280]{1,0:T(8,128)(2,1)S(1)}, bf16[640,1280]{1,0:T(8,128)(2,1)S(1)}, u32[]{:S(2)}, u32[]{:S(2)}) collective-permute-start(bf16[640,1280]{1,0:T(8,128)(2,1)S(1)} %pad_maximum_fusion.4), channel_id=1, source_target_pairs={{0,4},{4,0},{8,12},{12,8},{16,20},{20,16},{24,28},{28,24},{1,5},{5... | collective-permute-start | bytes 4915208 | tf_op jit(solution)/shard_map/ppermute | solution.py:157
  297.5 37.7 %collective-permute-start.40 = (bf16[640,1280]{1,0:T(8,128)(2,1)}, bf16[640,1280]{1,0:T(8,128)(2,1)}, u32[]{:S(2)}, u32[]{:S(2)}) collective-permute-start(bf16[640,1280]{1,0:T(8,128)(2,1)} %pad_maximum_fusion.5), channel_id=1, source_target_pairs={{0,4},{4,0},{8,12},{12,8},{16,20},{20,16},{24,28},{28,24},{1,5},{5... | collective-permute-start | bytes 4915208 | tf_op jit(solution)/shard_map/ppermute | solution.py:157
  298.2 34.5 %collective-permute-start.39 = (bf16[512,1280]{1,0:T(8,128)(2,1)}, bf16[512,1280]{1,0:T(8,128)(2,1)}, u32[]{:S(2)}, u32[]{:S(2)}) collective-permute-start(bf16[512,1280]{1,0:T(8,128)(2,1)} %get-tuple-element.342), channel_id=1, source_target_pairs={{0,2},{1,3},{2,0},{3,1},{4,6},{5,7},{6,4},{7,5},{8,10},{9,11},{10,... | collective-permute-start | bytes 3932168 | tf_op jit(solution)/shard_map/ppermute | solution.py:157
  303.1 29.6 %collective-permute-start.41 = (bf16[160,1280]{1,0:T(8,128)(2,1)}, bf16[160,1280]{1,0:T(8,128)(2,1)}, u32[]{:S(2)}, u32[]{:S(2)}) collective-permute-start(bf16[160,1280]{1,0:T(8,128)(2,1)} %get-tuple-element.351), channel_id=1, source_target_pairs={{0,8},{4,12},{8,0},{12,4},{16,24},{20,28},{24,16},{28,20},{1,9},{5... | collective-permute-start | bytes 1228808 | tf_op jit(solution)/shard_map/ppermute | solution.py:157
  304.2 28.5 %collective-permute-start.42 = (bf16[160,1280]{1,0:T(8,128)(2,1)}, bf16[160,1280]{1,0:T(8,128)(2,1)}, u32[]{:S(2)}, u32[]{:S(2)}) collective-permute-start(bf16[160,1280]{1,0:T(8,128)(2,1)} %get-tuple-element.350), channel_id=1, source_target_pairs={{0,16},{4,20},{8,24},{12,28},{16,0},{20,4},{24,8},{28,12},{1,17},{... | collective-permute-start | bytes 1228808 | tf_op jit(solution)/shard_map/ppermute | solution.py:157
  335.1 15.9 %collective-permute-start.43 = (bf16[512,1280]{1,0:T(8,128)(2,1)}, bf16[512,1280]{1,0:T(8,128)(2,1)S(1)}, u32[]{:S(2)}, u32[]{:S(2)}) collective-permute-start(bf16[512,1280]{1,0:T(8,128)(2,1)} %collective-permute-done.39), channel_id=1, source_target_pairs={{0,1},{1,0},{2,3},{3,2},{4,5},{5,4},{6,7},{7,6},{8,9},{9,8},{10,11... | collective-permute-start | bytes 3932168 | tf_op jit(solution)/shard_map/ppermute | solution.py:157
  343.0 35.9 %collective-permute-start.47 = (bf16[512,1280]{1,0:T(8,128)(2,1)}, bf16[512,1280]{1,0:T(8,128)(2,1)}, u32[]{:S(2)}, u32[]{:S(2)}) collective-permute-start(bf16[512,1280]{1,0:T(8,128)(2,1)} %fusion.50), channel_id=1, source_target_pairs={{0,2},{1,3},{2,0},{3,1},{4,6},{5,7},{6,4},{7,5},{8,10},{9,11},{10,... | collective-permute-start | bytes 3932168 | tf_op jit(solution)/shard_map/ppermute | solution.py:157
  346.7 30.7 %collective-permute-start.44 = (bf16[160,1280]{1,0:T(8,128)(2,1)}, bf16[160,1280]{1,0:T(8,128)(2,1)S(1)}, u32[]{:S(2)}, u32[]{:S(2)}) collective-permute-start(bf16[160,1280]{1,0:T(8,128)(2,1)} %get-tuple-element.347), channel_id=1, source_target_pairs={{0,8},{4,12},{8,0},{12,4},{16,24},{20,28},{24,16},{28,20},{1,9},{5... | collective-permute-start | bytes 1228808 | tf_op jit(solution)/shard_map/ppermute | solution.py:157
  347.8 31.0 %collective-permute-start.45 = (bf16[160,1280]{1,0:T(8,128)(2,1)}, bf16[160,1280]{1,0:T(8,128)(2,1)S(1)}, u32[]{:S(2)}, u32[]{:S(2)}) collective-permute-start(bf16[160,1280]{1,0:T(8,128)(2,1)} %get-tuple-element.346), channel_id=1, source_target_pairs={{0,16},{4,20},{8,24},{12,28},{16,0},{20,4},{24,8},{28,12},{1,17},{... | collective-permute-start | bytes 1228808 | tf_op jit(solution)/shard_map/ppermute | solution.py:157
  348.9 30.0 %collective-permute-start.46 = (bf16[160,1280]{1,0:T(8,128)(2,1)}, bf16[160,1280]{1,0:T(8,128)(2,1)}, u32[]{:S(2)}, u32[]{:S(2)}) collective-permute-start(bf16[160,1280]{1,0:T(8,128)(2,1)} %get-tuple-element.254), channel_id=1, source_target_pairs={{0,24},{4,28},{8,16},{12,20},{16,8},{20,12},{24,0},{28,4},{1,25},{... | collective-permute-start | bytes 1228808 | tf_op jit(solution)/shard_map/ppermute | solution.py:157
  386.1 11.0 %collective-permute-start.48 = (bf16[160,960]{1,0:T(8,128)(2,1)S(1)}, bf16[160,960]{1,0:T(8,128)(2,1)S(1)}, u32[]{:S(2)}, u32[]{:S(2)}) collective-permute-start(bf16[160,960]{1,0:T(8,128)(2,1)S(1)} %get-tuple-element.363), channel_id=1, source_target_pairs={{0,4},{4,0},{8,12},{12,8},{16,20},{20,16},{24,28},{28,24},{1,5},{5... | collective-permute-start | bytes 921608 | tf_op jit(solution)/shard_map/ppermute | solution.py:157
  390.3 13.3 %collective-permute-start.49 = (bf16[512,1280]{1,0:T(8,128)(2,1)S(1)}, bf16[512,1280]{1,0:T(8,128)(2,1)S(1)}, u32[]{:S(2)}, u32[]{:S(2)}) collective-permute-start(bf16[512,1280]{1,0:T(8,128)(2,1)S(1)} %convolution_convert_fusion.3), channel_id=1, source_target_pairs={{0,1},{1,0},{2,3},{3,2},{4,5},{5,4},{6,7},{7,6},{8,9},{9,8},{10,11... | collective-permute-start | bytes 3932168 | tf_op jit(solution)/shard_map/ppermute | solution.py:157
  390.5 13.2 %collective-permute-start.50 = (bf16[160,1280]{1,0:T(8,128)(2,1)S(1)}, bf16[160,1280]{1,0:T(8,128)(2,1)S(1)}, u32[]{:S(2)}, u32[]{:S(2)}) collective-permute-start(bf16[160,1280]{1,0:T(8,128)(2,1)S(1)} %pad_maximum_fusion.9), channel_id=1, source_target_pairs={{0,4},{4,0},{8,12},{12,8},{16,20},{20,16},{24,28},{28,24},{1,5},{5... | collective-permute-start | bytes 1228808 | tf_op jit(solution)/shard_map/ppermute | solution.py:157
  391.8 24.1 %collective-permute-start.52 = (bf16[160,1280]{1,0:T(8,128)(2,1)S(1)}, bf16[160,1280]{1,0:T(8,128)(2,1)S(1)}, u32[]{:S(2)}, u32[]{:S(2)}) collective-permute-start(bf16[160,1280]{1,0:T(8,128)(2,1)S(1)} %copy-done.83), channel_id=1, source_target_pairs={{0,24},{4,28},{8,16},{12,20},{16,8},{20,12},{24,0},{28,4},{1,25},{... | collective-permute-start | bytes 1228808 | tf_op jit(solution)/shard_map/ppermute | solution.py:157
  393.3 28.4 %collective-permute-start.58 = (bf16[160,960]{1,0:T(8,128)(2,1)}, bf16[160,960]{1,0:T(8,128)(2,1)}, u32[]{:S(2)}, u32[]{:S(2)}) collective-permute-start(bf16[160,960]{1,0:T(8,128)(2,1)} %get-tuple-element.361), channel_id=1, source_target_pairs={{0,4},{4,0},{8,12},{12,8},{16,20},{20,16},{24,28},{28,24},{1,5},{5... | collective-permute-start | bytes 921608 | tf_op jit(solution)/shard_map/ppermute | solution.py:157
  397.1 33.8 %collective-permute-start.57 = (bf16[160,960]{1,0:T(8,128)(2,1)}, bf16[160,960]{1,0:T(8,128)(2,1)}, u32[]{:S(2)}, u32[]{:S(2)}) collective-permute-start(bf16[160,960]{1,0:T(8,128)(2,1)} %get-tuple-element.362), channel_id=1, source_target_pairs={{0,4},{4,0},{8,12},{12,8},{16,20},{20,16},{24,28},{28,24},{1,5},{5... | collective-permute-start | bytes 921608 | tf_op jit(solution)/shard_map/ppermute | solution.py:157
  408.2 41.6 %collective-permute-start.51 = (bf16[512,1280]{1,0:T(8,128)(2,1)}, bf16[512,1280]{1,0:T(8,128)(2,1)}, u32[]{:S(2)}, u32[]{:S(2)}) collective-permute-start(bf16[512,1280]{1,0:T(8,128)(2,1)} %fusion.48), channel_id=1, source_target_pairs={{0,2},{1,3},{2,0},{3,1},{4,6},{5,7},{6,4},{7,5},{8,10},{9,11},{10,... | collective-permute-start | bytes 3932168 | tf_op jit(solution)/shard_map/ppermute | solution.py:157
  413.8 36.0 %collective-permute-start.59 = (bf16[512,1280]{1,0:T(8,128)(2,1)}, bf16[512,1280]{1,0:T(8,128)(2,1)}, u32[]{:S(2)}, u32[]{:S(2)}) collective-permute-start(bf16[512,1280]{1,0:T(8,128)(2,1)} %convolution_convert_fusion.2), channel_id=1, source_target_pairs={{0,1},{1,0},{2,3},{3,2},{4,5},{5,4},{6,7},{7,6},{8,9},{9,8},{10,11... | collective-permute-start | bytes 3932168 | tf_op jit(solution)/shard_map/ppermute | solution.py:157
  420.0 14.1 %collective-permute-start.55 = (bf16[40,1280]{1,0:T(8,128)(2,1)S(1)}, bf16[40,1280]{1,0:T(8,128)(2,1)S(1)}, u32[]{:S(2)}, u32[]{:S(2)}) collective-permute-start(bf16[40,1280]{1,0:T(8,128)(2,1)S(1)} %get-tuple-element.367), channel_id=1, source_target_pairs={{0,24},{4,28},{8,16},{12,20},{16,8},{20,12},{24,0},{28,4},{1,25},{... | collective-permute-start | bytes 307208 | tf_op jit(solution)/shard_map/ppermute | solution.py:157
  421.8 12.4 %collective-permute-start.54 = (bf16[40,1280]{1,0:T(8,128)(2,1)S(1)}, bf16[40,1280]{1,0:T(8,128)(2,1)S(1)}, u32[]{:S(2)}, u32[]{:S(2)}) collective-permute-start(bf16[40,1280]{1,0:T(8,128)(2,1)S(1)} %get-tuple-element.368), channel_id=1, source_target_pairs={{0,8},{4,12},{8,0},{12,4},{16,24},{20,28},{24,16},{28,20},{1,9},{5... | collective-permute-start | bytes 307208 | tf_op jit(solution)/shard_map/ppermute | solution.py:157
  430.9 15.9 %collective-permute-start.53 = (bf16[40,1280]{1,0:T(8,128)(2,1)S(1)}, bf16[40,1280]{1,0:T(8,128)(2,1)S(1)}, u32[]{:S(2)}, u32[]{:S(2)}) collective-permute-start(bf16[40,1280]{1,0:T(8,128)(2,1)S(1)} %get-tuple-element.366), channel_id=1, source_target_pairs={{0,16},{4,20},{8,24},{12,28},{16,0},{20,4},{24,8},{28,12},{1,17},{... | collective-permute-start | bytes 307208 | tf_op jit(solution)/shard_map/ppermute | solution.py:157
  434.2 27.7 %collective-permute-start.62 = (bf16[160,960]{1,0:T(8,128)(2,1)}, bf16[160,960]{1,0:T(8,128)(2,1)}, u32[]{:S(2)}, u32[]{:S(2)}) collective-permute-start(bf16[160,960]{1,0:T(8,128)(2,1)} %get-tuple-element.360), channel_id=1, source_target_pairs={{0,4},{4,0},{8,12},{12,8},{16,20},{20,16},{24,28},{28,24},{1,5},{5... | collective-permute-start | bytes 921608 | tf_op jit(solution)/shard_map/ppermute | solution.py:157
  434.2 28.9 %collective-permute-start.56 = (bf16[160,960]{1,0:T(8,128)(2,1)}, bf16[160,960]{1,0:T(8,128)(2,1)}, u32[]{:S(2)}, u32[]{:S(2)}) collective-permute-start(bf16[160,960]{1,0:T(8,128)(2,1)} %add_convert_fusion.14), channel_id=1, source_target_pairs={{0,16},{4,20},{8,24},{12,28},{16,0},{20,4},{24,8},{28,12},{1,17},{... | collective-permute-start | bytes 921608 | tf_op jit(solution)/shard_map/ppermute | solution.py:157
  453.6 13.9 %collective-permute-start.60 = (bf16[160,960]{1,0:T(8,128)(2,1)S(1)}, bf16[160,960]{1,0:T(8,128)(2,1)S(1)}, u32[]{:S(2)}, u32[]{:S(2)}) collective-permute-start(bf16[160,960]{1,0:T(8,128)(2,1)S(1)} %copy-done.86), channel_id=1, source_target_pairs={{0,8},{4,12},{8,0},{12,4},{16,24},{20,28},{24,16},{28,20},{1,9},{5... | collective-permute-start | bytes 921608 | tf_op jit(solution)/shard_map/ppermute | solution.py:157
  453.6 13.8 %collective-permute-start.61 = (bf16[160,960]{1,0:T(8,128)(2,1)S(1)}, bf16[160,960]{1,0:T(8,128)(2,1)S(1)}, u32[]{:S(2)}, u32[]{:S(2)}) collective-permute-start(bf16[160,960]{1,0:T(8,128)(2,1)S(1)} %copy-done.85), channel_id=1, source_target_pairs={{0,24},{4,28},{8,16},{12,20},{16,8},{20,12},{24,0},{28,4},{1,25},{... | collective-permute-start | bytes 921608 | tf_op jit(solution)/shard_map/ppermute | solution.py:157
  471.3 3.9 collective-permute-start.64
  475.5 3.9 collective-permute-start.65
  479.3 3.9 collective-permute-start.66
  483.2 5.0 collective-permute-start.67
  (111 other events, 1323.6 us)
